TPU v7x, 32 devices: a whole 2x2x4 slice. The times are simulated.
32 devices in a mesh: groups: 2 (over y), ep: 4 (over z), pf: 4 (over x, core).
Axes of the slice: x: 2, y: 2, z: 4, core: 2. Of those that a mesh axis runs over, the one named last changes fastest.
Arguments:
- cache_codes: bfloat16 [128, 32, 576], P(('groups', 'pf'), 'ep'), parts along dimension 0, may hold values from -4 to 4
- cache_scales: bfloat16 [128, 32, 5], P(('groups', 'pf'), 'ep'), parts along dimension 0, may hold values from 0.29 to 3.1, as said below
- queries: bfloat16 [128, 128, 576], P(('groups', 'pf', 'ep')), parts along dimension 0, may hold values from -8192 to 8192
- new_latent: bfloat16 [128, 576], P(('groups', 'pf', 'ep')), parts along dimension 0, may hold values from -16 to 16
- prompt_lengths: int32 [128], P(('groups', 'pf', 'ep')), parts along dimension 0, may hold values from 1 to 32, 1228 in all
- tokens: bfloat16 [128, 7168], P(('groups', 'ep')), parts along dimension 0, may hold values from -6 to 6
- expert_ids: int32 [128, 8], P(('groups', 'ep')), parts along dimension 0, may hold values from 0 to 31, all different within a row; in each aligned block of 16 rows (0 to 15, 16 to 31, ...) at most 8 rows name the same one
- routing_weights: float32 [128, 8], P(('groups', 'ep')), parts along dimension 0, may hold values from 0.25 to 2.5
- w_gate: bfloat16 [32, 7168, 1024], P('ep', None, 'pf'), may hold values from -0.0625 to 0.0625
- w_up: bfloat16 [32, 7168, 1024], P('ep', None, 'pf'), may hold values from -0.0625 to 0.0625
Outputs:
- attention_out: bfloat16 [128, 128, 512], P(('groups', 'pf', 'ep')), parts along dimension 0
- moe_hidden: bfloat16 [128, 8, 1024], P(('groups', 'ep'), None, 'pf'), parts along dimension 0
There are 2 independent parts, one for each index of `groups`. A program takes and returns all parts, laid end to end along the dimension named above; an argument that names none is the same for every part. Nothing has to cross between parts.
Inputs may be any that keep to these rules, and one draw needn't show every extreme that they name: `cache_scales`: positive scales. `prompt_lengths`: the largest length is exactly 32. `expert_ids`: each row names 8 different experts; within the rows of one ep device no expert is named more than 8 times, a bound that some block reaches.
All inputs are finite; a program needn't handle non-finite values. No bound on the sum of `prompt_lengths` on one device may be relied on, other than what follows from the above.
Results may differ from a plain program's by a relative error of at most 0.012.
Values may be sent and summed in bfloat16 or wider, within the bound.
No kernel may reach another device: no remote copies, remote signals or barrier semaphores. Data moves between devices by JAX's collectives and lax.ppermute only.
A program may use at most 192 MiB of HBM per device.

v0:
```python
import jax
import jax.numpy as jnp
from jax import lax
from jax.sharding import PartitionSpec as P

LAT = 512
ROPE = 64
GROUP = 128


qk_scale = 192.0 ** (-0.5)


def spread_scales(scale_block):
    latent_part = jnp.repeat(scale_block[..., :-1], GROUP, axis=-1, total_repeat_length=LAT)
    rope_part = jnp.repeat(scale_block[..., -1:], ROPE, axis=-1, total_repeat_length=ROPE)
    return jnp.concatenate([latent_part, rope_part], axis=-1)


def attend(queries, latent_cache, new_latent, prompt_lengths):
    scores = (
        jnp.einsum("rhc,rtc->rht", queries, latent_cache, preferred_element_type=jnp.float32)
        * qk_scale
    )
    own_score = (
        jnp.einsum("rhc,rc->rh", queries, new_latent, preferred_element_type=jnp.float32) * qk_scale
    )
    positions = jnp.arange(latent_cache.shape[1], dtype=jnp.int32)
    live_mask = (positions[None, :] < prompt_lengths[:, None])[:, None, :]
    peak = jnp.maximum(jnp.max(jnp.where(live_mask, scores, -jnp.inf), axis=2), own_score)
    exponent = jnp.where(live_mask, jnp.exp(scores - peak[..., None]), 0.0)
    own_exponent = jnp.exp(own_score - peak)
    denominator = jnp.sum(exponent, axis=2) + own_exponent
    weights = (exponent / denominator[..., None]).astype(jnp.bfloat16)
    own_weight = (own_exponent / denominator).astype(jnp.bfloat16)
    mixed = jnp.einsum(
        "rht,rtc->rhc", weights, latent_cache[:, :, :LAT], preferred_element_type=jnp.float32
    )
    mixed = mixed + own_weight.astype(jnp.float32)[..., None] * new_latent[:, None, :LAT].astype(
        jnp.float32
    )
    return mixed.astype(jnp.bfloat16)


def local(
    cache_codes,
    cache_scales,
    queries,
    new_latent,
    prompt_lengths,
    tokens,
    expert_ids,
    routing_weights,
    w_gate,
    w_up,
):
    code_blocks, scale_blocks = (
        lax.all_to_all(cache_codes, "ep", split_axis=0, concat_axis=1, tiled=True),
        lax.all_to_all(cache_scales, "ep", split_axis=0, concat_axis=1, tiled=True),
    )
    latent_cache = (
        code_blocks.astype(jnp.float32) * spread_scales(scale_blocks.astype(jnp.float32))
    ).astype(jnp.bfloat16)
    attention_out = attend(queries, latent_cache, new_latent, prompt_lengths)
    row_count, top_count = expert_ids.shape
    per_device = w_gate.shape[0]
    experts_all = per_device * lax.axis_size("ep")
    capacity = row_count // 2
    chosen = expert_ids.reshape(-1)
    matches = (chosen[:, None] == jnp.arange(experts_all, dtype=jnp.int32)[None, :]).astype(
        jnp.int32
    )
    earlier = jnp.cumsum(matches, axis=0) - matches
    slot_index = jnp.sum(earlier * matches, axis=1)
    destination = chosen * capacity + slot_index
    placement = (
        jnp.arange(experts_all * capacity, dtype=jnp.int32)[:, None] == destination[None, :]
    ).astype(jnp.int32)
    row_placement = jnp.sum(
        placement.reshape(experts_all * capacity, row_count, top_count), axis=2
    ).astype(jnp.bfloat16)
    outgoing = jnp.dot(row_placement, tokens, preferred_element_type=jnp.float32).astype(
        jnp.bfloat16
    )
    outgoing = outgoing.reshape(experts_all, capacity, tokens.shape[1])
    received = lax.all_to_all(outgoing, "ep", split_axis=0, concat_axis=0, tiled=True)
    slot_count = received.shape[1]
    grouped = received.reshape(-1, per_device, slot_count, received.shape[2])
    gate_part = jnp.einsum("seid,edf->seif", grouped, w_gate, preferred_element_type=jnp.float32)
    up_part = jnp.einsum("seid,edf->seif", grouped, w_up, preferred_element_type=jnp.float32)
    hidden = (jax.nn.silu(gate_part) * up_part).astype(jnp.bfloat16)
    hidden = hidden.reshape(-1, slot_count, w_gate.shape[2])
    returned = lax.all_to_all(hidden, "ep", split_axis=0, concat_axis=0, tiled=True)
    picked = jnp.dot(
        placement.astype(jnp.bfloat16).T,
        returned.reshape(experts_all * capacity, -1),
        preferred_element_type=jnp.float32,
    )
    moe_hidden = (picked.reshape(row_count, top_count, -1) * routing_weights[:, :, None]).astype(
        jnp.bfloat16
    )
    return (attention_out, moe_hidden)


def solution(mesh):
    return jax.shard_map(
        local,
        mesh=mesh,
        in_specs=(
            P(("groups", "pf"), "ep", None),
            P(("groups", "pf"), "ep", None),
            P(("groups", "pf", "ep"), None, None),
            P(("groups", "pf", "ep"), None),
            P(("groups", "pf", "ep")),
            P(("groups", "ep"), None),
            P(("groups", "ep"), None),
            P(("groups", "ep"), None),
            P("ep", None, "pf"),
            P("ep", None, "pf"),
        ),
        out_specs=(P(("groups", "pf", "ep"), None, None), P(("groups", "ep"), None, "pf")),
        check_vma=False,
    )
```

profile of v0, /device:TPU:0, one launch (start us, length us, event | category | flops | bytes accessed | tf_op | source)
XLA Modules:
  0.0 149.1 jit_solution(17537169782438293591)
XLA Ops:
  0.6 0.0 copy-start
  0.6 1.5 copy.50
  2.1 6.3 %all-to-all-start.1 = ((bf16[16,8,5]{1,2,0:T(8,128)(2,1)}), bf16[16,8,5]{1,2,0:T(8,128)(2,1)S(1)}, u32[]{:S(2)}, u32[]{:S(2)}) async-start(bf16[16,8,5]{1,2,0:T(8,128)(2,1)} %copy.50), calls=%async_computation.1 | async-start | bytes 65536 | tf_op jit(solution)/shard_map/all_to_all | solution.py:59
  8.4 0.8 copy.55
  9.2 0.1 reshape.224
  9.3 0.1 fusion.36
  9.4 0.2 reduce_window_sum.53
  9.5 0.2 select_reduce_fusion
  9.7 0.1 reduce_sum.31
  9.8 4.3 %all-to-all-done.1 = bf16[16,8,5]{1,2,0:T(8,128)(2,1)S(1)} async-done(((bf16[16,8,5]{1,2,0:T(8,128)(2,1)}), bf16[16,8,5]{1,2,0:T(8,128)(2,1)S(1)}, u32[]{:S(2)}, u32[]{:S(2)}) %all-to-all-start.1) | async-done | bytes 1312 | tf_op jit(solution)/shard_map/all_to_all | solution.py:59
  14.1 3.3 %all-to-all-start = ((bf16[16,8,576]{2,1,0:T(8,128)(2,1)}), bf16[16,8,576]{2,1,0:T(8,128)(2,1)S(1)}, u32[]{:S(2)}, u32[]{:S(2)}) async-start(bf16[16,8,576]{2,1,0:T(8,128)(2,1)} %param.16), calls=%async_computation | async-start | bytes 327680 | tf_op jit(solution)/shard_map/all_to_all | solution.py:58
  17.4 0.1 convert_reduce_fusion
  17.6 3.9 %fusion.4 = bf16[32,8,7168]{2,1,0:T(8,128)(2,1)} fusion(bf16[16,7168]{1,0:T(8,128)(2,1)} %param.21, s32[256,16]{0,1:T(8,128)S(1)} %convert_reduce_fusion), kind=kOutput, calls=%fused_computation.6 | convolution fusion | flops 60559360 | bytes 3915776 | tf_op jit(solution)/shard_map/dot_general | solution.py:82
  21.5 0.0 copy-start.3
  21.5 0.0 copy-start.4
  21.5 0.0 copy-start.2
  21.5 1.9 %all-to-all-done = bf16[16,8,576]{2,1,0:T(8,128)(2,1)S(1)} async-done(((bf16[16,8,576]{2,1,0:T(8,128)(2,1)}), bf16[16,8,576]{2,1,0:T(8,128)(2,1)S(1)}, u32[]{:S(2)}, u32[]{:S(2)}) %all-to-all-start) | async-done | bytes 147488 | tf_op jit(solution)/shard_map/all_to_all | solution.py:58
  23.4 4.7 %all-to-all-start.2 = ((bf16[32,8,7168]{2,1,0:T(8,128)(2,1)}), bf16[32,8,7168]{2,1,0:T(8,128)(2,1)}, u32[]{:S(2)}, u32[]{:S(2)}) async-start(bf16[32,8,7168]{2,1,0:T(8,128)(2,1)} %fusion.4), calls=%async_computation.2 | async-start | bytes 7340032 | tf_op jit(solution)/shard_map/all_to_all | solution.py:86
  28.2 0.0 copy-done.3
  28.2 0.1 copy.60
  28.3 0.0 copy-done.4
  28.3 0.1 iota_compare_fusion.3
  28.4 0.0 copy-done.2
  28.4 0.0 copy-done
  28.4 0.2 fusion.42
  28.6 0.1 copy.51
  28.7 0.1 copy.52
  28.8 0.1 reshape.231
  28.9 2.1 %gather_fusion = f32[512,4,32]{2,1,0:T(4,128)S(1)} fusion(f32[4,32,4]{1,0,2:T(4,128)S(1)} %slice.52, s32[1024]{0:T(1024)S(1)} %pad_clamp_fusion), kind=kCustom, calls=%fused_computation | custom fusion | bytes 526336 | tf_op jit(solution)/shard_map/jit(_take)/gather | solution.py:15
  31.0 0.3 copy.54
  31.4 0.1 broadcast.184
  31.5 0.2 select_reduce_fusion.1
  31.8 0.1 bitcast_reduce_fusion
  31.9 75.9 %all-to-all-done.2 = bf16[32,8,7168]{2,1,0:T(8,128)(2,1)} async-done(((bf16[32,8,7168]{2,1,0:T(8,128)(2,1)}), bf16[32,8,7168]{2,1,0:T(8,128)(2,1)}, u32[]{:S(2)}, u32[]{:S(2)}) %all-to-all-start.2) | async-done | bytes 3670048 | tf_op jit(solution)/shard_map/all_to_all | solution.py:86
  107.8 15.2 %fusion.8 = f32[4,8,8,256]{3,2,0,1:T(8,128)S(1)} fusion(bf16[8,7168,256]{2,1,0:T(8,128)(2,1)} %param.24, bf16[4,8,8,7168]{3,2,1,0:T(8,128)(2,1)} %bitcast.18), kind=kOutput, calls=%fused_computation.11 | convolution fusion | flops 939524096 | bytes 33292288 | tf_op jit(solution)/shard_map/seid,edf->seif/dot_general | solution.py:89
  123.1 0.0 copy-start.1
  123.1 15.2 %fusion.23 = bf16[4,8,8,256]{3,2,0,1:T(8,128)(2,1)S(1)} fusion(bf16[8,7168,256]{2,1,0:T(8,128)(2,1)} %param.25, bf16[4,8,8,7168]{3,2,1,0:T(8,128)(2,1)} %bitcast.18, f32[4,8,8,256]{3,2,0,1:T(8,128)S(1)} %fusion.8), kind=kOutput, calls=%fused_computation.14 | convolution fusion | flops 939917312 | bytes 33423360 | tf_op jit(solution)/shard_map/seid,edf->seif/dot_general | solution.py:90
  138.3 0.7 copy.59
  139.0 3.3 %all-to-all-start.3 = ((bf16[32,8,256]{2,1,0:T(8,128)(2,1)}), bf16[32,8,256]{2,1,0:T(8,128)(2,1)S(1)}, u32[]{:S(2)}, u32[]{:S(2)}) async-start(bf16[32,8,256]{2,1,0:T(8,128)(2,1)} %bitcast.25), calls=%async_computation.3 | async-start | bytes 262144 | tf_op jit(solution)/shard_map/all_to_all | solution.py:93
  142.3 1.2 fusion.7
  143.6 4.6 %all-to-all-done.3 = bf16[32,8,256]{2,1,0:T(8,128)(2,1)S(1)} async-done(((bf16[32,8,256]{2,1,0:T(8,128)(2,1)}), bf16[32,8,256]{2,1,0:T(8,128)(2,1)S(1)}, u32[]{:S(2)}, u32[]{:S(2)}) %all-to-all-start.3) | async-done | bytes 131104 | tf_op jit(solution)/shard_map/all_to_all | solution.py:93
  148.2 0.8 fusion.28
  149.1 0.0 copy-done.1
  (15 shorter events, 0.2 us)
Async XLA Ops:
  0.6 27.8 %copy-start = (bf16[4,128,576]{1,2,0:T(8,128)(2,1)S(1)}, bf16[4,128,576]{1,2,0:T(8,128)(2,1)}, u32[]{:S(2)}) copy-start(bf16[4,128,576]{1,2,0:T(8,128)(2,1)} %param.18) | copy-start | bytes 1769476
  2.1 12.0 %all-to-all-start.1 = ((bf16[16,8,5]{1,2,0:T(8,128)(2,1)}), bf16[16,8,5]{1,2,0:T(8,128)(2,1)S(1)}, u32[]{:S(2)}, u32[]{:S(2)}) async-start(bf16[16,8,5]{1,2,0:T(8,128)(2,1)} %copy.50), calls=%async_computation.1 | async-start | bytes 65536 | tf_op jit(solution)/shard_map/all_to_all | solution.py:59
  14.1 9.3 %all-to-all-start = ((bf16[16,8,576]{2,1,0:T(8,128)(2,1)}), bf16[16,8,576]{2,1,0:T(8,128)(2,1)S(1)}, u32[]{:S(2)}, u32[]{:S(2)}) async-start(bf16[16,8,576]{2,1,0:T(8,128)(2,1)} %param.16), calls=%async_computation | async-start | bytes 327680 | tf_op jit(solution)/shard_map/all_to_all | solution.py:58
  21.5 6.7 %copy-start.3 = (f32[16,8]{0,1:T(8,128)S(1)}, f32[16,8]{0,1:T(8,128)}, u32[]{:S(2)}) copy-start(f32[16,8]{0,1:T(8,128)} %param.23) | copy-start | bytes 1540
  21.5 6.8 %copy-start.4 = (s32[4]{0:T(128)S(1)}, s32[4]{0:T(128)}, u32[]{:S(2)}) copy-start(s32[4]{0:T(128)} %param.20) | copy-start | bytes 52
  21.5 6.9 %copy-start.2 = (bf16[4,576]{1,0:T(4,128)(2,1)S(1)}, bf16[4,576]{1,0:T(4,128)(2,1)}, u32[]{:S(2)}) copy-start(bf16[4,576]{1,0:T(4,128)(2,1)} %param.19) | copy-start | bytes 13828
  23.4 84.4 %all-to-all-start.2 = ((bf16[32,8,7168]{2,1,0:T(8,128)(2,1)}), bf16[32,8,7168]{2,1,0:T(8,128)(2,1)}, u32[]{:S(2)}, u32[]{:S(2)}) async-start(bf16[32,8,7168]{2,1,0:T(8,128)(2,1)} %fusion.4), calls=%async_computation.2 | async-start | bytes 7340032 | tf_op jit(solution)/shard_map/all_to_all | solution.py:86
  123.1 26.0 %copy-start.1 = (bf16[4,128,576]{1,2,0:T(8,128)(2,1)S(1)}, bf16[4,128,576]{1,2,0:T(8,128)(2,1)}, u32[]{:S(2)}) copy-start(bf16[4,128,576]{1,2,0:T(8,128)(2,1)} %param.18) | copy-start | bytes 1769476
  139.0 9.2 %all-to-all-start.3 = ((bf16[32,8,256]{2,1,0:T(8,128)(2,1)}), bf16[32,8,256]{2,1,0:T(8,128)(2,1)S(1)}, u32[]{:S(2)}, u32[]{:S(2)}) async-start(bf16[32,8,256]{2,1,0:T(8,128)(2,1)} %bitcast.25), calls=%async_computation.3 | async-start | bytes 262144 | tf_op jit(solution)/shard_map/all_to_all | solution.py:93
where the time goes:
time: 150 us; the launch traced here: 149 us
  waiting for transfers between devices  86.8 us (58%)
  matrix products  36.9 us (25%)
  starting transfers between devices  17.7 us (12%)
  local copies, waits for them, and re-layouts  5.94 us (4%)
    all_to_all x1, waiting for transfers between devices, local(): lax.all_to_all(outgoing, 'ep', split_axis=0, concat_axis=0, tiled=True)  75.9 us
    dot_general x1, matrix products, local(): jnp.einsum('seid,edf->seif', grouped, w_up, preferred_element_type=jnp.fl...  15.2 us
    dot_general x1, matrix products, local(): jnp.einsum('seid,edf->seif', grouped, w_gate, preferred_element_type=jnp....  15.2 us
    all_to_all x1, starting transfers between devices, local(): lax.all_to_all(cache_scales, 'ep', split_axis=0, concat_axis=1, tiled=True)  6.32 us
    all_to_all x1, starting transfers between devices, local(): lax.all_to_all(outgoing, 'ep', split_axis=0, concat_axis=0, tiled=True)  4.75 us
    all_to_all x1, waiting for transfers between devices, local(): lax.all_to_all(hidden, 'ep', split_axis=0, concat_axis=0, tiled=True)  4.65 us
    all_to_all x1, waiting for transfers between devices, local(): lax.all_to_all(cache_scales, 'ep', split_axis=0, concat_axis=1, tiled=True)  4.26 us
    dot_general x1, matrix products, local(): jnp.dot(row_placement, tokens, preferred_element_type=jnp.float32)  3.91 us
  transfers between devices with their start and end apart: 4, of which 4 were waited for; matrix products, arithmetic and copies ran while one was open for 7% of the time, Pallas kernels for 0%

commit v1 on v0

v1 whole, which is shorter than its diff:
```python
import functools

import jax
import jax.numpy as jnp
from jax import lax
from jax.experimental import pallas as pl
from jax.experimental.pallas import tpu as pltpu
from jax.sharding import PartitionSpec as P

LAT = 512
ROPE = 64
GROUP = 128
CHANNELS = 640

qk_scale = 192.0 ** (-0.5)
VM = pl.BlockSpec(memory_space=pltpu.VMEM)
SM = pl.BlockSpec(memory_space=pltpu.SMEM)
ANY = pl.BlockSpec(memory_space=pl.ANY)


def spread_scales(scale_block):
    latent_part = jnp.repeat(scale_block[..., :-1], GROUP, axis=-1, total_repeat_length=LAT)
    rope_part = jnp.repeat(scale_block[..., -1:], ROPE, axis=-1, total_repeat_length=ROPE)
    return jnp.concatenate([latent_part, rope_part], axis=-1)


def decode_cache(codes, scales):
    return (codes.astype(jnp.float32) * spread_scales(scales.astype(jnp.float32))).astype(
        jnp.bfloat16
    )


def attend_kernel(per, q_ref, new_ref, len_ref, at_ref, *refs):
    pieces, (o_ref, kv_ref) = refs[:-2], refs[-2:]
    rows, width, heads = q_ref.shape
    total = kv_ref.shape[0]
    block = rows * per
    count = len(pieces) * block
    kv_ref[pl.ds(count, total - count), :] = jnp.zeros((total - count, width), jnp.bfloat16)
    for d, piece in enumerate(pieces):
        kv_ref[pl.ds(d * block, block), :] = piece[:, piece.shape[1] - CHANNELS :][:, :width]
    kv_ref[pl.ds(count, rows), :] = new_ref[...]
    kv = kv_ref[...]
    place = lax.broadcasted_iota(jnp.int32, (total, 1), 0)
    start = jnp.zeros_like(place)
    for d in range(len(pieces)):
        start = jnp.where(place // block == d, at_ref[d], start)
    row_of = place % block // per
    position = start + place % per
    for r in range(rows):
        live = ((place < count) & (row_of == r) & (position < len_ref[r])) | (place == count + r)
        scores = jnp.dot(kv, q_ref[r], preferred_element_type=jnp.float32) * qk_scale
        scores = jnp.where(live, scores, -jnp.inf)
        exponent = jnp.exp(scores - jnp.max(scores, axis=0, keepdims=True))
        weights = exponent / jnp.sum(exponent, axis=0, keepdims=True)
        o_ref[r] = lax.dot_general(
            weights.astype(jnp.bfloat16),
            kv[:, :LAT],
            (((0,), (0,)), ((), ())),
            preferred_element_type=jnp.float32,
        ).astype(jnp.bfloat16)


def attend(queries, new_latent, prompt_lengths, starts, per, pieces):
    rows, heads, width = queries.shape
    count = sum(p.shape[0] for p in pieces)
    total = -(-(count + rows) // 128) * 128
    return pl.pallas_call(
        functools.partial(attend_kernel, per),
        in_specs=[VM, VM, SM, SM] + [VM] * len(pieces),
        out_specs=VM,
        out_shape=jax.ShapeDtypeStruct((rows, heads, LAT), jnp.bfloat16),
        scratch_shapes=[pltpu.VMEM((total, width), jnp.bfloat16)],
        cost_estimate=pl.CostEstimate(
            flops=4 * rows * heads * total * width,
            bytes_accessed=2 * rows * heads * (width + LAT),
            transcendentals=rows * heads * total,
        ),
        compiler_params=pltpu.CompilerParams(vmem_limit_bytes=8 << 20),
        name="attend",
    )(queries.swapaxes(1, 2), new_latent, prompt_lengths, starts, *pieces)


def pack_kernel(n_ep, codes_ref, scales_ref, tokens_ref, *refs):
    outs, own = refs[:-1], refs[-1]
    total, width = codes_ref.shape
    block = total // n_ep
    here, me = lax.axis_index("ep"), lax.axis_index("pf")
    group = lax.broadcasted_iota(jnp.int32, (scales_ref.shape[1], width), 1) // GROUP
    spread = group == lax.broadcasted_iota(jnp.int32, group.shape, 0)
    scales = jnp.dot(
        scales_ref[...],
        jnp.where(spread, 1.0, 0.0).astype(jnp.bfloat16),
        preferred_element_type=jnp.float32,
    )
    latent = (codes_ref[...].astype(jnp.float32) * scales).astype(jnp.bfloat16)
    rows = tokens_ref.shape[0]
    half = tokens_ref.shape[1] // 8
    fill = jnp.zeros((block, CHANNELS - width), jnp.bfloat16)
    for j in range(n_ep):
        part = latent[j * block : (j + 1) * block]

        @pl.when(here == j)
        def _():
            own[:, :width] = part
            own[:, width:] = fill

        for d, out in enumerate(outs, 1):

            @pl.when(lax.rem(here + d, n_ep) == j)
            def _():
                out[:, half : half + width] = part
                out[:, half + width :] = fill

    for out in outs:
        for c in range(2):
            start = pl.multiple_of((2 * me + c) * half, 128)
            out[c * rows : (c + 1) * rows, :half] = tokens_ref[:, pl.ds(start, half)]


def pack(codes, scales, tokens, n_ep):
    rows, per, width = codes.shape
    block = rows * per // n_ep
    wide = tokens.shape[1] // 8 + CHANNELS
    return pl.pallas_call(
        functools.partial(pack_kernel, n_ep),
        in_specs=[VM] * 3,
        out_specs=[VM] * n_ep,
        out_shape=[jax.ShapeDtypeStruct((block, wide), jnp.bfloat16)] * (n_ep - 1)
        + [jax.ShapeDtypeStruct((block, CHANNELS), jnp.bfloat16)],
        name="pack",
    )(codes.reshape(rows * per, width), scales.reshape(rows * per, -1), tokens)


def hold_kernel(g_ref, u_ref, go_ref, uo_ref, sems):
    copies = []
    for e in range(go_ref.shape[0]):
        copies.append(pltpu.make_async_copy(g_ref.at[e], go_ref.at[e], sems.at[0, e]))
        copies.append(pltpu.make_async_copy(u_ref.at[e], uo_ref.at[e], sems.at[1, e]))
    for copy in copies:
        copy.start()
    for copy in copies:
        copy.wait()


def hold(w_gate, w_up, count):
    shape = (count,) + w_gate.shape[1:]
    return pl.pallas_call(
        hold_kernel,
        in_specs=[ANY, ANY],
        out_specs=[VM, VM],
        out_shape=[pltpu.VMEM(shape, jnp.bfloat16)] * 2,
        scratch_shapes=[pltpu.SemaphoreType.DMA((2, count))],
        cost_estimate=pl.CostEstimate(
            flops=0, bytes_accessed=4 * count * shape[1] * shape[2], transcendentals=0
        ),
        compiler_params=pltpu.CompilerParams(vmem_limit_bytes=2 << 20),
        name="hold",
    )(w_gate, w_up)


def experts_kernel(n_ep, slots, *refs):
    own, xs, (hg, hu, g_hbm, u_hbm), rest = refs[0], refs[1:5], refs[5:9], refs[9:]
    outs, (x_all, gb, ub, sems) = rest[:n_ep], rest[n_ep:]
    held = hg.shape[0]
    experts = g_hbm.shape[0]
    quarter = xs[0].shape[1]
    part = own.shape[0]
    me = lax.axis_index("pf")

    def copies(e, s):
        return (
            pltpu.make_async_copy(g_hbm.at[e], gb.at[s], sems.at[0, s]),
            pltpu.make_async_copy(u_hbm.at[e], ub.at[s], sems.at[1, s]),
        )

    for s in range(min(slots, experts - held)):
        for copy in copies(held + s, s):
            copy.start()
    x_all[:part, :] = own[...]
    for b in range(4):
        start = pl.multiple_of((me ^ b) * quarter, 128)
        x_all[part:, pl.ds(start, quarter)] = xs[b][...]

    def run(e, g_weights, u_weights, at):
        gate = up = jnp.zeros((x_all.shape[0], gb.shape[2]), jnp.float32)
        for k in range(0, x_all.shape[1], quarter):
            x = x_all[:, k : k + quarter]
            gate += jnp.dot(
                x, g_weights[at, k : k + quarter], preferred_element_type=jnp.float32
            )
            up += jnp.dot(x, u_weights[at, k : k + quarter], preferred_element_type=jnp.float32)
        hidden = (gate * jax.nn.sigmoid(gate) * up).astype(jnp.bfloat16)
        for d in range(n_ep):
            outs[d][e] = hidden[d * part : (d + 1) * part]

    @pl.loop(0, held)
    def _(e):
        run(e, hg, hu, e)

    @pl.loop(held, experts)
    def _(e):
        s = lax.rem(e - held, slots)
        for copy in copies(e, s):
            copy.wait()
        run(e, gb, ub, s)

        @pl.when(e + slots < experts)
        def _():
            for copy in copies(e + slots, s):
                copy.start()


def experts_call(own, xs, held_gate, held_up, w_gate, w_up, n_ep):
    experts, depth, wide = w_gate.shape
    rows = own.shape[0] * n_ep
    held = held_gate.shape[0]
    slots = 2
    out = jax.ShapeDtypeStruct((experts, rows // n_ep, wide), jnp.bfloat16)
    return pl.pallas_call(
        functools.partial(experts_kernel, n_ep, slots),
        in_specs=[VM] * 7 + [ANY] * 2,
        out_specs=[VM] * n_ep,
        out_shape=[out] * n_ep,
        scratch_shapes=[
            pltpu.VMEM((rows, depth), jnp.bfloat16),
            pltpu.VMEM((slots, depth, wide), jnp.bfloat16),
            pltpu.VMEM((slots, depth, wide), jnp.bfloat16),
            pltpu.SemaphoreType.DMA((2, slots)),
        ],
        cost_estimate=pl.CostEstimate(
            flops=4 * rows * depth * wide * experts,
            bytes_accessed=4 * (experts - held) * depth * wide,
            transcendentals=experts * rows * wide,
        ),
        compiler_params=pltpu.CompilerParams(vmem_limit_bytes=18 << 20),
        name="experts",
    )(
        own,
        *xs,
        pltpu.with_memory_space_constraint(held_gate, pltpu.VMEM),
        pltpu.with_memory_space_constraint(held_up, pltpu.VMEM),
        w_gate,
        w_up,
    )


def pick_kernel(ids_ref, weight_ref, base_ref, *refs):
    blocks, o_ref = refs[:-1], refs[-1]
    experts, rows, wide = blocks[0].shape
    pairs = ids_ref.shape[0]
    top = pairs // rows
    row = lax.broadcasted_iota(jnp.int32, (pairs, 1), 0) // top
    column = lax.broadcasted_iota(jnp.int32, (1, experts * rows), 1)
    total = jnp.zeros((pairs, wide), jnp.float32)
    for d, block in enumerate(blocks):
        match = (ids_ref[...] == base_ref[d] + column // rows) & (row == column % rows)
        total += jnp.dot(
            jnp.where(match, 1.0, 0.0).astype(jnp.bfloat16),
            block[...].reshape(experts * rows, wide),
            preferred_element_type=jnp.float32,
        )
    o_ref[...] = (total * weight_ref[...]).astype(jnp.bfloat16)


def pick(expert_ids, routing_weights, bases, blocks):
    rows, top = expert_ids.shape
    wide = blocks[0].shape[2]
    out = pl.pallas_call(
        pick_kernel,
        in_specs=[VM, VM, SM] + [VM] * len(blocks),
        out_specs=VM,
        out_shape=jax.ShapeDtypeStruct((rows * top, wide), jnp.bfloat16),
        name="pick",
    )(expert_ids.reshape(-1, 1), routing_weights.reshape(-1, 1), bases, *blocks)
    return out.reshape(rows, top, wide)


def shifted(x, axis, d):
    n = lax.axis_size(axis)
    return lax.ppermute(x, axis, [(s, (s + d) % n) for s in range(n)])


def crossed(x, axis, bit):
    n = lax.axis_size(axis)
    return lax.ppermute(x, axis, [(s, s ^ bit) for s in range(n)])


def local_ring(
    cache_codes,
    cache_scales,
    queries,
    new_latent,
    prompt_lengths,
    tokens,
    expert_ids,
    routing_weights,
    w_gate,
    w_up,
):
    n_ep = lax.axis_size("ep")
    here = lax.axis_index("ep")
    per = cache_codes.shape[1]
    half = tokens.shape[1] // 8
    rows = tokens.shape[0]
    *sent, own_piece = pack(cache_codes, cache_scales, tokens, n_ep)
    came = [shifted(x, "ep", d) for d, x in enumerate(sent, 1)]
    held_gate, held_up = hold(w_gate, w_up, 4)
    x0 = jnp.concatenate(
        [jnp.concatenate([x[:rows, :half], x[rows:, :half]], axis=1) for x in came], axis=0
    )
    x1 = crossed(x0, "pf", 1)
    x2 = crossed(x0, "pf", 2)
    x3 = crossed(x2, "pf", 1)
    order = jnp.arange(n_ep, dtype=jnp.int32)
    starts = (here - order) % n_ep * per
    attention_out = attend(
        queries, new_latent, prompt_lengths, starts, per, [own_piece] + came
    )
    blocks = experts_call(tokens, [x0, x1, x2, x3], held_gate, held_up, w_gate, w_up, n_ep)
    back = [blocks[0]] + [shifted(blocks[d], "ep", -d) for d in range(1, n_ep)]
    bases = (here + order) % n_ep * w_gate.shape[0]
    return attention_out, pick(expert_ids, routing_weights, bases, back)


def local_wide(
    cache_codes,
    cache_scales,
    queries,
    new_latent,
    prompt_lengths,
    tokens,
    expert_ids,
    routing_weights,
    w_gate,
    w_up,
):
    n_ep = lax.axis_size("ep")
    here = lax.axis_index("ep")
    latent = decode_cache(cache_codes, cache_scales)
    rows_dev = queries.shape[0]
    cache = lax.all_to_all(latent, "ep", split_axis=0, concat_axis=1, tiled=True)
    per = cache.shape[1]
    cache = jnp.pad(cache, ((0, 0), (0, 0), (0, CHANNELS - cache.shape[2])))
    starts = jnp.zeros((1,), jnp.int32)
    attention_out = attend(
        queries, new_latent, prompt_lengths, starts, per, [cache.reshape(-1, CHANNELS)]
    )
    x = lax.all_gather(tokens, "ep", axis=0, tiled=True)
    gate = jnp.einsum("rd,edf->erf", x, w_gate, preferred_element_type=jnp.float32)
    up = jnp.einsum("rd,edf->erf", x, w_up, preferred_element_type=jnp.float32)
    hidden = (jax.nn.silu(gate) * up).astype(jnp.bfloat16)
    back = lax.all_to_all(hidden, "ep", split_axis=1, concat_axis=0, tiled=True)
    match = expert_ids[:, :, None] == jnp.arange(back.shape[0], dtype=jnp.int32)
    picked = jnp.einsum(
        "rke,erf->rkf", match.astype(jnp.bfloat16), back, preferred_element_type=jnp.float32
    )
    return attention_out, (picked * routing_weights[:, :, None]).astype(jnp.bfloat16)


def solution(mesh):
    near = mesh.shape["ep"] == 4 and mesh.shape["pf"] == 4
    return jax.shard_map(
        local_ring if near else local_wide,
        mesh=mesh,
        in_specs=(
            P(("groups", "pf"), "ep", None),
            P(("groups", "pf"), "ep", None),
            P(("groups", "pf", "ep"), None, None),
            P(("groups", "pf", "ep"), None),
            P(("groups", "pf", "ep")),
            P(("groups", "ep"), None),
            P(("groups", "ep"), None),
            P(("groups", "ep"), None),
            P("ep", None, "pf"),
            P("ep", None, "pf"),
        ),
        out_specs=(P(("groups", "pf", "ep"), None, None), P(("groups", "ep"), None, "pf")),
        check_vma=False,
    )
```

time: 150 us -> 60.9 us (0.41)
  waiting for transfers between devices: 86.8 us -> 12.3 us
  matrix products: 36.9 us -> 0 us
  Pallas kernels: 0 us -> 30.2 us
  starting transfers between devices: 17.7 us -> 12.6 us
  local copies, waits for them, and re-layouts: 5.94 us -> 4.29 us
    all_to_all x4 -> x0, waiting for transfers between devices: 86.8 us -> none  [the longest x1 75.9 us: local(): lax.all_to_all(outgoing, 'ep', split_axis=0, concat_axis=0, tiled=True)]
    dot_general x7 -> x0, matrix products: 36.9 us -> none  [the longest x1 15.2 us: local(): jnp.einsum('seid,edf->seif', grouped, w_up, preferred_element_type=jnp.fl...]
    pallas_call x0 -> x5, Pallas kernels: none -> 30.2 us  [the longest x1 13.7 us: experts_call(): pl.pallas_call(functools.partial(experts_kernel, n_ep, slots), in_specs=[...]
    all_to_all x4 -> x0, starting transfers between devices: 17.7 us -> none  [the longest x1 6.32 us: local(): lax.all_to_all(cache_scales, 'ep', split_axis=0, concat_axis=1, tiled=True)]
    ppermute x0 -> x9, starting transfers between devices: none -> 12.6 us  [the longest x6 11.1 us: shifted(): return lax.ppermute(x, axis, [(s, (s + d) % n) for s in range(n)])]
    ppermute x0 -> x9, waiting for transfers between devices: none -> 12.3 us  [the longest x6 7.58 us: shifted(): return lax.ppermute(x, axis, [(s, (s + d) % n) for s in range(n)])]
    gather x4 -> x0, local copies, waits for them, and re-layouts: 2.49 us -> none  [the longest x2 2.41 us: spread_scales(): jnp.repeat(scale_block[..., :-1], GROUP, axis=-1, total_repeat_length=LAT)]
  transfers between devices with their start and end apart: 4 -> 9, of which waited for: 4 -> 4; matrix products, arithmetic and copies ran while one was open for 7% -> 3% of each run, Pallas kernels for 0% -> 21%
where the time goes in v1:
time: 60.9 us; the launch traced here: 60.7 us
  Pallas kernels  30.2 us (50%)
  starting transfers between devices  12.6 us (21%)
  waiting for transfers between devices  12.3 us (20%)
  local copies, waits for them, and re-layouts  4.29 us (7%)
  between operations  0.74 us (1%)
    pallas_call x1, Pallas kernels, experts_call(): pl.pallas_call(functools.partial(experts_kernel, n_ep, slots), in_specs=[...  13.7 us
    ppermute x6, starting transfers between devices, shifted(): return lax.ppermute(x, axis, [(s, (s + d) % n) for s in range(n)])  11.1 us
    pallas_call x1, Pallas kernels, hold(): pl.pallas_call(hold_kernel, in_specs=[ANY, ANY], out_specs=[VM, VM], out_...  9.52 us
    ppermute x6, waiting for transfers between devices, shifted(): return lax.ppermute(x, axis, [(s, (s + d) % n) for s in range(n)])  7.58 us
    ppermute x3, waiting for transfers between devices, crossed(): return lax.ppermute(x, axis, [(s, s ^ bit) for s in range(n)])  4.7 us
    pallas_call x1, Pallas kernels, attend(): pl.pallas_call(functools.partial(attend_kernel, per), in_specs=[VM, VM, S...  3 us
    unnamed x25, local copies, waits for them, and re-layouts  2.88 us
    pallas_call x1, Pallas kernels, pack(): pl.pallas_call(functools.partial(pack_kernel, n_ep), in_specs=[VM] * 3, o...  2.02 us
  transfers between devices with their start and end apart: 9, of which 4 were waited for; matrix products, arithmetic and copies ran while one was open for 3% of the time, Pallas kernels for 21%

profile of v1, /device:TPU:0, one launch (start us, length us, event | category | flops | bytes accessed | tf_op | source)
XLA Modules:
  0.0 60.7 jit_solution(13450510660217005913)
XLA Ops:
  0.6 1.4 %copy.17 = bf16[16,8,5]{2,1,0:T(8,128)(2,1)} copy(bf16[16,8,5]{0,1,2:T(8,128)(2,1)} %param.11) | data formatting | bytes 2560 | tf_op args[1]
  2.1 2.0 %pack.1 = (bf16[32,1536]{1,0:T(8,128)(2,1)}, bf16[32,1536]{1,0:T(8,128)(2,1)}, bf16[32,1536]{1,0:T(8,128)(2,1)}, bf16[32,640]{1,0:T(8,128)(2,1)}) custom-call(bf16[128,576]{1,0:T(8,128)(2,1)} %bitcast.5, bf16[128,5]{1,0:T(8,128)(2,1)} %bitcast.6, bf16[16,7168]{1,0:T(8,128)(2,1)} %refs_0_.1), custom_call_target="tpu_custom_call" | custom-call | tf_op jit(solution)/shard_map/pack/pallas_call | solution.py:125
  4.1 3.0 %collective-permute-start = (bf16[32,1536]{1,0:T(8,128)(2,1)}, bf16[32,1536]{1,0:T(8,128)(2,1)S(1)}, u32[]{:S(2)}, u32[]{:S(2)}) collective-permute-start(bf16[32,1536]{1,0:T(8,128)(2,1)} %get-tuple-element.13), channel_id=1, source_target_pairs={{0,4},{4,8},{8,12},{12,0},{1,5},{5,9},{9,13},{13,1},{2,6},{6,10},{... | collective-permute-start | bytes 294920 | tf_op jit(solution)/shard_map/ppermute | solution.py:281
  7.1 2.6 %collective-permute-start.1 = (bf16[32,1536]{1,0:T(8,128)(2,1)}, bf16[32,1536]{1,0:T(8,128)(2,1)S(1)}, u32[]{:S(2)}, u32[]{:S(2)}) collective-permute-start(bf16[32,1536]{1,0:T(8,128)(2,1)} %get-tuple-element.14), channel_id=1, source_target_pairs={{0,8},{4,12},{8,0},{12,4},{1,9},{5,13},{9,1},{13,5},{2,10},{6,14},... | collective-permute-start | bytes 294920 | tf_op jit(solution)/shard_map/ppermute | solution.py:281
  9.7 1.3 %collective-permute-start.2 = (bf16[32,1536]{1,0:T(8,128)(2,1)}, bf16[32,1536]{1,0:T(8,128)(2,1)S(1)}, u32[]{:S(2)}, u32[]{:S(2)}) collective-permute-start(bf16[32,1536]{1,0:T(8,128)(2,1)} %get-tuple-element.15), channel_id=1, source_target_pairs={{0,12},{4,0},{8,4},{12,8},{1,13},{5,1},{9,5},{13,9},{2,14},{6,2},{... | collective-permute-start | bytes 294920 | tf_op jit(solution)/shard_map/ppermute | solution.py:281
  11.0 2.0 %collective-permute-done.refs_1_ = bf16[32,1536]{1,0:T(8,128)(2,1)S(1)} collective-permute-done((bf16[32,1536]{1,0:T(8,128)(2,1)}, bf16[32,1536]{1,0:T(8,128)(2,1)S(1)}, u32[]{:S(2)}, u32[]{:S(2)}) %collective-permute-start) | collective-permute-done | bytes 98336 | tf_op jit(solution)/shard_map/ppermute | solution.py:281
  13.0 3.5 %collective-permute-done.1.refs_2_ = bf16[32,1536]{1,0:T(8,128)(2,1)S(1)} collective-permute-done((bf16[32,1536]{1,0:T(8,128)(2,1)}, bf16[32,1536]{1,0:T(8,128)(2,1)S(1)}, u32[]{:S(2)}, u32[]{:S(2)}) %collective-permute-start.1) | collective-permute-done | bytes 98336 | tf_op jit(solution)/shard_map/ppermute | solution.py:281
  16.5 0.0 collective-permute-done.2.refs_3_
  16.6 1.6 %collective-permute-start.4 = (bf16[48,1792]{1,0:T(8,128)(2,1)S(1)}, bf16[48,1792]{1,0:T(8,128)(2,1)S(1)}, u32[]{:S(2)}, u32[]{:S(2)}) collective-permute-start(bf16[48,1792]{1,0:T(8,128)(2,1)S(1)} %maximum_maximum_fusion.refs_1_), channel_id=1, source_target_pairs={{0,2},{1,3},{2,0},{3,1},{4,6},{5,7},{6,4},{7,5},{8,10},{9,11},{10,... | collective-permute-start | bytes 516104 | tf_op jit(solution)/shard_map/ppermute | solution.py:286
  18.1 0.0 collective-permute-start.3
  18.1 4.7 %collective-permute-done.4.refs_3_ = bf16[48,1792]{1,0:T(8,128)(2,1)S(1)} collective-permute-done((bf16[48,1792]{1,0:T(8,128)(2,1)S(1)}, bf16[48,1792]{1,0:T(8,128)(2,1)S(1)}, u32[]{:S(2)}, u32[]{:S(2)}) %collective-permute-start.4) | collective-permute-done | bytes 172064 | tf_op jit(solution)/shard_map/ppermute | solution.py:286
  22.8 0.0 collective-permute-start.5
  22.8 0.0 copy-start
  22.8 9.5 %hold.1 = (bf16[4,7168,256]{2,1,0:T(8,128)(2,1)S(1)}, bf16[4,7168,256]{2,1,0:T(8,128)(2,1)S(1)}) custom-call(bf16[8,7168,256]{2,1,0:T(8,128)(2,1)} %refs_7_.1, bf16[8,7168,256]{2,1,0:T(8,128)(2,1)} %refs_8_.1), custom_call_target="tpu_custom_call" | custom-call | bytes 29360128 | tf_op jit(solution)/shard_map/hold/pallas_call | solution.py:148
  32.4 0.5 fusion.1.base_ref
  32.9 0.0 collective-permute-done.3.refs_2_
  32.9 0.0 collective-permute-done.5.refs_4_
  32.9 0.0 copy-done
  32.9 0.0 copy-start.9
  32.9 0.0 copy-start.10
  32.9 0.0 copy-start.1
  32.9 0.0 copy-start.3
  33.0 0.0 copy-start.4
  33.0 0.0 copy-start.5
  33.0 13.7 %experts.1 = (bf16[8,16,256]{2,1,0:T(8,128)(2,1)S(1)}, bf16[8,16,256]{2,1,0:T(8,128)(2,1)S(1)}, bf16[8,16,256]{2,1,0:T(8,128)(2,1)S(1)}, bf16[8,16,256]{2,1,0:T(8,128)(2,1)S(1)}) custom-call(bf16[16,7168]{1,0:T(8,128)(2,1)S(1)} %copy-done, bf16[48,1792]{1,0:T(8,128)(2,1)S(1)} %maximum_maximum_fusion.refs_1_, ...), custom_call_target="tpu_custom_call" | custom-call | flops 3758096384 | bytes 29360128 | tf_op jit(solution)/shard_map/experts/pallas_call | solution.py:220
  46.7 0.0 copy-start.2
  46.7 0.6 %copy-done.2 = bf16[8,16,256]{2,1,0:T(8,128)(2,1)} copy-done((bf16[8,16,256]{2,1,0:T(8,128)(2,1)}, bf16[8,16,256]{2,1,0:T(8,128)(2,1)S(1)}, u32[]{:S(2)}) %copy-start.2) | copy-done | bytes 65560
  47.3 2.8 %collective-permute-start.6 = (bf16[8,16,256]{2,1,0:T(8,128)(2,1)S(1)}, bf16[8,16,256]{2,1,0:T(8,128)(2,1)S(1)}, u32[]{:S(2)}, u32[]{:S(2)}) collective-permute-start(bf16[8,16,256]{2,1,0:T(8,128)(2,1)S(1)} %get-tuple-element.19), channel_id=1, source_target_pairs={{0,12},{4,0},{8,4},{12,8},{1,13},{5,1},{9,5},{13,9},{2,14},{6,2},{... | collective-permute-start | bytes 196616 | tf_op jit(solution)/shard_map/ppermute | solution.py:281
  50.1 1.3 %collective-permute-start.7 = (bf16[8,16,256]{2,1,0:T(8,128)(2,1)S(1)}, bf16[8,16,256]{2,1,0:T(8,128)(2,1)S(1)}, u32[]{:S(2)}, u32[]{:S(2)}) collective-permute-start(bf16[8,16,256]{2,1,0:T(8,128)(2,1)S(1)} %get-tuple-element.20), channel_id=1, source_target_pairs={{0,8},{4,12},{8,0},{12,4},{1,9},{5,13},{9,1},{13,5},{2,10},{6,14},... | collective-permute-start | bytes 196616 | tf_op jit(solution)/shard_map/ppermute | solution.py:281
  51.4 0.0 collective-permute-start.8
  51.5 0.0 copy-done.9
  51.5 0.1 copy.18
  51.5 0.7 %reshape.24.ids_ref = s32[128,1]{1,0:T(8,128)} reshape(s32[16,8]{1,0:T(8,128)S(1)} %copy.18) | data formatting | bytes 1024 | tf_op jit(solution)/shard_map/reshape | solution.py:275
  52.2 0.0 copy-done.10
  52.3 0.1 copy.19
  52.3 0.7 %reshape.25.weight_ref = f32[128,1]{1,0:T(8,128)} reshape(f32[16,8]{1,0:T(8,128)S(1)} %copy.19) | data formatting | bytes 1024 | tf_op jit(solution)/shard_map/reshape | solution.py:275
  53.0 0.0 copy-done.1
  53.0 0.0 copy-done.3
  53.0 0.0 copy-done.4
  53.0 0.0 copy-done.5
  53.0 3.0 %attend.1 = bf16[4,128,512]{2,1,0:T(8,128)(2,1)} custom-call(bf16[4,576,128]{2,1,0:T(8,128)(2,1)S(1)} %bitcast.4, bf16[4,576]{1,0:T(4,128)(2,1)S(1)} %copy-done.4, s32[4]{0:T(128)S(1)} %copy-done.5, s32[4]{0:T(128)S(1)} %fusion.at_ref, bf16[32,640]{1,0:T(8,128)(2,1)S(1)} %copy-done.3, bf16[32,1536]{1,0:T(8,128)(2,1)S(1)} %collective-permute-done.refs_1_, ...), custom_call_target="tpu_custom_call" | custom-call | flops 301989888 | bytes 1114112 | tf_op jit(solution)/shard_map/attend/pallas_call | solution.py:68
  56.0 0.0 collective-permute-done.6.refs_1_
  56.0 2.1 %collective-permute-done.7.refs_2_ = bf16[8,16,256]{2,1,0:T(8,128)(2,1)S(1)} collective-permute-done((bf16[8,16,256]{2,1,0:T(8,128)(2,1)S(1)}, bf16[8,16,256]{2,1,0:T(8,128)(2,1)S(1)}, u32[]{:S(2)}, u32[]{:S(2)}) %collective-permute-start.7) | collective-permute-done | bytes 65568 | tf_op jit(solution)/shard_map/ppermute | solution.py:281
  58.1 0.0 collective-permute-done.8.refs_3_
  58.1 0.0 copy-done.6
  58.2 0.6 %copy-done.7 = bf16[8,16,256]{2,1,0:T(8,128)(2,1)} copy-done((bf16[8,16,256]{2,1,0:T(8,128)(2,1)}, bf16[8,16,256]{2,1,0:T(8,128)(2,1)S(1)}, u32[]{:S(2)}) %copy-start.7) | copy-done | bytes 65560
  58.8 0.0 copy-done.8
  58.8 1.9 %pick.1 = bf16[128,256]{1,0:T(8,128)(2,1)} custom-call(s32[128,1]{1,0:T(8,128)} %reshape.24.ids_ref, f32[128,1]{1,0:T(8,128)} %reshape.25.weight_ref, s32[4]{0:T(128)} %fusion.1.base_ref, bf16[8,16,256]{2,1,0:T(8,128)(2,1)} %copy-done.2, bf16[8,16,256]{2,1,0:T(8,128)(2,1)} %copy-done.6, bf16[8,16,256]{2,1,0:T(8,128)(2,1)} %copy-done.7, ...), custom_call_target="tpu_custom_call" | custom-call | tf_op jit(solution)/shard_map/pick/pallas_call | solution.py:269
  (8 shorter events, 0.0 us)
Async XLA Ops:
  4.1 8.9 %collective-permute-start = (bf16[32,1536]{1,0:T(8,128)(2,1)}, bf16[32,1536]{1,0:T(8,128)(2,1)S(1)}, u32[]{:S(2)}, u32[]{:S(2)}) collective-permute-start(bf16[32,1536]{1,0:T(8,128)(2,1)} %get-tuple-element.13), channel_id=1, source_target_pairs={{0,4},{4,8},{8,12},{12,0},{1,5},{5,9},{9,13},{13,1},{2,6},{6,10},{... | collective-permute-start | bytes 294920 | tf_op jit(solution)/shard_map/ppermute | solution.py:281
  7.1 9.4 %collective-permute-start.1 = (bf16[32,1536]{1,0:T(8,128)(2,1)}, bf16[32,1536]{1,0:T(8,128)(2,1)S(1)}, u32[]{:S(2)}, u32[]{:S(2)}) collective-permute-start(bf16[32,1536]{1,0:T(8,128)(2,1)} %get-tuple-element.14), channel_id=1, source_target_pairs={{0,8},{4,12},{8,0},{12,4},{1,9},{5,13},{9,1},{13,5},{2,10},{6,14},... | collective-permute-start | bytes 294920 | tf_op jit(solution)/shard_map/ppermute | solution.py:281
  9.7 6.8 %collective-permute-start.2 = (bf16[32,1536]{1,0:T(8,128)(2,1)}, bf16[32,1536]{1,0:T(8,128)(2,1)S(1)}, u32[]{:S(2)}, u32[]{:S(2)}) collective-permute-start(bf16[32,1536]{1,0:T(8,128)(2,1)} %get-tuple-element.15), channel_id=1, source_target_pairs={{0,12},{4,0},{8,4},{12,8},{1,13},{5,1},{9,5},{13,9},{2,14},{6,2},{... | collective-permute-start | bytes 294920 | tf_op jit(solution)/shard_map/ppermute | solution.py:281
  16.6 6.3 %collective-permute-start.4 = (bf16[48,1792]{1,0:T(8,128)(2,1)S(1)}, bf16[48,1792]{1,0:T(8,128)(2,1)S(1)}, u32[]{:S(2)}, u32[]{:S(2)}) collective-permute-start(bf16[48,1792]{1,0:T(8,128)(2,1)S(1)} %maximum_maximum_fusion.refs_1_), channel_id=1, source_target_pairs={{0,2},{1,3},{2,0},{3,1},{4,6},{5,7},{6,4},{7,5},{8,10},{9,11},{10,... | collective-permute-start | bytes 516104 | tf_op jit(solution)/shard_map/ppermute | solution.py:286
  18.1 14.8 %collective-permute-start.3 = (bf16[48,1792]{1,0:T(8,128)(2,1)S(1)}, bf16[48,1792]{1,0:T(8,128)(2,1)S(1)}, u32[]{:S(2)}, u32[]{:S(2)}) collective-permute-start(bf16[48,1792]{1,0:T(8,128)(2,1)S(1)} %maximum_maximum_fusion.refs_1_), channel_id=1, source_target_pairs={{0,1},{1,0},{2,3},{3,2},{4,5},{5,4},{6,7},{7,6},{8,9},{9,8},{10,11... | collective-permute-start | bytes 516104 | tf_op jit(solution)/shard_map/ppermute | solution.py:286
  22.8 10.1 %collective-permute-start.5 = (bf16[48,1792]{1,0:T(8,128)(2,1)S(1)}, bf16[48,1792]{1,0:T(8,128)(2,1)S(1)}, u32[]{:S(2)}, u32[]{:S(2)}) collective-permute-start(bf16[48,1792]{1,0:T(8,128)(2,1)S(1)} %collective-permute-done.4.refs_3_), channel_id=1, source_target_pairs={{0,1},{1,0},{2,3},{3,2},{4,5},{5,4},{6,7},{7,6},{8,9},{9,8},{10,11... | collective-permute-start | bytes 516104 | tf_op jit(solution)/shard_map/ppermute | solution.py:286
  22.8 10.1 %copy-start = (bf16[16,7168]{1,0:T(8,128)(2,1)S(1)}, bf16[16,7168]{1,0:T(8,128)(2,1)}, u32[]{:S(2)}) copy-start(bf16[16,7168]{1,0:T(8,128)(2,1)} %refs_0_.1) | copy-start | bytes 688132
  32.9 18.6 %copy-start.9 = (s32[16,8]{0,1:T(8,128)S(1)}, s32[16,8]{0,1:T(8,128)}, u32[]{:S(2)}) copy-start(s32[16,8]{0,1:T(8,128)} %param.16) | copy-start | bytes 1540
  32.9 19.3 %copy-start.10 = (f32[16,8]{0,1:T(8,128)S(1)}, f32[16,8]{0,1:T(8,128)}, u32[]{:S(2)}) copy-start(f32[16,8]{0,1:T(8,128)} %param.17) | copy-start | bytes 1540
  32.9 20.1 %copy-start.1 = (bf16[4,128,576]{1,2,0:T(8,128)(2,1)S(1)}, bf16[4,128,576]{1,2,0:T(8,128)(2,1)}, u32[]{:S(2)}) copy-start(bf16[4,128,576]{1,2,0:T(8,128)(2,1)} %param.12) | copy-start | bytes 1769476
  32.9 20.1 %copy-start.3 = (bf16[32,640]{1,0:T(8,128)(2,1)S(1)}, bf16[32,640]{1,0:T(8,128)(2,1)}, u32[]{:S(2)}) copy-start(bf16[32,640]{1,0:T(8,128)(2,1)} %get-tuple-element.12.refs_0_) | copy-start | bytes 122884
  33.0 20.1 %copy-start.4 = (bf16[4,576]{1,0:T(4,128)(2,1)S(1)}, bf16[4,576]{1,0:T(4,128)(2,1)}, u32[]{:S(2)}) copy-start(bf16[4,576]{1,0:T(4,128)(2,1)} %new_ref.1) | copy-start | bytes 13828
  33.0 20.1 %copy-start.5 = (s32[4]{0:T(128)S(1)}, s32[4]{0:T(128)}, u32[]{:S(2)}) copy-start(s32[4]{0:T(128)} %len_ref.1) | copy-start | bytes 52
  46.7 0.6 %copy-start.2 = (bf16[8,16,256]{2,1,0:T(8,128)(2,1)}, bf16[8,16,256]{2,1,0:T(8,128)(2,1)S(1)}, u32[]{:S(2)}) copy-start(bf16[8,16,256]{2,1,0:T(8,128)(2,1)S(1)} %get-tuple-element.18.refs_0_) | copy-start | bytes 196612
  47.3 8.7 %collective-permute-start.6 = (bf16[8,16,256]{2,1,0:T(8,128)(2,1)S(1)}, bf16[8,16,256]{2,1,0:T(8,128)(2,1)S(1)}, u32[]{:S(2)}, u32[]{:S(2)}) collective-permute-start(bf16[8,16,256]{2,1,0:T(8,128)(2,1)S(1)} %get-tuple-element.19), channel_id=1, source_target_pairs={{0,12},{4,0},{8,4},{12,8},{1,13},{5,1},{9,5},{13,9},{2,14},{6,2},{... | collective-permute-start | bytes 196616 | tf_op jit(solution)/shard_map/ppermute | solution.py:281
  50.1 8.0 %collective-permute-start.7 = (bf16[8,16,256]{2,1,0:T(8,128)(2,1)S(1)}, bf16[8,16,256]{2,1,0:T(8,128)(2,1)S(1)}, u32[]{:S(2)}, u32[]{:S(2)}) collective-permute-start(bf16[8,16,256]{2,1,0:T(8,128)(2,1)S(1)} %get-tuple-element.20), channel_id=1, source_target_pairs={{0,8},{4,12},{8,0},{12,4},{1,9},{5,13},{9,1},{13,5},{2,10},{6,14},... | collective-permute-start | bytes 196616 | tf_op jit(solution)/shard_map/ppermute | solution.py:281
  51.4 6.7 %collective-permute-start.8 = (bf16[8,16,256]{2,1,0:T(8,128)(2,1)S(1)}, bf16[8,16,256]{2,1,0:T(8,128)(2,1)S(1)}, u32[]{:S(2)}, u32[]{:S(2)}) collective-permute-start(bf16[8,16,256]{2,1,0:T(8,128)(2,1)S(1)} %get-tuple-element.21), channel_id=1, source_target_pairs={{0,4},{4,8},{8,12},{12,0},{1,5},{5,9},{9,13},{13,1},{2,6},{6,10},{... | collective-permute-start | bytes 196616 | tf_op jit(solution)/shard_map/ppermute | solution.py:281
  56.0 2.1 %copy-start.6 = (bf16[8,16,256]{2,1,0:T(8,128)(2,1)}, bf16[8,16,256]{2,1,0:T(8,128)(2,1)S(1)}, u32[]{:S(2)}) copy-start(bf16[8,16,256]{2,1,0:T(8,128)(2,1)S(1)} %collective-permute-done.6.refs_1_) | copy-start | bytes 196612
  58.1 0.6 %copy-start.7 = (bf16[8,16,256]{2,1,0:T(8,128)(2,1)}, bf16[8,16,256]{2,1,0:T(8,128)(2,1)S(1)}, u32[]{:S(2)}) copy-start(bf16[8,16,256]{2,1,0:T(8,128)(2,1)S(1)} %collective-permute-done.7.refs_2_) | copy-start | bytes 196612
  58.1 0.6 %copy-start.8 = (bf16[8,16,256]{2,1,0:T(8,128)(2,1)}, bf16[8,16,256]{2,1,0:T(8,128)(2,1)S(1)}, u32[]{:S(2)}) copy-start(bf16[8,16,256]{2,1,0:T(8,128)(2,1)S(1)} %collective-permute-done.8.refs_3_) | copy-start | bytes 196612

commit v2 on v1

v2 whole, which is shorter than its diff:
```python
import functools

import jax
import jax.numpy as jnp
from jax import lax
from jax.experimental import pallas as pl
from jax.experimental.pallas import tpu as pltpu
from jax.sharding import PartitionSpec as P

LAT = 512
ROPE = 64
GROUP = 128
CHANNELS = 640

qk_scale = 192.0 ** (-0.5)
VM = pl.BlockSpec(memory_space=pltpu.VMEM)
SM = pl.BlockSpec(memory_space=pltpu.SMEM)
HBM = pl.BlockSpec(memory_space=pltpu.HBM)


def spread_scales(scale_block):
    latent_part = jnp.repeat(scale_block[..., :-1], GROUP, axis=-1, total_repeat_length=LAT)
    rope_part = jnp.repeat(scale_block[..., -1:], ROPE, axis=-1, total_repeat_length=ROPE)
    return jnp.concatenate([latent_part, rope_part], axis=-1)


def decode_cache(codes, scales):
    return (codes.astype(jnp.float32) * spread_scales(scales.astype(jnp.float32))).astype(
        jnp.bfloat16
    )


def attend_kernel(per, q_ref, new_ref, len_ref, at_ref, *refs):
    pieces, (o_ref, kv_ref) = refs[:-2], refs[-2:]
    rows, width, heads = q_ref.shape
    total = kv_ref.shape[0]
    block = rows * per
    count = len(pieces) * block
    kv_ref[pl.ds(count, total - count), :] = jnp.zeros((total - count, width), jnp.bfloat16)
    for d, piece in enumerate(pieces):
        kv_ref[pl.ds(d * block, block), :] = piece[:, piece.shape[1] - CHANNELS :][:, :width]
    kv_ref[pl.ds(count, rows), :] = new_ref[...]
    kv = kv_ref[...]
    place = lax.broadcasted_iota(jnp.int32, (total, 1), 0)
    start = jnp.zeros_like(place)
    for d in range(len(pieces)):
        start = jnp.where(place // block == d, at_ref[d], start)
    row_of = place % block // per
    position = start + place % per
    for r in range(rows):
        live = ((place < count) & (row_of == r) & (position < len_ref[r])) | (place == count + r)
        scores = jnp.dot(kv, q_ref[r], preferred_element_type=jnp.float32) * qk_scale
        scores = jnp.where(live, scores, -jnp.inf)
        exponent = jnp.exp(scores - jnp.max(scores, axis=0, keepdims=True))
        weights = exponent / jnp.sum(exponent, axis=0, keepdims=True)
        o_ref[r] = lax.dot_general(
            weights.astype(jnp.bfloat16),
            kv[:, :LAT],
            (((0,), (0,)), ((), ())),
            preferred_element_type=jnp.float32,
        ).astype(jnp.bfloat16)


def attend(queries, new_latent, prompt_lengths, starts, per, pieces):
    rows, heads, width = queries.shape
    count = sum(p.shape[0] for p in pieces)
    total = -(-(count + rows) // 128) * 128
    return pl.pallas_call(
        functools.partial(attend_kernel, per),
        in_specs=[VM, VM, SM, SM] + [VM] * len(pieces),
        out_specs=VM,
        out_shape=jax.ShapeDtypeStruct((rows, heads, LAT), jnp.bfloat16),
        scratch_shapes=[pltpu.VMEM((total, width), jnp.bfloat16)],
        cost_estimate=pl.CostEstimate(
            flops=4 * rows * heads * total * width,
            bytes_accessed=2 * rows * heads * (width + LAT),
            transcendentals=rows * heads * total,
        ),
        compiler_params=pltpu.CompilerParams(vmem_limit_bytes=8 << 20),
        name="attend",
    )(queries.swapaxes(1, 2), new_latent, prompt_lengths, starts, *pieces)


def pack_kernel(codes_ref, scales_ref, tokens_ref, *refs):
    outs, own, lat_ref = refs[:-2], refs[-2], refs[-1]
    rows, per, width = codes_ref.shape
    groups = scales_ref.shape[0]
    block = own.shape[0]
    here, me = lax.axis_index("ep"), lax.axis_index("pf")
    scales = scales_ref[...].astype(jnp.float32)
    lat_ref[:, width:] = jnp.zeros((rows * per, CHANNELS - width), jnp.float32)
    for r in range(rows):
        for g in range(groups):
            columns = slice(g * GROUP, min((g + 1) * GROUP, width))
            lat_ref[r * per : (r + 1) * per, columns] = (
                codes_ref[r, :, columns].astype(jnp.float32) * scales[g, :, r : r + 1]
            )
    half = tokens_ref.shape[1] // 8
    for d in range(len(outs) + 1):
        start = pl.multiple_of((here ^ d) * block, block)
        part = lat_ref[pl.ds(start, block), :].astype(jnp.bfloat16)
        if d == 0:
            own[...] = part
            continue
        outs[d - 1][:, half:] = part
        for c in range(2):
            start = pl.multiple_of((2 * me + c) * half, 128)
            outs[d - 1][c * block // 2 : (c + 1) * block // 2, :half] = tokens_ref[
                :, pl.ds(start, half)
            ]


def pack(codes, scales, tokens, n_ep):
    rows, per, width = codes.shape
    block = rows * per // n_ep
    wide = tokens.shape[1] // 8 + CHANNELS
    return pl.pallas_call(
        pack_kernel,
        in_specs=[VM] * 3,
        out_specs=[VM] * n_ep,
        out_shape=[jax.ShapeDtypeStruct((block, wide), jnp.bfloat16)] * (n_ep - 1)
        + [jax.ShapeDtypeStruct((block, CHANNELS), jnp.bfloat16)],
        scratch_shapes=[pltpu.VMEM((rows * per, CHANNELS), jnp.float32)],
        name="pack",
    )(codes, scales.transpose(2, 1, 0), tokens)


def part_copies(b, g_ref, u_ref, g_to, u_to, sems):
    depth = g_to.shape[1]
    start = pl.multiple_of((lax.axis_index("pf") ^ b) * depth, 128)
    return [
        (
            pltpu.make_async_copy(g_ref.at[e, pl.ds(start, depth)], g_to.at[e], sems.at[0, e]),
            pltpu.make_async_copy(u_ref.at[e, pl.ds(start, depth)], u_to.at[e], sems.at[1, e]),
        )
        for e in range(g_to.shape[0])
    ]


def hold_kernel(ids_ref, weight_ref, g_ref, u_ref, go_ref, uo_ref, select_ref, column_ref, sems):
    copies = part_copies(0, g_ref, u_ref, go_ref, uo_ref, sems)
    for pair in copies:
        for copy in pair:
            copy.start()
    top, rows = ids_ref.shape
    experts = g_ref.shape[0]
    here = lax.axis_index("ep")
    pair = lax.broadcasted_iota(jnp.int32, (top * rows, 1), 0)
    ids = jnp.zeros((top * rows, rows), jnp.int32)
    weight = jnp.zeros((top * rows, rows), jnp.float32)
    mine = lax.broadcasted_iota(jnp.int32, (top * rows, rows), 1) == pair // top
    for k in range(top):
        chosen = mine & (pair % top == k)
        ids = jnp.where(chosen, ids_ref[k : k + 1, :], ids)
        weight = jnp.where(chosen, weight_ref[k : k + 1, :], weight)
    ids = jnp.sum(ids, axis=1, keepdims=True)
    column_ref[...] = jnp.sum(weight, axis=1, keepdims=True)
    column = lax.broadcasted_iota(jnp.int32, (1, experts * rows), 1)
    for d in range(select_ref.shape[1] // (experts * rows)):
        match = (ids == (here ^ d) * experts + column // rows) & (column % rows == pair // top)
        select_ref[:, d * experts * rows : (d + 1) * experts * rows] = jnp.where(
            match, 1.0, 0.0
        ).astype(jnp.bfloat16)
    for pair in copies:
        for copy in pair:
            copy.wait()


def hold(expert_ids, routing_weights, w_gate, w_up, n_ep):
    experts, depth, wide = w_gate.shape
    rows, top = expert_ids.shape
    shape = (experts, depth // 4, wide)
    return pl.pallas_call(
        hold_kernel,
        in_specs=[VM, VM, HBM, HBM],
        out_specs=[VM] * 4,
        out_shape=[pltpu.VMEM(shape, jnp.bfloat16)] * 2
        + [
            jax.ShapeDtypeStruct((rows * top, n_ep * experts * rows), jnp.bfloat16),
            jax.ShapeDtypeStruct((rows * top, 1), jnp.float32),
        ],
        scratch_shapes=[pltpu.SemaphoreType.DMA((2, experts))],
        cost_estimate=pl.CostEstimate(
            flops=0, bytes_accessed=4 * experts * shape[1] * wide, transcendentals=0
        ),
        compiler_params=pltpu.CompilerParams(vmem_limit_bytes=4 << 20),
        name="hold",
    )(expert_ids.T, routing_weights.T, w_gate, w_up)


def set_rows(b, x_ref, own_ref, came_ref):
    rows, quarter = own_ref.shape[0], came_ref.shape[1]
    start = pl.multiple_of((lax.axis_index("pf") ^ b) * quarter, 128)
    x_ref[:rows, :] = own_ref[:, pl.ds(start, quarter)]
    x_ref[rows:, :] = came_ref[...]


def times(x_ref, w_ref, e):
    return jnp.dot(x_ref[...], w_ref[e], preferred_element_type=jnp.float32)


def stage_kernel(b, own, came, hg, hu, g_hbm, u_hbm, *refs):
    total, (gate, up, g_next, u_next, x_ref, sems) = refs[:-6], refs[-6:]
    copies = part_copies(b + 1, g_hbm, u_hbm, g_next, u_next, sems)
    for pair in copies:
        for copy in pair:
            copy.start()
    set_rows(b, x_ref, own, came)

    @pl.loop(0, hg.shape[0])
    def _(e):
        gate_part, up_part = times(x_ref, hg, e), times(x_ref, hu, e)
        gate[e] = gate_part + total[0][e] if total else gate_part
        up[e] = up_part + total[1][e] if total else up_part

    for pair in copies:
        for copy in pair:
            copy.wait()


def in_vmem(x):
    return pltpu.with_memory_space_constraint(x, pltpu.VMEM)


def stage(b, own, came, held, total, w_gate, w_up):
    experts, depth, wide = w_gate.shape
    rows = own.shape[0] + came.shape[0]
    sums = jax.ShapeDtypeStruct((experts, rows, wide), jnp.float32)
    *total, g_next, u_next = pl.pallas_call(
        functools.partial(stage_kernel, b),
        in_specs=[VM] * 4 + [HBM] * 2 + [VM] * len(total),
        out_specs=[VM] * 4,
        out_shape=[sums] * 2 + [pltpu.VMEM((experts, depth // 4, wide), jnp.bfloat16)] * 2,
        scratch_shapes=[
            pltpu.VMEM((rows, depth // 4), jnp.bfloat16),
            pltpu.SemaphoreType.DMA((2, experts)),
        ],
        cost_estimate=pl.CostEstimate(
            flops=rows * depth * wide * experts,
            bytes_accessed=experts * depth * wide,
            transcendentals=0,
        ),
        compiler_params=pltpu.CompilerParams(vmem_limit_bytes=8 << 20),
        name="stage",
    )(own, came, *[in_vmem(x) for x in held], w_gate, w_up, *total)
    return total, (g_next, u_next)


def last_kernel(n_ep, own, came, came_too, hg, hu, g_hbm, u_hbm, gate, up, *refs):
    outs, (x_ref, y_ref, gb, ub, sems) = refs[:n_ep], refs[n_ep:]
    experts, part = hg.shape[0], own.shape[0]
    copies = part_copies(3, g_hbm, u_hbm, gb, ub, sems)
    for pair in copies:
        for copy in pair:
            copy.start()
    set_rows(2, x_ref, own, came)
    set_rows(3, y_ref, own, came_too)
    for e in range(experts):
        gate_part = gate[e] + times(x_ref, hg, e)
        up_part = up[e] + times(x_ref, hu, e)
        for copy in copies[e]:
            copy.wait()
        gate_part += times(y_ref, gb, e)
        up_part += times(y_ref, ub, e)
        hidden = (gate_part * jax.nn.sigmoid(gate_part) * up_part).astype(jnp.bfloat16)
        for d in range(n_ep):
            outs[d][e] = hidden[d * part : (d + 1) * part]


def last(n_ep, own, came, came_too, held, total, w_gate, w_up):
    experts, depth, wide = w_gate.shape
    rows = own.shape[0] + came.shape[0]
    held_shape = (experts, depth // 4, wide)
    out = jax.ShapeDtypeStruct((experts, own.shape[0], wide), jnp.bfloat16)
    return pl.pallas_call(
        functools.partial(last_kernel, n_ep),
        in_specs=[VM] * 5 + [HBM] * 2 + [VM] * 2,
        out_specs=[VM] * n_ep,
        out_shape=[out] * n_ep,
        scratch_shapes=[
            pltpu.VMEM((rows, depth // 4), jnp.bfloat16),
            pltpu.VMEM((rows, depth // 4), jnp.bfloat16),
            pltpu.VMEM(held_shape, jnp.bfloat16),
            pltpu.VMEM(held_shape, jnp.bfloat16),
            pltpu.SemaphoreType.DMA((2, experts)),
        ],
        cost_estimate=pl.CostEstimate(
            flops=2 * rows * depth * wide * experts,
            bytes_accessed=experts * depth * wide,
            transcendentals=experts * rows * wide,
        ),
        compiler_params=pltpu.CompilerParams(vmem_limit_bytes=24 << 20),
        name="last",
    )(own, came, came_too, *[in_vmem(x) for x in held], w_gate, w_up, *total)


def pick_kernel(select_ref, column_ref, *refs):
    blocks, o_ref = refs[:-1], refs[-1]
    experts, rows, wide = blocks[0].shape
    total = jnp.zeros((select_ref.shape[0], wide), jnp.float32)
    for d, block in enumerate(blocks):
        total += jnp.dot(
            select_ref[:, d * experts * rows : (d + 1) * experts * rows],
            block[...].reshape(experts * rows, wide),
            preferred_element_type=jnp.float32,
        )
    o_ref[...] = (total * column_ref[...]).astype(jnp.bfloat16)


def pick(select, column, blocks):
    pairs, wide = select.shape[0], blocks[0].shape[2]
    return pl.pallas_call(
        pick_kernel,
        in_specs=[VM] * (2 + len(blocks)),
        out_specs=VM,
        out_shape=jax.ShapeDtypeStruct((pairs, wide), jnp.bfloat16),
        name="pick",
    )(select, column, *blocks)


def crossed(x, axis, bit):
    n = lax.axis_size(axis)
    return lax.ppermute(x, axis, [(s, s ^ bit) for s in range(n)])


def local_ring(
    cache_codes,
    cache_scales,
    queries,
    new_latent,
    prompt_lengths,
    tokens,
    expert_ids,
    routing_weights,
    w_gate,
    w_up,
):
    n_ep = lax.axis_size("ep")
    here = lax.axis_index("ep")
    per = cache_codes.shape[1]
    half = tokens.shape[1] // 8
    rows = tokens.shape[0]
    *sent, own_piece = pack(cache_codes, cache_scales, tokens, n_ep)
    came = [crossed(x, "ep", d) for d, x in enumerate(sent, 1)]
    w_gate, w_up = [pltpu.with_memory_space_constraint(w, pltpu.HBM) for w in (w_gate, w_up)]
    *held, select, column = hold(expert_ids, routing_weights, w_gate, w_up, n_ep)
    came, held, select, column = lax.optimization_barrier((came, held, select, column))
    x0 = jnp.concatenate(
        [jnp.concatenate([x[:rows, :half], x[rows:, :half]], axis=1) for x in came], axis=0
    )
    x1 = crossed(x0, "pf", 1)
    x2 = crossed(x0, "pf", 2)
    total, held = stage(0, tokens, x0, held, (), w_gate, w_up)
    x2, total = lax.optimization_barrier((x2, total))
    x3 = crossed(x2, "pf", 1)
    total, held = stage(1, tokens, x1, held, total, w_gate, w_up)
    blocks = last(n_ep, tokens, x2, x3, held, total, w_gate, w_up)
    back = [blocks[0]] + [crossed(blocks[d], "ep", d) for d in range(1, n_ep)]
    starts = (here ^ jnp.arange(n_ep, dtype=jnp.int32)) * per
    attention_out = attend(
        queries, new_latent, prompt_lengths, starts, per, [own_piece] + came
    )
    moe_hidden = pick(select, column, back)
    return attention_out, moe_hidden.reshape(rows, -1, moe_hidden.shape[1])


def local_wide(
    cache_codes,
    cache_scales,
    queries,
    new_latent,
    prompt_lengths,
    tokens,
    expert_ids,
    routing_weights,
    w_gate,
    w_up,
):
    n_ep = lax.axis_size("ep")
    here = lax.axis_index("ep")
    latent = decode_cache(cache_codes, cache_scales)
    rows_dev = queries.shape[0]
    cache = lax.all_to_all(latent, "ep", split_axis=0, concat_axis=1, tiled=True)
    per = cache.shape[1]
    cache = jnp.pad(cache, ((0, 0), (0, 0), (0, CHANNELS - cache.shape[2])))
    starts = jnp.zeros((1,), jnp.int32)
    attention_out = attend(
        queries, new_latent, prompt_lengths, starts, per, [cache.reshape(-1, CHANNELS)]
    )
    x = lax.all_gather(tokens, "ep", axis=0, tiled=True)
    gate = jnp.einsum("rd,edf->erf", x, w_gate, preferred_element_type=jnp.float32)
    up = jnp.einsum("rd,edf->erf", x, w_up, preferred_element_type=jnp.float32)
    hidden = (jax.nn.silu(gate) * up).astype(jnp.bfloat16)
    back = lax.all_to_all(hidden, "ep", split_axis=1, concat_axis=0, tiled=True)
    match = expert_ids[:, :, None] == jnp.arange(back.shape[0], dtype=jnp.int32)
    picked = jnp.einsum(
        "rke,erf->rkf", match.astype(jnp.bfloat16), back, preferred_element_type=jnp.float32
    )
    return attention_out, (picked * routing_weights[:, :, None]).astype(jnp.bfloat16)


def solution(mesh):
    near = mesh.shape["ep"] == 4 and mesh.shape["pf"] == 4
    return jax.shard_map(
        local_ring if near else local_wide,
        mesh=mesh,
        in_specs=(
            P(("groups", "pf"), "ep", None),
            P(("groups", "pf"), "ep", None),
            P(("groups", "pf", "ep"), None, None),
            P(("groups", "pf", "ep"), None),
            P(("groups", "pf", "ep")),
            P(("groups", "ep"), None),
            P(("groups", "ep"), None),
            P(("groups", "ep"), None),
            P("ep", None, "pf"),
            P("ep", None, "pf"),
        ),
        out_specs=(P(("groups", "pf", "ep"), None, None), P(("groups", "ep"), None, "pf")),
        check_vma=False,
    )
```

time: 60.9 us -> 60.7 us (level)
  local copies, waits for them, and re-layouts: 4.29 us -> 14.1 us
  waiting for transfers between devices: 12.3 us -> 3.74 us
    unnamed x25 -> x34, local copies, waits for them, and re-layouts: 2.88 us -> 14.1 us
    ppermute x6 -> x0, starting transfers between devices: 11.1 us -> none  [shifted(): return lax.ppermute(x, axis, [(s, (s + d) % n) for s in range(n)])]
    ppermute x3 -> x9, starting transfers between devices: 1.56 us -> 12.1 us  [crossed(): return lax.ppermute(x, axis, [(s, s ^ bit) for s in range(n)])]
    ppermute x6 -> x0, waiting for transfers between devices: 7.58 us -> none  [shifted(): return lax.ppermute(x, axis, [(s, (s + d) % n) for s in range(n)])]
    reshape x2 -> x0, local copies, waits for them, and re-layouts: 1.4 us -> none  [the longest x1 0.7 us: pick(): expert_ids.reshape(-1, 1)]
    ppermute x3 -> x9, waiting for transfers between devices: 4.7 us -> 3.74 us  [crossed(): return lax.ppermute(x, axis, [(s, s ^ bit) for s in range(n)])]
    pallas_call x4 -> x6, Pallas kernels: 27.2 us -> 26.6 us  [the longest x2 10.7 us: stage(): pl.pallas_call(functools.partial(stage_kernel, b), in_specs=[VM] * 4 + [H...]
  transfers between devices with their start and end apart: 9 -> 9, of which waited for: 4 -> 3; matrix products, arithmetic and copies ran while one was open for 3% -> 0% of each run, Pallas kernels for 21% -> 32%
where the time goes in v2:
time: 60.7 us; the launch traced here: 60.4 us
  Pallas kernels  29.6 us (49%)
  local copies, waits for them, and re-layouts  14.1 us (23%)
  starting transfers between devices  12.1 us (20%)
  waiting for transfers between devices  3.74 us (6%)
  between operations  0.82 us (1%)
    unnamed x34, local copies, waits for them, and re-layouts  14.1 us
    ppermute x9, starting transfers between devices, crossed(): return lax.ppermute(x, axis, [(s, s ^ bit) for s in range(n)])  12.1 us
    pallas_call x2, Pallas kernels, stage(): pl.pallas_call(functools.partial(stage_kernel, b), in_specs=[VM] * 4 + [H...  10.7 us
    pallas_call x1, Pallas kernels, last(): pl.pallas_call(functools.partial(last_kernel, n_ep), in_specs=[VM] * 5 +...  6.72 us
    pallas_call x1, Pallas kernels, hold(): pl.pallas_call(hold_kernel, in_specs=[VM, VM, HBM, HBM], out_specs=[VM] *...  5.44 us
    ppermute x9, waiting for transfers between devices, crossed(): return lax.ppermute(x, axis, [(s, s ^ bit) for s in range(n)])  3.74 us
    pallas_call x1, Pallas kernels, attend(): pl.pallas_call(functools.partial(attend_kernel, per), in_specs=[VM, VM, S...  3 us
    pallas_call x1, Pallas kernels, pack(): pl.pallas_call(pack_kernel, in_specs=[VM] * 3, out_specs=[VM] * n_ep, out...  1.91 us
  transfers between devices with their start and end apart: 9, of which 3 were waited for; matrix products, arithmetic and copies ran while one was open for 0% of the time, Pallas kernels for 32%

profile of v2, /device:TPU:0, one launch (start us, length us, event | category | flops | bytes accessed | tf_op | source)
XLA Modules:
  0.0 60.4 jit_solution(11234150486087382728)
XLA Ops:
  0.6 1.9 %pack.1 = (bf16[32,1536]{1,0:T(8,128)(2,1)}, bf16[32,1536]{1,0:T(8,128)(2,1)}, bf16[32,1536]{1,0:T(8,128)(2,1)}, bf16[32,640]{1,0:T(8,128)(2,1)}) custom-call(bf16[16,8,576]{2,1,0:T(8,128)(2,1)} %codes_ref.1, bf16[5,8,16]{2,1,0:T(8,128)(2,1)} %bitcast.9, bf16[16,7168]{1,0:T(8,128)(2,1)} %own.5), custom_call_target="tpu_custom_call" | custom-call | tf_op jit(solution)/shard_map/pack/pallas_call | solution.py:117
  2.5 3.0 %collective-permute-start = (bf16[32,1536]{1,0:T(8,128)(2,1)}, bf16[32,1536]{1,0:T(8,128)(2,1)S(1)}, u32[]{:S(2)}, u32[]{:S(2)}) collective-permute-start(bf16[32,1536]{1,0:T(8,128)(2,1)} %get-tuple-element.33), channel_id=1, source_target_pairs={{0,4},{4,0},{8,12},{12,8},{1,5},{5,1},{9,13},{13,9},{2,6},{6,2},{1... | collective-permute-start | bytes 294920 | tf_op jit(solution)/shard_map/ppermute | solution.py:323
  5.6 2.6 %collective-permute-start.1 = (bf16[32,1536]{1,0:T(8,128)(2,1)}, bf16[32,1536]{1,0:T(8,128)(2,1)S(1)}, u32[]{:S(2)}, u32[]{:S(2)}) collective-permute-start(bf16[32,1536]{1,0:T(8,128)(2,1)} %get-tuple-element.34), channel_id=1, source_target_pairs={{0,8},{4,12},{8,0},{12,4},{1,9},{5,13},{9,1},{13,5},{2,10},{6,14},... | collective-permute-start | bytes 294920 | tf_op jit(solution)/shard_map/ppermute | solution.py:323
  8.2 0.0 collective-permute-start.2
  8.2 0.7 %copy-done.11 = s32[16,8]{0,1:T(8,128)S(1)} copy-done((s32[16,8]{0,1:T(8,128)S(1)}, s32[16,8]{0,1:T(8,128)}, u32[]{:S(2)}) %copy-start.11) | copy-done | bytes 536
  8.8 0.7 %copy-done.12 = f32[16,8]{0,1:T(8,128)S(1)} copy-done((f32[16,8]{0,1:T(8,128)S(1)}, f32[16,8]{0,1:T(8,128)}, u32[]{:S(2)}) %copy-start.12) | copy-done | bytes 536
  9.5 5.4 %hold.1 = (bf16[8,1792,256]{2,1,0:T(8,128)(2,1)S(1)}, bf16[8,1792,256]{2,1,0:T(8,128)(2,1)S(1)}, bf16[128,512]{1,0:T(8,128)(2,1)S(1)}, f32[128,1]{1,0:T(8,128)S(1)}) custom-call(s32[8,16]{1,0:T(8,128)S(1)} %bitcast.6, f32[8,16]{1,0:T(8,128)S(1)} %bitcast.7, bf16[8,7168,256]{2,1,0:T(8,128)(2,1)} %g_hbm.5, bf16[8,7168,256]{2,1,0:T(8,128)(2,1)} %u_hbm.5), custom_call_target="tpu_custom_call" | custom-call | bytes 14680064 | tf_op jit(solution)/shard_map/hold/pallas_call | solution.py:173
  15.0 0.0 copy-start.6
  15.0 0.0 copy-start.7
  15.0 0.0 collective-permute-done.refs_1_
  15.0 1.2 %collective-permute-done.1.refs_2_ = bf16[32,1536]{1,0:T(8,128)(2,1)S(1)} collective-permute-done((bf16[32,1536]{1,0:T(8,128)(2,1)}, bf16[32,1536]{1,0:T(8,128)(2,1)S(1)}, u32[]{:S(2)}, u32[]{:S(2)}) %collective-permute-start.1) | collective-permute-done | bytes 98336 | tf_op jit(solution)/shard_map/ppermute | solution.py:323
  16.2 0.0 collective-permute-done.2.refs_3_
  16.2 0.0 copy-done.6
  16.2 0.0 copy-done.7
  16.3 1.6 %collective-permute-start.3 = (bf16[48,1792]{1,0:T(8,128)(2,1)S(1)}, bf16[48,1792]{1,0:T(8,128)(2,1)S(1)}, u32[]{:S(2)}, u32[]{:S(2)}) collective-permute-start(bf16[48,1792]{1,0:T(8,128)(2,1)S(1)} %maximum_maximum_fusion.came), channel_id=1, source_target_pairs={{0,2},{1,3},{2,0},{3,1},{4,6},{5,7},{6,4},{7,5},{8,10},{9,11},{10,... | collective-permute-start | bytes 516104 | tf_op jit(solution)/shard_map/ppermute | solution.py:323
  17.8 0.0 collective-permute-start.5
  17.8 0.0 copy-done.4
  17.8 5.3 %stage.2 = (f32[8,64,256]{2,1,0:T(8,128)S(1)}, f32[8,64,256]{2,1,0:T(8,128)S(1)}, bf16[8,1792,256]{2,1,0:T(8,128)(2,1)S(1)}, bf16[8,1792,256]{2,1,0:T(8,128)(2,1)S(1)}) custom-call(bf16[16,7168]{1,0:T(8,128)(2,1)S(1)} %copy-done.4, bf16[48,1792]{1,0:T(8,128)(2,1)S(1)} %maximum_maximum_fusion.came, bf16[8,1792,256]{2,1,0:T(8,128)(2,1)S(1)} %get-tuple-element.45.hg, ...), custom_call_target="tpu_custom_call" | custom-call | flops 939524096 | bytes 14680064 | tf_op jit(solution)/shard_map/stage/pallas_call | solution.py:229
  23.2 0.0 copy-start
  23.2 2.9 %copy-done = bf16[8,1792,256]{2,1,0:T(8,128)(2,1)} copy-done((bf16[8,1792,256]{2,1,0:T(8,128)(2,1)}, bf16[8,1792,256]{2,1,0:T(8,128)(2,1)S(1)}, u32[]{:S(2)}) %copy-start) | copy-done | bytes 7340056
  26.1 3.0 %copy-done.2 = bf16[8,1792,256]{2,1,0:T(8,128)(2,1)} copy-done((bf16[8,1792,256]{2,1,0:T(8,128)(2,1)}, bf16[8,1792,256]{2,1,0:T(8,128)(2,1)S(1)}, u32[]{:S(2)}) %copy-start.2) | copy-done | bytes 7340056
  29.1 0.0 collective-permute-done.3.came
  29.1 0.5 collective-permute-start.4
  29.6 0.0 collective-permute-done.5.came
  29.6 3.1 %copy-done.1 = bf16[8,1792,256]{2,1,0:T(8,128)(2,1)S(1)} copy-done((bf16[8,1792,256]{2,1,0:T(8,128)(2,1)S(1)}, bf16[8,1792,256]{2,1,0:T(8,128)(2,1)}, u32[]{:S(2)}) %copy-start.1) | copy-done | bytes 7340056
  32.7 3.1 %copy-done.3 = bf16[8,1792,256]{2,1,0:T(8,128)(2,1)S(1)} copy-done((bf16[8,1792,256]{2,1,0:T(8,128)(2,1)S(1)}, bf16[8,1792,256]{2,1,0:T(8,128)(2,1)}, u32[]{:S(2)}) %copy-start.3) | copy-done | bytes 7340056
  35.8 5.3 %stage.3 = (f32[8,64,256]{2,1,0:T(8,128)S(1)}, f32[8,64,256]{2,1,0:T(8,128)S(1)}, bf16[8,1792,256]{2,1,0:T(8,128)(2,1)S(1)}, bf16[8,1792,256]{2,1,0:T(8,128)(2,1)S(1)}) custom-call(bf16[16,7168]{1,0:T(8,128)(2,1)S(1)} %copy-done.4, bf16[48,1792]{1,0:T(8,128)(2,1)S(1)} %collective-permute-done.5.came, bf16[8,1792,256]{2,1,0:T(8,128)(2,1)S(1)} %copy-done.1, ...), custom_call_target="tpu_custom_call" | custom-call | flops 939524096 | bytes 14680064 | tf_op jit(solution)/shard_map/stage/pallas_call | solution.py:229
  41.1 0.0 collective-permute-done.4.came_too
  41.1 0.0 copy-start.5
  41.1 0.0 copy-start.9
  41.1 0.0 copy-start.10
  41.2 0.0 copy-start.13
  41.2 6.7 %last.1 = (bf16[8,16,256]{2,1,0:T(8,128)(2,1)S(1)}, bf16[8,16,256]{2,1,0:T(8,128)(2,1)S(1)}, bf16[8,16,256]{2,1,0:T(8,128)(2,1)S(1)}, bf16[8,16,256]{2,1,0:T(8,128)(2,1)S(1)}) custom-call(bf16[16,7168]{1,0:T(8,128)(2,1)S(1)} %copy-done.4, bf16[48,1792]{1,0:T(8,128)(2,1)S(1)} %collective-permute-done.3.came, ...), custom_call_target="tpu_custom_call" | custom-call | flops 1879048192 | bytes 14680064 | tf_op jit(solution)/shard_map/last/pallas_call | solution.py:275
  47.9 0.0 copy-start.8
  47.9 1.7 %collective-permute-start.6 = (bf16[8,16,256]{2,1,0:T(8,128)(2,1)S(1)}, bf16[8,16,256]{2,1,0:T(8,128)(2,1)S(1)}, u32[]{:S(2)}, u32[]{:S(2)}) collective-permute-start(bf16[8,16,256]{2,1,0:T(8,128)(2,1)S(1)} %get-tuple-element.59), channel_id=1, source_target_pairs={{0,4},{4,0},{8,12},{12,8},{1,5},{5,1},{9,13},{13,9},{2,6},{6,2},{1... | collective-permute-start | bytes 196616 | tf_op jit(solution)/shard_map/ppermute | solution.py:323
  49.6 2.2 %collective-permute-start.7 = (bf16[8,16,256]{2,1,0:T(8,128)(2,1)S(1)}, bf16[8,16,256]{2,1,0:T(8,128)(2,1)S(1)}, u32[]{:S(2)}, u32[]{:S(2)}) collective-permute-start(bf16[8,16,256]{2,1,0:T(8,128)(2,1)S(1)} %get-tuple-element.60), channel_id=1, source_target_pairs={{0,8},{4,12},{8,0},{12,4},{1,9},{5,13},{9,1},{13,5},{2,10},{6,14},... | collective-permute-start | bytes 196616 | tf_op jit(solution)/shard_map/ppermute | solution.py:323
  51.8 0.6 collective-permute-start.8
  52.4 0.0 copy-done.5
  52.4 0.0 copy-done.9
  52.4 0.0 copy-done.10
  52.4 3.0 %attend.1 = bf16[4,128,512]{2,1,0:T(8,128)(2,1)} custom-call(bf16[4,576,128]{2,1,0:T(8,128)(2,1)S(1)} %bitcast.5, bf16[4,576]{1,0:T(4,128)(2,1)S(1)} %copy-done.10, s32[4]{0:T(128)S(1)} %copy-done.13, s32[4]{0:T(128)S(1)} %xor_multiply_fusion.at_ref, bf16[32,640]{1,0:T(8,128)(2,1)S(1)} %copy-done.9, bf16[32,1536]{1,0:T(8,128)(2,1)S(1)} %collective-permute-done.refs_1_, ...), custom_call_target="tpu_custom_call" | custom-call | flops 301989888 | bytes 1114112 | tf_op jit(solution)/shard_map/attend/pallas_call | solution.py:68
  55.4 0.0 copy-done.8
  55.4 0.0 collective-permute-done.6.refs_1_
  55.4 1.6 %collective-permute-done.7.refs_2_ = bf16[8,16,256]{2,1,0:T(8,128)(2,1)S(1)} collective-permute-done((bf16[8,16,256]{2,1,0:T(8,128)(2,1)S(1)}, bf16[8,16,256]{2,1,0:T(8,128)(2,1)S(1)}, u32[]{:S(2)}, u32[]{:S(2)}) %collective-permute-start.7) | collective-permute-done | bytes 65568 | tf_op jit(solution)/shard_map/ppermute | solution.py:323
  57.0 0.9 %collective-permute-done.8.refs_3_ = bf16[8,16,256]{2,1,0:T(8,128)(2,1)S(1)} collective-permute-done((bf16[8,16,256]{2,1,0:T(8,128)(2,1)S(1)}, bf16[8,16,256]{2,1,0:T(8,128)(2,1)S(1)}, u32[]{:S(2)}, u32[]{:S(2)}) %collective-permute-start.8) | collective-permute-done | bytes 65568 | tf_op jit(solution)/shard_map/ppermute | solution.py:323
  57.9 0.0 copy-done.14
  58.0 0.6 %copy-done.16 = bf16[8,16,256]{2,1,0:T(8,128)(2,1)} copy-done((bf16[8,16,256]{2,1,0:T(8,128)(2,1)}, bf16[8,16,256]{2,1,0:T(8,128)(2,1)S(1)}, u32[]{:S(2)}) %copy-start.16) | copy-done | bytes 65560
  58.6 1.9 %pick.1 = bf16[128,256]{1,0:T(8,128)(2,1)} custom-call(bf16[128,512]{1,0:T(8,128)(2,1)} %copy-done.6, f32[128,1]{1,0:T(8,128)} %copy-done.7, bf16[8,16,256]{2,1,0:T(8,128)(2,1)} %copy-done.8, bf16[8,16,256]{2,1,0:T(8,128)(2,1)} %copy-done.14, bf16[8,16,256]{2,1,0:T(8,128)(2,1)} %copy-done.15, bf16[8,16,256]{2,1,0:T(8,128)(2,1)} %copy-done.16), custom_call_target="tpu_custom_call" | custom-call | tf_op jit(solution)/shard_map/pick/pallas_call | solution.py:312
  (15 shorter events, 0.1 us)
Async XLA Ops:
  2.5 12.5 %collective-permute-start = (bf16[32,1536]{1,0:T(8,128)(2,1)}, bf16[32,1536]{1,0:T(8,128)(2,1)S(1)}, u32[]{:S(2)}, u32[]{:S(2)}) collective-permute-start(bf16[32,1536]{1,0:T(8,128)(2,1)} %get-tuple-element.33), channel_id=1, source_target_pairs={{0,4},{4,0},{8,12},{12,8},{1,5},{5,1},{9,13},{13,9},{2,6},{6,2},{1... | collective-permute-start | bytes 294920 | tf_op jit(solution)/shard_map/ppermute | solution.py:323
  5.6 10.6 %collective-permute-start.1 = (bf16[32,1536]{1,0:T(8,128)(2,1)}, bf16[32,1536]{1,0:T(8,128)(2,1)S(1)}, u32[]{:S(2)}, u32[]{:S(2)}) collective-permute-start(bf16[32,1536]{1,0:T(8,128)(2,1)} %get-tuple-element.34), channel_id=1, source_target_pairs={{0,8},{4,12},{8,0},{12,4},{1,9},{5,13},{9,1},{13,5},{2,10},{6,14},... | collective-permute-start | bytes 294920 | tf_op jit(solution)/shard_map/ppermute | solution.py:323
  8.2 8.0 %collective-permute-start.2 = (bf16[32,1536]{1,0:T(8,128)(2,1)}, bf16[32,1536]{1,0:T(8,128)(2,1)S(1)}, u32[]{:S(2)}, u32[]{:S(2)}) collective-permute-start(bf16[32,1536]{1,0:T(8,128)(2,1)} %get-tuple-element.35), channel_id=1, source_target_pairs={{0,12},{4,8},{8,4},{12,0},{1,13},{5,9},{9,5},{13,1},{2,14},{6,10},... | collective-permute-start | bytes 294920 | tf_op jit(solution)/shard_map/ppermute | solution.py:323
  8.2 0.7 %copy-start.11 = (s32[16,8]{0,1:T(8,128)S(1)}, s32[16,8]{0,1:T(8,128)}, u32[]{:S(2)}) copy-start(s32[16,8]{0,1:T(8,128)} %param.16) | copy-start | bytes 1540
  8.8 0.7 %copy-start.12 = (f32[16,8]{0,1:T(8,128)S(1)}, f32[16,8]{0,1:T(8,128)}, u32[]{:S(2)}) copy-start(f32[16,8]{0,1:T(8,128)} %param.17) | copy-start | bytes 1540
  9.5 8.3 %copy-start.4 = (bf16[16,7168]{1,0:T(8,128)(2,1)S(1)}, bf16[16,7168]{1,0:T(8,128)(2,1)}, u32[]{:S(2)}) copy-start(bf16[16,7168]{1,0:T(8,128)(2,1)} %own.5) | copy-start | bytes 688132
  15.0 1.2 %copy-start.6 = (bf16[128,512]{1,0:T(8,128)(2,1)}, bf16[128,512]{1,0:T(8,128)(2,1)S(1)}, u32[]{:S(2)}) copy-start(bf16[128,512]{1,0:T(8,128)(2,1)S(1)} %get-tuple-element.43.select_ref) | copy-start | bytes 393220
  15.0 1.2 %copy-start.7 = (f32[128,1]{1,0:T(8,128)}, f32[128,1]{1,0:T(8,128)S(1)}, u32[]{:S(2)}) copy-start(f32[128,1]{1,0:T(8,128)S(1)} %get-tuple-element.44.column_ref) | copy-start | bytes 1540
  16.3 12.8 %collective-permute-start.3 = (bf16[48,1792]{1,0:T(8,128)(2,1)S(1)}, bf16[48,1792]{1,0:T(8,128)(2,1)S(1)}, u32[]{:S(2)}, u32[]{:S(2)}) collective-permute-start(bf16[48,1792]{1,0:T(8,128)(2,1)S(1)} %maximum_maximum_fusion.came), channel_id=1, source_target_pairs={{0,2},{1,3},{2,0},{3,1},{4,6},{5,7},{6,4},{7,5},{8,10},{9,11},{10,... | collective-permute-start | bytes 516104 | tf_op jit(solution)/shard_map/ppermute | solution.py:323
  17.8 11.8 %collective-permute-start.5 = (bf16[48,1792]{1,0:T(8,128)(2,1)S(1)}, bf16[48,1792]{1,0:T(8,128)(2,1)S(1)}, u32[]{:S(2)}, u32[]{:S(2)}) collective-permute-start(bf16[48,1792]{1,0:T(8,128)(2,1)S(1)} %maximum_maximum_fusion.came), channel_id=1, source_target_pairs={{0,1},{1,0},{2,3},{3,2},{4,5},{5,4},{6,7},{7,6},{8,9},{9,8},{10,11... | collective-permute-start | bytes 516104 | tf_op jit(solution)/shard_map/ppermute | solution.py:323
  23.2 2.9 %copy-start = (bf16[8,1792,256]{2,1,0:T(8,128)(2,1)}, bf16[8,1792,256]{2,1,0:T(8,128)(2,1)S(1)}, u32[]{:S(2)}) copy-start(bf16[8,1792,256]{2,1,0:T(8,128)(2,1)S(1)} %get-tuple-element.50.hg) | copy-start | bytes 22020100
  26.1 3.0 %copy-start.2 = (bf16[8,1792,256]{2,1,0:T(8,128)(2,1)}, bf16[8,1792,256]{2,1,0:T(8,128)(2,1)S(1)}, u32[]{:S(2)}) copy-start(bf16[8,1792,256]{2,1,0:T(8,128)(2,1)S(1)} %get-tuple-element.51.hu) | copy-start | bytes 22020100
  29.1 12.0 %collective-permute-start.4 = (bf16[48,1792]{1,0:T(8,128)(2,1)S(1)}, bf16[48,1792]{1,0:T(8,128)(2,1)S(1)}, u32[]{:S(2)}, u32[]{:S(2)}) collective-permute-start(bf16[48,1792]{1,0:T(8,128)(2,1)S(1)} %collective-permute-done.3.came), channel_id=1, source_target_pairs={{0,1},{1,0},{2,3},{3,2},{4,5},{5,4},{6,7},{7,6},{8,9},{9,8},{10,11... | collective-permute-start | bytes 516104 | tf_op jit(solution)/shard_map/ppermute | solution.py:323
  29.6 3.1 %copy-start.1 = (bf16[8,1792,256]{2,1,0:T(8,128)(2,1)S(1)}, bf16[8,1792,256]{2,1,0:T(8,128)(2,1)}, u32[]{:S(2)}) copy-start(bf16[8,1792,256]{2,1,0:T(8,128)(2,1)} %copy-done) | copy-start | bytes 22020100
  32.7 3.1 %copy-start.3 = (bf16[8,1792,256]{2,1,0:T(8,128)(2,1)S(1)}, bf16[8,1792,256]{2,1,0:T(8,128)(2,1)}, u32[]{:S(2)}) copy-start(bf16[8,1792,256]{2,1,0:T(8,128)(2,1)} %copy-done.2) | copy-start | bytes 22020100
  41.1 11.2 %copy-start.5 = (bf16[4,128,576]{1,2,0:T(8,128)(2,1)S(1)}, bf16[4,128,576]{1,2,0:T(8,128)(2,1)}, u32[]{:S(2)}) copy-start(bf16[4,128,576]{1,2,0:T(8,128)(2,1)} %param.12) | copy-start | bytes 1769476
  41.1 11.2 %copy-start.9 = (bf16[32,640]{1,0:T(8,128)(2,1)S(1)}, bf16[32,640]{1,0:T(8,128)(2,1)}, u32[]{:S(2)}) copy-start(bf16[32,640]{1,0:T(8,128)(2,1)} %get-tuple-element.32.refs_0_) | copy-start | bytes 122884
  41.1 11.2 %copy-start.10 = (bf16[4,576]{1,0:T(4,128)(2,1)S(1)}, bf16[4,576]{1,0:T(4,128)(2,1)}, u32[]{:S(2)}) copy-start(bf16[4,576]{1,0:T(4,128)(2,1)} %new_ref.1) | copy-start | bytes 13828
  41.2 11.2 %copy-start.13 = (s32[4]{0:T(128)S(1)}, s32[4]{0:T(128)}, u32[]{:S(2)}) copy-start(s32[4]{0:T(128)} %len_ref.1) | copy-start | bytes 52
  47.9 7.5 %copy-start.8 = (bf16[8,16,256]{2,1,0:T(8,128)(2,1)}, bf16[8,16,256]{2,1,0:T(8,128)(2,1)S(1)}, u32[]{:S(2)}) copy-start(bf16[8,16,256]{2,1,0:T(8,128)(2,1)S(1)} %get-tuple-element.58.refs_0_) | copy-start | bytes 196612
  47.9 7.5 %collective-permute-start.6 = (bf16[8,16,256]{2,1,0:T(8,128)(2,1)S(1)}, bf16[8,16,256]{2,1,0:T(8,128)(2,1)S(1)}, u32[]{:S(2)}, u32[]{:S(2)}) collective-permute-start(bf16[8,16,256]{2,1,0:T(8,128)(2,1)S(1)} %get-tuple-element.59), channel_id=1, source_target_pairs={{0,4},{4,0},{8,12},{12,8},{1,5},{5,1},{9,13},{13,9},{2,6},{6,2},{1... | collective-permute-start | bytes 196616 | tf_op jit(solution)/shard_map/ppermute | solution.py:323
  49.6 7.5 %collective-permute-start.7 = (bf16[8,16,256]{2,1,0:T(8,128)(2,1)S(1)}, bf16[8,16,256]{2,1,0:T(8,128)(2,1)S(1)}, u32[]{:S(2)}, u32[]{:S(2)}) collective-permute-start(bf16[8,16,256]{2,1,0:T(8,128)(2,1)S(1)} %get-tuple-element.60), channel_id=1, source_target_pairs={{0,8},{4,12},{8,0},{12,4},{1,9},{5,13},{9,1},{13,5},{2,10},{6,14},... | collective-permute-start | bytes 196616 | tf_op jit(solution)/shard_map/ppermute | solution.py:323
  51.8 6.2 %collective-permute-start.8 = (bf16[8,16,256]{2,1,0:T(8,128)(2,1)S(1)}, bf16[8,16,256]{2,1,0:T(8,128)(2,1)S(1)}, u32[]{:S(2)}, u32[]{:S(2)}) collective-permute-start(bf16[8,16,256]{2,1,0:T(8,128)(2,1)S(1)} %get-tuple-element.61), channel_id=1, source_target_pairs={{0,12},{4,8},{8,4},{12,0},{1,13},{5,9},{9,5},{13,1},{2,14},{6,10},... | collective-permute-start | bytes 196616 | tf_op jit(solution)/shard_map/ppermute | solution.py:323
  55.4 2.6 %copy-start.14 = (bf16[8,16,256]{2,1,0:T(8,128)(2,1)}, bf16[8,16,256]{2,1,0:T(8,128)(2,1)S(1)}, u32[]{:S(2)}) copy-start(bf16[8,16,256]{2,1,0:T(8,128)(2,1)S(1)} %collective-permute-done.6.refs_1_) | copy-start | bytes 196612
  57.0 0.9 %copy-start.15 = (bf16[8,16,256]{2,1,0:T(8,128)(2,1)}, bf16[8,16,256]{2,1,0:T(8,128)(2,1)S(1)}, u32[]{:S(2)}) copy-start(bf16[8,16,256]{2,1,0:T(8,128)(2,1)S(1)} %collective-permute-done.7.refs_2_) | copy-start | bytes 196612
  57.9 0.6 %copy-start.16 = (bf16[8,16,256]{2,1,0:T(8,128)(2,1)}, bf16[8,16,256]{2,1,0:T(8,128)(2,1)S(1)}, u32[]{:S(2)}) copy-start(bf16[8,16,256]{2,1,0:T(8,128)(2,1)S(1)} %collective-permute-done.8.refs_3_) | copy-start | bytes 196612

commit v3 on v2

--- a/solution.py
+++ b/solution.py
@@ -11,6 +11,8 @@
 ROPE = 64
 GROUP = 128
 CHANNELS = 640
+SCOPE = 4 << 20
+HELD = 14 << 20
 
 qk_scale = 192.0 ** (-0.5)
 VM = pl.BlockSpec(memory_space=pltpu.VMEM)
@@ -30,7 +32,7 @@
     )
 
 
-def attend_kernel(per, q_ref, new_ref, len_ref, at_ref, *refs):
+def attend_kernel(per, q_ref, new_ref, len_ref, *refs):
     pieces, (o_ref, kv_ref) = refs[:-2], refs[-2:]
     rows, width, heads = q_ref.shape
     total = kv_ref.shape[0]
@@ -43,8 +45,8 @@
     kv = kv_ref[...]
     place = lax.broadcasted_iota(jnp.int32, (total, 1), 0)
     start = jnp.zeros_like(place)
-    for d in range(len(pieces)):
-        start = jnp.where(place // block == d, at_ref[d], start)
+    for d in range(len(pieces)) if len(pieces) > 1 else ():
+        start = jnp.where(place // block == d, (lax.axis_index("ep") ^ d) * per, start)
     row_of = place % block // per
     position = start + place % per
     for r in range(rows):
@@ -61,13 +63,13 @@
         ).astype(jnp.bfloat16)
 
 
-def attend(queries, new_latent, prompt_lengths, starts, per, pieces):
+def attend(queries, new_latent, prompt_lengths, per, pieces):
     rows, heads, width = queries.shape
     count = sum(p.shape[0] for p in pieces)
     total = -(-(count + rows) // 128) * 128
     return pl.pallas_call(
         functools.partial(attend_kernel, per),
-        in_specs=[VM, VM, SM, SM] + [VM] * len(pieces),
+        in_specs=[VM, VM, SM] + [VM] * len(pieces),
         out_specs=VM,
         out_shape=jax.ShapeDtypeStruct((rows, heads, LAT), jnp.bfloat16),
         scratch_shapes=[pltpu.VMEM((total, width), jnp.bfloat16)],
@@ -76,9 +78,9 @@
             bytes_accessed=2 * rows * heads * (width + LAT),
             transcendentals=rows * heads * total,
         ),
-        compiler_params=pltpu.CompilerParams(vmem_limit_bytes=8 << 20),
+        compiler_params=pltpu.CompilerParams(vmem_limit_bytes=SCOPE),
         name="attend",
-    )(queries.swapaxes(1, 2), new_latent, prompt_lengths, starts, *pieces)
+    )(queries.swapaxes(1, 2), new_latent, prompt_lengths, *pieces)
 
 
 def pack_kernel(codes_ref, scales_ref, tokens_ref, *refs):
@@ -121,8 +123,30 @@
         out_shape=[jax.ShapeDtypeStruct((block, wide), jnp.bfloat16)] * (n_ep - 1)
         + [jax.ShapeDtypeStruct((block, CHANNELS), jnp.bfloat16)],
         scratch_shapes=[pltpu.VMEM((rows * per, CHANNELS), jnp.float32)],
+        compiler_params=pltpu.CompilerParams(vmem_limit_bytes=SCOPE),
         name="pack",
     )(codes, scales.transpose(2, 1, 0), tokens)
+
+
+def merge_kernel(*refs):
+    sources, out = refs[:-1], refs[-1]
+    rows, half = out.shape[0] // len(sources), out.shape[1] // 2
+    for d, source in enumerate(sources):
+        for c in range(2):
+            out[d * rows : (d + 1) * rows, c * half : (c + 1) * half] = source[
+                c * rows : (c + 1) * rows, :half
+            ]
+
+
+def merge(came, rows, half):
+    return pl.pallas_call(
+        merge_kernel,
+        in_specs=[VM] * len(came),
+        out_specs=VM,
+        out_shape=jax.ShapeDtypeStruct((len(came) * rows, 2 * half), jnp.bfloat16),
+        compiler_params=pltpu.CompilerParams(vmem_limit_bytes=SCOPE),
+        name="merge",
+    )(*came)
 
 
 def part_copies(b, g_ref, u_ref, g_to, u_to, sems):
@@ -183,7 +207,7 @@
         cost_estimate=pl.CostEstimate(
             flops=0, bytes_accessed=4 * experts * shape[1] * wide, transcendentals=0
         ),
-        compiler_params=pltpu.CompilerParams(vmem_limit_bytes=4 << 20),
+        compiler_params=pltpu.CompilerParams(vmem_limit_bytes=SCOPE),
         name="hold",
     )(expert_ids.T, routing_weights.T, w_gate, w_up)
 
@@ -199,7 +223,7 @@
     return jnp.dot(x_ref[...], w_ref[e], preferred_element_type=jnp.float32)
 
 
-def stage_kernel(b, own, came, hg, hu, g_hbm, u_hbm, *refs):
+def stage_kernel(b, first, own, came, hg, hu, g_hbm, u_hbm, *refs):
     total, (gate, up, g_next, u_next, x_ref, sems) = refs[:-6], refs[-6:]
     copies = part_copies(b + 1, g_hbm, u_hbm, g_next, u_next, sems)
     for pair in copies:
@@ -210,8 +234,8 @@
     @pl.loop(0, hg.shape[0])
     def _(e):
         gate_part, up_part = times(x_ref, hg, e), times(x_ref, hu, e)
-        gate[e] = gate_part + total[0][e] if total else gate_part
-        up[e] = up_part + total[1][e] if total else up_part
+        gate[e] = gate_part if first else gate_part + total[0][e]
+        up[e] = up_part if first else up_part + total[1][e]
 
     for pair in copies:
         for copy in pair:
@@ -227,7 +251,7 @@
     rows = own.shape[0] + came.shape[0]
     sums = jax.ShapeDtypeStruct((experts, rows, wide), jnp.float32)
     *total, g_next, u_next = pl.pallas_call(
-        functools.partial(stage_kernel, b),
+        functools.partial(stage_kernel, b, not total),
         in_specs=[VM] * 4 + [HBM] * 2 + [VM] * len(total),
         out_specs=[VM] * 4,
         out_shape=[sums] * 2 + [pltpu.VMEM((experts, depth // 4, wide), jnp.bfloat16)] * 2,
@@ -240,14 +264,14 @@
             bytes_accessed=experts * depth * wide,
             transcendentals=0,
         ),
-        compiler_params=pltpu.CompilerParams(vmem_limit_bytes=8 << 20),
+        compiler_params=pltpu.CompilerParams(vmem_limit_bytes=SCOPE + b * HELD),
         name="stage",
-    )(own, came, *[in_vmem(x) for x in held], w_gate, w_up, *total)
+    )(own, came, *map(in_vmem, held), w_gate, w_up, *total)
     return total, (g_next, u_next)
 
 
 def last_kernel(n_ep, own, came, came_too, hg, hu, g_hbm, u_hbm, gate, up, *refs):
-    outs, (x_ref, y_ref, gb, ub, sems) = refs[:n_ep], refs[n_ep:]
+    outs, (gb, ub, x_ref, y_ref, sems) = refs[:-5], refs[-5:]
     experts, part = hg.shape[0], own.shape[0]
     copies = part_copies(3, g_hbm, u_hbm, gb, ub, sems)
     for pair in copies:
@@ -270,7 +294,6 @@
 def last(n_ep, own, came, came_too, held, total, w_gate, w_up):
     experts, depth, wide = w_gate.shape
     rows = own.shape[0] + came.shape[0]
-    held_shape = (experts, depth // 4, wide)
     out = jax.ShapeDtypeStruct((experts, own.shape[0], wide), jnp.bfloat16)
     return pl.pallas_call(
         functools.partial(last_kernel, n_ep),
@@ -278,10 +301,10 @@
         out_specs=[VM] * n_ep,
         out_shape=[out] * n_ep,
         scratch_shapes=[
+            pltpu.VMEM((experts, depth // 4, wide), jnp.bfloat16),
+            pltpu.VMEM((experts, depth // 4, wide), jnp.bfloat16),
             pltpu.VMEM((rows, depth // 4), jnp.bfloat16),
             pltpu.VMEM((rows, depth // 4), jnp.bfloat16),
-            pltpu.VMEM(held_shape, jnp.bfloat16),
-            pltpu.VMEM(held_shape, jnp.bfloat16),
             pltpu.SemaphoreType.DMA((2, experts)),
         ],
         cost_estimate=pl.CostEstimate(
@@ -289,9 +312,9 @@
             bytes_accessed=experts * depth * wide,
             transcendentals=experts * rows * wide,
         ),
-        compiler_params=pltpu.CompilerParams(vmem_limit_bytes=24 << 20),
+        compiler_params=pltpu.CompilerParams(vmem_limit_bytes=SCOPE + 2 * HELD),
         name="last",
-    )(own, came, came_too, *[in_vmem(x) for x in held], w_gate, w_up, *total)
+    )(own, came, came_too, *map(in_vmem, held), w_gate, w_up, *total)
 
 
 def pick_kernel(select_ref, column_ref, *refs):
@@ -314,6 +337,7 @@
         in_specs=[VM] * (2 + len(blocks)),
         out_specs=VM,
         out_shape=jax.ShapeDtypeStruct((pairs, wide), jnp.bfloat16),
+        compiler_params=pltpu.CompilerParams(vmem_limit_bytes=SCOPE),
         name="pick",
     )(select, column, *blocks)
 
@@ -336,7 +360,6 @@
     w_up,
 ):
     n_ep = lax.axis_size("ep")
-    here = lax.axis_index("ep")
     per = cache_codes.shape[1]
     half = tokens.shape[1] // 8
     rows = tokens.shape[0]
@@ -345,21 +368,15 @@
     w_gate, w_up = [pltpu.with_memory_space_constraint(w, pltpu.HBM) for w in (w_gate, w_up)]
     *held, select, column = hold(expert_ids, routing_weights, w_gate, w_up, n_ep)
     came, held, select, column = lax.optimization_barrier((came, held, select, column))
-    x0 = jnp.concatenate(
-        [jnp.concatenate([x[:rows, :half], x[rows:, :half]], axis=1) for x in came], axis=0
-    )
+    x0 = merge(came, rows, half)
     x1 = crossed(x0, "pf", 1)
     x2 = crossed(x0, "pf", 2)
+    x3 = crossed(x0, "pf", 3)
     total, held = stage(0, tokens, x0, held, (), w_gate, w_up)
-    x2, total = lax.optimization_barrier((x2, total))
-    x3 = crossed(x2, "pf", 1)
     total, held = stage(1, tokens, x1, held, total, w_gate, w_up)
     blocks = last(n_ep, tokens, x2, x3, held, total, w_gate, w_up)
     back = [blocks[0]] + [crossed(blocks[d], "ep", d) for d in range(1, n_ep)]
-    starts = (here ^ jnp.arange(n_ep, dtype=jnp.int32)) * per
-    attention_out = attend(
-        queries, new_latent, prompt_lengths, starts, per, [own_piece] + came
-    )
+    attention_out = attend(queries, new_latent, prompt_lengths, per, [own_piece] + came)
     moe_hidden = pick(select, column, back)
     return attention_out, moe_hidden.reshape(rows, -1, moe_hidden.shape[1])
 
@@ -376,17 +393,12 @@
     w_gate,
     w_up,
 ):
-    n_ep = lax.axis_size("ep")
-    here = lax.axis_index("ep")
     latent = decode_cache(cache_codes, cache_scales)
-    rows_dev = queries.shape[0]
     cache = lax.all_to_all(latent, "ep", split_axis=0, concat_axis=1, tiled=True)
     per = cache.shape[1]
     cache = jnp.pad(cache, ((0, 0), (0, 0), (0, CHANNELS - cache.shape[2])))
-    starts = jnp.zeros((1,), jnp.int32)
-    attention_out = attend(
-        queries, new_latent, prompt_lengths, starts, per, [cache.reshape(-1, CHANNELS)]
-    )
+    cache = cache.reshape(-1, CHANNELS)
+    attention_out = attend(queries, new_latent, prompt_lengths, per, [cache])
     x = lax.all_gather(tokens, "ep", axis=0, tiled=True)
     gate = jnp.einsum("rd,edf->erf", x, w_gate, preferred_element_type=jnp.float32)
     up = jnp.einsum("rd,edf->erf", x, w_up, preferred_element_type=jnp.float32)

time: 60.7 us -> 47.6 us (0.78)
  local copies, waits for them, and re-layouts: 14.1 us -> 3.95 us
  Pallas kernels: 29.6 us -> 26.9 us
    unnamed x34 -> x18, local copies, waits for them, and re-layouts: 14.1 us -> 3.95 us
    pallas_call x1, Pallas kernels: 1.91 us -> 0.15 us  [pack(): pl.pallas_call(pack_kernel, in_specs=[VM] * 3, out_specs=[VM] * n_ep, out...]
    pallas_call x1, Pallas kernels: 1.87 us -> 0.85 us  [pick(): pl.pallas_call(pick_kernel, in_specs=[VM] * (2 + len(blocks)), out_specs=...]
    pallas_call x2 -> x3, Pallas kernels: 10.7 us -> 10.7 us  [the longest x2 10.7 us: stage(): pl.pallas_call(functools.partial(stage_kernel, b, not total), in_specs=[V...]
  transfers between devices with their start and end apart: 9 -> 9, of which waited for: 3 -> 2; matrix products, arithmetic and copies ran while one was open for 0% -> 0% of each run, Pallas kernels for 32% -> 40%
where the time goes in v3:
time: 47.6 us; the launch traced here: 47.3 us
  Pallas kernels  26.9 us (57%)
  starting transfers between devices  12.1 us (25%)
  local copies, waits for them, and re-layouts  3.95 us (8%)
  waiting for transfers between devices  3.57 us (8%)
  between operations  0.76 us (2%)
    ppermute x9, starting transfers between devices, crossed(): return lax.ppermute(x, axis, [(s, s ^ bit) for s in range(n)])  12.1 us
    pallas_call x2, Pallas kernels, stage(): pl.pallas_call(functools.partial(stage_kernel, b, not total), in_specs=[V...  10.7 us
    pallas_call x1, Pallas kernels, last(): pl.pallas_call(functools.partial(last_kernel, n_ep), in_specs=[VM] * 5 +...  6.79 us
    pallas_call x1, Pallas kernels, hold(): pl.pallas_call(hold_kernel, in_specs=[VM, VM, HBM, HBM], out_specs=[VM] *...  5.44 us
    unnamed x18, local copies, waits for them, and re-layouts  3.95 us
    ppermute x9, waiting for transfers between devices, crossed(): return lax.ppermute(x, axis, [(s, s ^ bit) for s in range(n)])  3.57 us
    pallas_call x1, Pallas kernels, attend(): pl.pallas_call(functools.partial(attend_kernel, per), in_specs=[VM, VM, S...  2.99 us
  transfers between devices with their start and end apart: 9, of which 2 were waited for; matrix products, arithmetic and copies ran while one was open for 0% of the time, Pallas kernels for 40%

profile of v3, /device:TPU:0, one launch (start us, length us, event | category | flops | bytes accessed | tf_op | source)
XLA Modules:
  0.0 47.3 jit_solution(6160468146222022781)
XLA Ops:
  0.6 0.0 copy-start
  0.6 0.9 %copy-done = bf16[16,7168]{1,0:T(8,128)(2,1)S(1)} copy-done((bf16[16,7168]{1,0:T(8,128)(2,1)S(1)}, bf16[16,7168]{1,0:T(8,128)(2,1)}, u32[]{:S(2)}) %copy-start) | copy-done | bytes 229400
  1.6 0.0 copy-start.3
  1.6 0.9 %copy-done.3 = bf16[16,8,576]{2,1,0:T(8,128)(2,1)S(1)} copy-done((bf16[16,8,576]{2,1,0:T(8,128)(2,1)S(1)}, bf16[16,8,576]{2,1,0:T(8,128)(2,1)}, u32[]{:S(2)}) %copy-start.3) | copy-done | bytes 147480
  2.5 0.0 copy-start.4
  2.5 0.7 %copy-done.4 = bf16[16,8,5]{0,1,2:T(8,128)(2,1)S(1)} copy-done((bf16[16,8,5]{0,1,2:T(8,128)(2,1)S(1)}, bf16[16,8,5]{0,1,2:T(8,128)(2,1)}, u32[]{:S(2)}) %copy-start.4) | copy-done | bytes 1304
  3.2 0.2 pack.1
  3.4 3.1 %collective-permute-start = (bf16[32,1536]{1,0:T(8,128)(2,1)S(1)}, bf16[32,1536]{1,0:T(8,128)(2,1)S(1)}, u32[]{:S(2)}, u32[]{:S(2)}) collective-permute-start(bf16[32,1536]{1,0:T(8,128)(2,1)S(1)} %get-tuple-element.30), channel_id=1, source_target_pairs={{0,4},{4,0},{8,12},{12,8},{1,5},{5,1},{9,13},{13,9},{2,6},{6,2},{1... | collective-permute-start | bytes 294920 | tf_op jit(solution)/shard_map/ppermute | solution.py:347
  6.4 2.6 %collective-permute-start.1 = (bf16[32,1536]{1,0:T(8,128)(2,1)S(1)}, bf16[32,1536]{1,0:T(8,128)(2,1)S(1)}, u32[]{:S(2)}, u32[]{:S(2)}) collective-permute-start(bf16[32,1536]{1,0:T(8,128)(2,1)S(1)} %get-tuple-element.31), channel_id=1, source_target_pairs={{0,8},{4,12},{8,0},{12,4},{1,9},{5,13},{9,1},{13,5},{2,10},{6,14},... | collective-permute-start | bytes 294920 | tf_op jit(solution)/shard_map/ppermute | solution.py:347
  9.0 0.0 collective-permute-start.2
  9.0 0.0 copy-start.6
  9.0 0.7 %copy-done.6 = s32[16,8]{0,1:T(8,128)S(1)} copy-done((s32[16,8]{0,1:T(8,128)S(1)}, s32[16,8]{0,1:T(8,128)}, u32[]{:S(2)}) %copy-start.6) | copy-done | bytes 536
  9.7 0.0 copy-start.7
  9.7 0.7 %copy-done.7 = f32[16,8]{0,1:T(8,128)S(1)} copy-done((f32[16,8]{0,1:T(8,128)S(1)}, f32[16,8]{0,1:T(8,128)}, u32[]{:S(2)}) %copy-start.7) | copy-done | bytes 536
  10.4 0.0 copy-start.1
  10.4 5.4 %hold.1 = (bf16[8,1792,256]{2,1,0:T(8,128)(2,1)S(1)}, bf16[8,1792,256]{2,1,0:T(8,128)(2,1)S(1)}, bf16[128,512]{1,0:T(8,128)(2,1)S(1)}, f32[128,1]{1,0:T(8,128)S(1)}) custom-call(s32[8,16]{1,0:T(8,128)S(1)} %bitcast.7, f32[8,16]{1,0:T(8,128)S(1)} %bitcast.8, bf16[8,7168,256]{2,1,0:T(8,128)(2,1)} %g_hbm.5, bf16[8,7168,256]{2,1,0:T(8,128)(2,1)} %u_hbm.5), custom_call_target="tpu_custom_call" | custom-call | bytes 14680064 | tf_op jit(solution)/shard_map/hold/pallas_call | solution.py:197
  15.9 0.0 collective-permute-done.refs_1_.refs_0_
  15.9 1.0 %collective-permute-done.1.refs_2_.refs_1_ = bf16[32,1536]{1,0:T(8,128)(2,1)S(1)} collective-permute-done((bf16[32,1536]{1,0:T(8,128)(2,1)S(1)}, bf16[32,1536]{1,0:T(8,128)(2,1)S(1)}, u32[]{:S(2)}, u32[]{:S(2)}) %collective-permute-start.1) | collective-permute-done | bytes 98336 | tf_op jit(solution)/shard_map/ppermute | solution.py:347
  16.9 0.0 collective-permute-done.2.refs_3_.refs_2_
  16.9 0.1 collective-permute-start.5
  17.0 1.6 %collective-permute-start.3 = (bf16[48,1792]{1,0:T(8,128)(2,1)S(1)}, bf16[48,1792]{1,0:T(8,128)(2,1)S(1)}, u32[]{:S(2)}, u32[]{:S(2)}) collective-permute-start(bf16[48,1792]{1,0:T(8,128)(2,1)S(1)} %merge.1.came), channel_id=1, source_target_pairs={{0,2},{1,3},{2,0},{3,1},{4,6},{5,7},{6,4},{7,5},{8,10},{9,11},{10,... | collective-permute-start | bytes 516104 | tf_op jit(solution)/shard_map/ppermute | solution.py:347
  18.5 0.3 collective-permute-start.4
  18.8 0.0 copy-done.1
  18.8 5.3 %stage.2 = (f32[8,64,256]{2,1,0:T(8,128)S(1)}, f32[8,64,256]{2,1,0:T(8,128)S(1)}, bf16[8,1792,256]{2,1,0:T(8,128)(2,1)S(1)}, bf16[8,1792,256]{2,1,0:T(8,128)(2,1)S(1)}) custom-call(bf16[16,7168]{1,0:T(8,128)(2,1)S(1)} %copy-done.1, bf16[48,1792]{1,0:T(8,128)(2,1)S(1)} %merge.1.came, bf16[8,1792,256]{2,1,0:T(8,128)(2,1)S(1)} %get-tuple-element.42.hg, ...), custom_call_target="tpu_custom_call" | custom-call | flops 939524096 | bytes 14680064 | tf_op jit(solution)/shard_map/stage/pallas_call | solution.py:253
  24.2 0.0 collective-permute-done.5.came
  24.2 5.3 %stage.3 = (f32[8,64,256]{2,1,0:T(8,128)S(1)}, f32[8,64,256]{2,1,0:T(8,128)S(1)}, bf16[8,1792,256]{2,1,0:T(8,128)(2,1)S(1)}, bf16[8,1792,256]{2,1,0:T(8,128)(2,1)S(1)}) custom-call(bf16[16,7168]{1,0:T(8,128)(2,1)S(1)} %copy-done.1, bf16[48,1792]{1,0:T(8,128)(2,1)S(1)} %collective-permute-done.5.came, bf16[8,1792,256]{2,1,0:T(8,128)(2,1)S(1)} %get-tuple-element.44.hg, ...), custom_call_target="tpu_custom_call" | custom-call | flops 939524096 | bytes 14680064 | tf_op jit(solution)/shard_map/stage/pallas_call | solution.py:253
  29.5 0.0 collective-permute-done.3.came
  29.5 0.0 collective-permute-done.4.came_too
  29.6 0.0 copy-start.2
  29.6 0.0 copy-start.5
  29.6 0.0 copy-start.8
  29.6 6.8 %last.1 = (bf16[8,16,256]{2,1,0:T(8,128)(2,1)S(1)}, bf16[8,16,256]{2,1,0:T(8,128)(2,1)S(1)}, bf16[8,16,256]{2,1,0:T(8,128)(2,1)S(1)}, bf16[8,16,256]{2,1,0:T(8,128)(2,1)S(1)}) custom-call(bf16[16,7168]{1,0:T(8,128)(2,1)S(1)} %copy-done.1, bf16[48,1792]{1,0:T(8,128)(2,1)S(1)} %collective-permute-done.3.came, ...), custom_call_target="tpu_custom_call" | custom-call | flops 1879048192 | bytes 14680064 | tf_op jit(solution)/shard_map/last/pallas_call | solution.py:298
  36.4 1.7 %collective-permute-start.6 = (bf16[8,16,256]{2,1,0:T(8,128)(2,1)S(1)}, bf16[8,16,256]{2,1,0:T(8,128)(2,1)S(1)}, u32[]{:S(2)}, u32[]{:S(2)}) collective-permute-start(bf16[8,16,256]{2,1,0:T(8,128)(2,1)S(1)} %get-tuple-element.53), channel_id=1, source_target_pairs={{0,4},{4,0},{8,12},{12,8},{1,5},{5,1},{9,13},{13,9},{2,6},{6,2},{1... | collective-permute-start | bytes 196616 | tf_op jit(solution)/shard_map/ppermute | solution.py:347
  38.1 1.8 %collective-permute-start.7 = (bf16[8,16,256]{2,1,0:T(8,128)(2,1)S(1)}, bf16[8,16,256]{2,1,0:T(8,128)(2,1)S(1)}, u32[]{:S(2)}, u32[]{:S(2)}) collective-permute-start(bf16[8,16,256]{2,1,0:T(8,128)(2,1)S(1)} %get-tuple-element.54), channel_id=1, source_target_pairs={{0,8},{4,12},{8,0},{12,4},{1,9},{5,13},{9,1},{13,5},{2,10},{6,14},... | collective-permute-start | bytes 196616 | tf_op jit(solution)/shard_map/ppermute | solution.py:347
  39.9 1.0 %collective-permute-start.8 = (bf16[8,16,256]{2,1,0:T(8,128)(2,1)S(1)}, bf16[8,16,256]{2,1,0:T(8,128)(2,1)S(1)}, u32[]{:S(2)}, u32[]{:S(2)}) collective-permute-start(bf16[8,16,256]{2,1,0:T(8,128)(2,1)S(1)} %get-tuple-element.55), channel_id=1, source_target_pairs={{0,12},{4,8},{8,4},{12,0},{1,13},{5,9},{9,5},{13,1},{2,14},{6,10},... | collective-permute-start | bytes 196616 | tf_op jit(solution)/shard_map/ppermute | solution.py:347
  40.8 0.0 copy-done.2
  40.8 0.0 copy-done.5
  40.8 0.0 copy-done.8
  40.8 3.0 %attend.1 = bf16[4,128,512]{2,1,0:T(8,128)(2,1)} custom-call(bf16[4,576,128]{2,1,0:T(8,128)(2,1)S(1)} %bitcast.5, bf16[4,576]{1,0:T(4,128)(2,1)S(1)} %copy-done.5, s32[4]{0:T(128)S(1)} %copy-done.8, bf16[32,640]{1,0:T(8,128)(2,1)S(1)} %get-tuple-element.29.refs_0_, bf16[32,1536]{1,0:T(8,128)(2,1)S(1)} %collective-permute-done.refs_1_.refs_0_, ...), custom_call_target="tpu_custom_call" | custom-call | flops 301989888 | bytes 1114112 | tf_op jit(solution)/shard_map/attend/pallas_call | solution.py:70
  43.8 0.0 collective-permute-done.6.refs_1_
  43.8 2.6 %collective-permute-done.7.refs_2_ = bf16[8,16,256]{2,1,0:T(8,128)(2,1)S(1)} collective-permute-done((bf16[8,16,256]{2,1,0:T(8,128)(2,1)S(1)}, bf16[8,16,256]{2,1,0:T(8,128)(2,1)S(1)}, u32[]{:S(2)}, u32[]{:S(2)}) %collective-permute-start.7) | collective-permute-done | bytes 65568 | tf_op jit(solution)/shard_map/ppermute | solution.py:347
  46.4 0.0 collective-permute-done.8.refs_3_
  46.4 0.9 %pick.1 = bf16[128,256]{1,0:T(8,128)(2,1)} custom-call(bf16[128,512]{1,0:T(8,128)(2,1)S(1)} %get-tuple-element.40.select_ref, f32[128,1]{1,0:T(8,128)S(1)} %get-tuple-element.41.column_ref, bf16[8,16,256]{2,1,0:T(8,128)(2,1)S(1)} %get-tuple-element.52.refs_0_, bf16[8,16,256]{2,1,0:T(8,128)(2,1)S(1)} %collective-permute-done.6.refs_1_, ...), custom_call_target="tpu_custom_call" | custom-call | tf_op jit(solution)/shard_map/pick/pallas_call | solution.py:335
  (1 shorter events, 0.0 us)
Async XLA Ops:
  0.6 0.9 %copy-start = (bf16[16,7168]{1,0:T(8,128)(2,1)S(1)}, bf16[16,7168]{1,0:T(8,128)(2,1)}, u32[]{:S(2)}) copy-start(bf16[16,7168]{1,0:T(8,128)(2,1)} %own.5) | copy-start | bytes 688132
  1.6 0.9 %copy-start.3 = (bf16[16,8,576]{2,1,0:T(8,128)(2,1)S(1)}, bf16[16,8,576]{2,1,0:T(8,128)(2,1)}, u32[]{:S(2)}) copy-start(bf16[16,8,576]{2,1,0:T(8,128)(2,1)} %codes_ref.1) | copy-start | bytes 442372
  2.5 0.7 %copy-start.4 = (bf16[16,8,5]{0,1,2:T(8,128)(2,1)S(1)}, bf16[16,8,5]{0,1,2:T(8,128)(2,1)}, u32[]{:S(2)}) copy-start(bf16[16,8,5]{0,1,2:T(8,128)(2,1)} %param.11) | copy-start | bytes 3844
  3.4 12.5 %collective-permute-start = (bf16[32,1536]{1,0:T(8,128)(2,1)S(1)}, bf16[32,1536]{1,0:T(8,128)(2,1)S(1)}, u32[]{:S(2)}, u32[]{:S(2)}) collective-permute-start(bf16[32,1536]{1,0:T(8,128)(2,1)S(1)} %get-tuple-element.30), channel_id=1, source_target_pairs={{0,4},{4,0},{8,12},{12,8},{1,5},{5,1},{9,13},{13,9},{2,6},{6,2},{1... | collective-permute-start | bytes 294920 | tf_op jit(solution)/shard_map/ppermute | solution.py:347
  6.4 10.4 %collective-permute-start.1 = (bf16[32,1536]{1,0:T(8,128)(2,1)S(1)}, bf16[32,1536]{1,0:T(8,128)(2,1)S(1)}, u32[]{:S(2)}, u32[]{:S(2)}) collective-permute-start(bf16[32,1536]{1,0:T(8,128)(2,1)S(1)} %get-tuple-element.31), channel_id=1, source_target_pairs={{0,8},{4,12},{8,0},{12,4},{1,9},{5,13},{9,1},{13,5},{2,10},{6,14},... | collective-permute-start | bytes 294920 | tf_op jit(solution)/shard_map/ppermute | solution.py:347
  9.0 7.8 %collective-permute-start.2 = (bf16[32,1536]{1,0:T(8,128)(2,1)S(1)}, bf16[32,1536]{1,0:T(8,128)(2,1)S(1)}, u32[]{:S(2)}, u32[]{:S(2)}) collective-permute-start(bf16[32,1536]{1,0:T(8,128)(2,1)S(1)} %get-tuple-element.32), channel_id=1, source_target_pairs={{0,12},{4,8},{8,4},{12,0},{1,13},{5,9},{9,5},{13,1},{2,14},{6,10},... | collective-permute-start | bytes 294920 | tf_op jit(solution)/shard_map/ppermute | solution.py:347
  9.0 0.7 %copy-start.6 = (s32[16,8]{0,1:T(8,128)S(1)}, s32[16,8]{0,1:T(8,128)}, u32[]{:S(2)}) copy-start(s32[16,8]{0,1:T(8,128)} %param.16) | copy-start | bytes 1540
  9.7 0.7 %copy-start.7 = (f32[16,8]{0,1:T(8,128)S(1)}, f32[16,8]{0,1:T(8,128)}, u32[]{:S(2)}) copy-start(f32[16,8]{0,1:T(8,128)} %param.17) | copy-start | bytes 1540
  10.4 8.4 %copy-start.1 = (bf16[16,7168]{1,0:T(8,128)(2,1)S(1)}, bf16[16,7168]{1,0:T(8,128)(2,1)}, u32[]{:S(2)}) copy-start(bf16[16,7168]{1,0:T(8,128)(2,1)} %own.5) | copy-start | bytes 688132
  16.9 7.3 %collective-permute-start.5 = (bf16[48,1792]{1,0:T(8,128)(2,1)S(1)}, bf16[48,1792]{1,0:T(8,128)(2,1)S(1)}, u32[]{:S(2)}, u32[]{:S(2)}) collective-permute-start(bf16[48,1792]{1,0:T(8,128)(2,1)S(1)} %merge.1.came), channel_id=1, source_target_pairs={{0,1},{1,0},{2,3},{3,2},{4,5},{5,4},{6,7},{7,6},{8,9},{9,8},{10,11... | collective-permute-start | bytes 516104 | tf_op jit(solution)/shard_map/ppermute | solution.py:347
  17.0 12.6 %collective-permute-start.3 = (bf16[48,1792]{1,0:T(8,128)(2,1)S(1)}, bf16[48,1792]{1,0:T(8,128)(2,1)S(1)}, u32[]{:S(2)}, u32[]{:S(2)}) collective-permute-start(bf16[48,1792]{1,0:T(8,128)(2,1)S(1)} %merge.1.came), channel_id=1, source_target_pairs={{0,2},{1,3},{2,0},{3,1},{4,6},{5,7},{6,4},{7,5},{8,10},{9,11},{10,... | collective-permute-start | bytes 516104 | tf_op jit(solution)/shard_map/ppermute | solution.py:347
  18.5 11.0 %collective-permute-start.4 = (bf16[48,1792]{1,0:T(8,128)(2,1)S(1)}, bf16[48,1792]{1,0:T(8,128)(2,1)S(1)}, u32[]{:S(2)}, u32[]{:S(2)}) collective-permute-start(bf16[48,1792]{1,0:T(8,128)(2,1)S(1)} %merge.1.came), channel_id=1, source_target_pairs={{0,3},{1,2},{2,1},{3,0},{4,7},{5,6},{6,5},{7,4},{8,11},{9,10},{10,... | collective-permute-start | bytes 516104 | tf_op jit(solution)/shard_map/ppermute | solution.py:347
  29.6 11.3 %copy-start.2 = (bf16[4,128,576]{1,2,0:T(8,128)(2,1)S(1)}, bf16[4,128,576]{1,2,0:T(8,128)(2,1)}, u32[]{:S(2)}) copy-start(bf16[4,128,576]{1,2,0:T(8,128)(2,1)} %param.12) | copy-start | bytes 1769476
  29.6 11.3 %copy-start.5 = (bf16[4,576]{1,0:T(4,128)(2,1)S(1)}, bf16[4,576]{1,0:T(4,128)(2,1)}, u32[]{:S(2)}) copy-start(bf16[4,576]{1,0:T(4,128)(2,1)} %new_ref.1) | copy-start | bytes 13828
  29.6 11.3 %copy-start.8 = (s32[4]{0:T(128)S(1)}, s32[4]{0:T(128)}, u32[]{:S(2)}) copy-start(s32[4]{0:T(128)} %len_ref.1) | copy-start | bytes 52
  36.4 7.5 %collective-permute-start.6 = (bf16[8,16,256]{2,1,0:T(8,128)(2,1)S(1)}, bf16[8,16,256]{2,1,0:T(8,128)(2,1)S(1)}, u32[]{:S(2)}, u32[]{:S(2)}) collective-permute-start(bf16[8,16,256]{2,1,0:T(8,128)(2,1)S(1)} %get-tuple-element.53), channel_id=1, source_target_pairs={{0,4},{4,0},{8,12},{12,8},{1,5},{5,1},{9,13},{13,9},{2,6},{6,2},{1... | collective-permute-start | bytes 196616 | tf_op jit(solution)/shard_map/ppermute | solution.py:347
  38.1 8.4 %collective-permute-start.7 = (bf16[8,16,256]{2,1,0:T(8,128)(2,1)S(1)}, bf16[8,16,256]{2,1,0:T(8,128)(2,1)S(1)}, u32[]{:S(2)}, u32[]{:S(2)}) collective-permute-start(bf16[8,16,256]{2,1,0:T(8,128)(2,1)S(1)} %get-tuple-element.54), channel_id=1, source_target_pairs={{0,8},{4,12},{8,0},{12,4},{1,9},{5,13},{9,1},{13,5},{2,10},{6,14},... | collective-permute-start | bytes 196616 | tf_op jit(solution)/shard_map/ppermute | solution.py:347
  39.9 6.5 %collective-permute-start.8 = (bf16[8,16,256]{2,1,0:T(8,128)(2,1)S(1)}, bf16[8,16,256]{2,1,0:T(8,128)(2,1)S(1)}, u32[]{:S(2)}, u32[]{:S(2)}) collective-permute-start(bf16[8,16,256]{2,1,0:T(8,128)(2,1)S(1)} %get-tuple-element.55), channel_id=1, source_target_pairs={{0,12},{4,8},{8,4},{12,0},{1,13},{5,9},{9,5},{13,1},{2,14},{6,10},... | collective-permute-start | bytes 196616 | tf_op jit(solution)/shard_map/ppermute | solution.py:347

commit v4 on v3

--- a/solution.py
+++ b/solution.py
@@ -10,8 +10,11 @@
 LAT = 512
 ROPE = 64
 GROUP = 128
+TOP = 8
+EARLY = 2
 CHANNELS = 640
 SCOPE = 4 << 20
+ORDER = (2, 3, 1)
 HELD = 14 << 20
 
 qk_scale = 192.0 ** (-0.5)
@@ -83,49 +86,91 @@
     )(queries.swapaxes(1, 2), new_latent, prompt_lengths, *pieces)
 
 
-def pack_kernel(codes_ref, scales_ref, tokens_ref, *refs):
-    outs, own, lat_ref = refs[:-2], refs[-2], refs[-1]
+def pack_kernel(codes_hbm, scales_hbm, tokens_hbm, ids_hbm, *refs):
+    outs, own, (codes_ref, scales_ref, ids_ref, lat_ref, sems, token_sems) = (
+        refs[:-7],
+        refs[-7],
+        refs[-6:],
+    )
     rows, per, width = codes_ref.shape
     groups = scales_ref.shape[0]
     block = own.shape[0]
+    half = tokens_hbm.shape[1] // 8
     here, me = lax.axis_index("ep"), lax.axis_index("pf")
+    cache = [
+        pltpu.make_async_copy(codes_hbm, codes_ref, sems.at[0]),
+        pltpu.make_async_copy(scales_hbm, scales_ref, sems.at[1]),
+        pltpu.make_async_copy(ids_hbm, ids_ref, sems.at[2]),
+    ]
+    token_copies = []
+    for d, out in enumerate(outs):
+        for c in range(2):
+            start = pl.multiple_of((2 * me + c) * half, 128)
+            token_copies.append(
+                pltpu.make_async_copy(
+                    tokens_hbm.at[:, pl.ds(start, half)],
+                    out.at[pl.ds(c * block // 2, block // 2), pl.ds(0, half)],
+                    token_sems.at[d, c],
+                )
+            )
+    for copy in cache + token_copies:
+        copy.start()
+    lat_ref[:, width:] = jnp.zeros((rows * per, CHANNELS - width), jnp.float32)
+    for copy in cache:
+        copy.wait()
     scales = scales_ref[...].astype(jnp.float32)
-    lat_ref[:, width:] = jnp.zeros((rows * per, CHANNELS - width), jnp.float32)
+    top, named = ids_ref.shape
+    for d in range(len(outs) + 1):
+        lat_ref[d * block : d * block + top, width : width + named] = ids_ref[...].astype(
+            jnp.float32
+        )
     for r in range(rows):
         for g in range(groups):
             columns = slice(g * GROUP, min((g + 1) * GROUP, width))
             lat_ref[r * per : (r + 1) * per, columns] = (
                 codes_ref[r, :, columns].astype(jnp.float32) * scales[g, :, r : r + 1]
             )
-    half = tokens_ref.shape[1] // 8
     for d in range(len(outs) + 1):
         start = pl.multiple_of((here ^ d) * block, block)
         part = lat_ref[pl.ds(start, block), :].astype(jnp.bfloat16)
         if d == 0:
             own[...] = part
-            continue
-        outs[d - 1][:, half:] = part
-        for c in range(2):
-            start = pl.multiple_of((2 * me + c) * half, 128)
-            outs[d - 1][c * block // 2 : (c + 1) * block // 2, :half] = tokens_ref[
-                :, pl.ds(start, half)
-            ]
-
-
-def pack(codes, scales, tokens, n_ep):
+        else:
+            outs[ORDER.index(d)][:, half:] = part
+    for copy in token_copies:
+        copy.wait()
+
+
+def in_hbm(x):
+    return pltpu.with_memory_space_constraint(x, pltpu.HBM)
+
+
+def in_vmem(x):
+    return pltpu.with_memory_space_constraint(x, pltpu.VMEM)
+
+
+def pack(codes, scales, tokens, expert_ids, n_ep):
     rows, per, width = codes.shape
     block = rows * per // n_ep
     wide = tokens.shape[1] // 8 + CHANNELS
+    scales, ids = scales.transpose(2, 1, 0), expert_ids.T
     return pl.pallas_call(
         pack_kernel,
-        in_specs=[VM] * 3,
+        in_specs=[HBM] * 4,
         out_specs=[VM] * n_ep,
         out_shape=[jax.ShapeDtypeStruct((block, wide), jnp.bfloat16)] * (n_ep - 1)
         + [jax.ShapeDtypeStruct((block, CHANNELS), jnp.bfloat16)],
-        scratch_shapes=[pltpu.VMEM((rows * per, CHANNELS), jnp.float32)],
+        scratch_shapes=[
+            pltpu.VMEM(codes.shape, jnp.bfloat16),
+            pltpu.VMEM(scales.shape, jnp.bfloat16),
+            pltpu.VMEM(ids.shape, jnp.int32),
+            pltpu.VMEM((rows * per, CHANNELS), jnp.float32),
+            pltpu.SemaphoreType.DMA((3,)),
+            pltpu.SemaphoreType.DMA((n_ep - 1, 2)),
+        ],
         compiler_params=pltpu.CompilerParams(vmem_limit_bytes=SCOPE),
         name="pack",
-    )(codes, scales.transpose(2, 1, 0), tokens)
+    )(in_hbm(codes), in_hbm(scales), in_hbm(tokens), in_hbm(ids))
 
 
 def merge_kernel(*refs):
@@ -149,67 +194,98 @@
     )(*came)
 
 
-def part_copies(b, g_ref, u_ref, g_to, u_to, sems):
+def part_copies(b, first, g_ref, u_ref, g_to, u_to, sems):
     depth = g_to.shape[1]
     start = pl.multiple_of((lax.axis_index("pf") ^ b) * depth, 128)
+    rows = pl.ds(start, depth)
     return [
         (
-            pltpu.make_async_copy(g_ref.at[e, pl.ds(start, depth)], g_to.at[e], sems.at[0, e]),
-            pltpu.make_async_copy(u_ref.at[e, pl.ds(start, depth)], u_to.at[e], sems.at[1, e]),
+            pltpu.make_async_copy(g_ref.at[first + e, rows], g_to.at[e], sems.at[0, e]),
+            pltpu.make_async_copy(u_ref.at[first + e, rows], u_to.at[e], sems.at[1, e]),
         )
         for e in range(g_to.shape[0])
     ]
 
 
-def hold_kernel(ids_ref, weight_ref, g_ref, u_ref, go_ref, uo_ref, select_ref, column_ref, sems):
-    copies = part_copies(0, g_ref, u_ref, go_ref, uo_ref, sems)
-    for pair in copies:
+def start_all(pairs):
+    for pair in pairs:
         for copy in pair:
             copy.start()
+
+
+def wait_all(pairs):
+    for pair in pairs:
+        for copy in pair:
+            copy.wait()
+
+
+def hold_kernel(ids_hbm, weight_hbm, g_ref, u_ref, *refs):
+    own_gate, own_up, next_gate, next_up, select_ref, column_ref = refs[:6]
+    ids_ref, weight_ref, few_sems, sems, next_sems = refs[6:]
+    few = [
+        (
+            pltpu.make_async_copy(ids_hbm, ids_ref, few_sems.at[0]),
+            pltpu.make_async_copy(weight_hbm, weight_ref, few_sems.at[1]),
+        )
+    ]
+    copies = part_copies(0, 0, g_ref, u_ref, own_gate, own_up, sems)
+    copies += part_copies(1, 0, g_ref, u_ref, next_gate, next_up, next_sems)
+    start_all(few)
+    start_all(copies)
+    wait_all(few)
     top, rows = ids_ref.shape
     experts = g_ref.shape[0]
+    slots = rows // 2
     here = lax.axis_index("ep")
     pair = lax.broadcasted_iota(jnp.int32, (top * rows, 1), 0)
+    other = lax.broadcasted_iota(jnp.int32, (top * rows, rows), 1)
     ids = jnp.zeros((top * rows, rows), jnp.int32)
     weight = jnp.zeros((top * rows, rows), jnp.float32)
-    mine = lax.broadcasted_iota(jnp.int32, (top * rows, rows), 1) == pair // top
     for k in range(top):
-        chosen = mine & (pair % top == k)
+        chosen = (other == pair // top) & (pair % top == k)
         ids = jnp.where(chosen, ids_ref[k : k + 1, :], ids)
         weight = jnp.where(chosen, weight_ref[k : k + 1, :], weight)
     ids = jnp.sum(ids, axis=1, keepdims=True)
     column_ref[...] = jnp.sum(weight, axis=1, keepdims=True)
-    column = lax.broadcasted_iota(jnp.int32, (1, experts * rows), 1)
-    for d in range(select_ref.shape[1] // (experts * rows)):
-        match = (ids == (here ^ d) * experts + column // rows) & (column % rows == pair // top)
-        select_ref[:, d * experts * rows : (d + 1) * experts * rows] = jnp.where(
+    earlier = jnp.zeros((top * rows, rows), jnp.int32)
+    for k in range(top):
+        earlier += jnp.where((ids_ref[k : k + 1, :] == ids) & (other < pair // top), 1, 0)
+    slot = jnp.sum(earlier, axis=1, keepdims=True)
+    column = lax.broadcasted_iota(jnp.int32, (1, experts * slots), 1)
+    for i, d in enumerate((0,) + ORDER):
+        match = (ids == (here ^ d) * experts + column // slots) & (column % slots == slot)
+        select_ref[:, i * experts * slots : (i + 1) * experts * slots] = jnp.where(
             match, 1.0, 0.0
         ).astype(jnp.bfloat16)
-    for pair in copies:
-        for copy in pair:
-            copy.wait()
+    wait_all(copies)
 
 
 def hold(expert_ids, routing_weights, w_gate, w_up, n_ep):
     experts, depth, wide = w_gate.shape
     rows, top = expert_ids.shape
-    shape = (experts, depth // 4, wide)
+    shapes = [(n, depth // 4, wide) for n in (experts, experts, EARLY, EARLY)]
     return pl.pallas_call(
         hold_kernel,
-        in_specs=[VM, VM, HBM, HBM],
-        out_specs=[VM] * 4,
-        out_shape=[pltpu.VMEM(shape, jnp.bfloat16)] * 2
+        in_specs=[HBM] * 4,
+        out_specs=[VM] * 6,
+        out_shape=[pltpu.VMEM(shape, jnp.bfloat16) for shape in shapes]
         + [
-            jax.ShapeDtypeStruct((rows * top, n_ep * experts * rows), jnp.bfloat16),
+            jax.ShapeDtypeStruct((rows * top, n_ep * experts * rows // 2), jnp.bfloat16),
             jax.ShapeDtypeStruct((rows * top, 1), jnp.float32),
         ],
-        scratch_shapes=[pltpu.SemaphoreType.DMA((2, experts))],
+        scratch_shapes=[
+            pltpu.VMEM((top, rows), jnp.int32),
+            pltpu.VMEM((top, rows), jnp.float32),
+            pltpu.SemaphoreType.DMA((2,)),
+            pltpu.SemaphoreType.DMA((2, experts)),
+            pltpu.SemaphoreType.DMA((2, EARLY)),
+        ],
         cost_estimate=pl.CostEstimate(
-            flops=0, bytes_accessed=4 * experts * shape[1] * wide, transcendentals=0
+            flops=0, bytes_accessed=(experts + EARLY) * depth * wide, transcendentals=0
         ),
         compiler_params=pltpu.CompilerParams(vmem_limit_bytes=SCOPE),
         name="hold",
-    )(expert_ids.T, routing_weights.T, w_gate, w_up)
+    )(in_hbm(expert_ids.T), in_hbm(routing_weights.T), w_gate, w_up)
 
 
 def set_rows(b, x_ref, own_ref, came_ref):
@@ -223,98 +299,163 @@
     return jnp.dot(x_ref[...], w_ref[e], preferred_element_type=jnp.float32)
 
 
-def stage_kernel(b, first, own, came, hg, hu, g_hbm, u_hbm, *refs):
-    total, (gate, up, g_next, u_next, x_ref, sems) = refs[:-6], refs[-6:]
-    copies = part_copies(b + 1, g_hbm, u_hbm, g_next, u_next, sems)
-    for pair in copies:
-        for copy in pair:
-            copy.start()
-    set_rows(b, x_ref, own, came)
-
-    @pl.loop(0, hg.shape[0])
+def set_slots(pieces, slots_ref, experts, rows, top):
+    n_ep = len(pieces)
+    slots = rows // 2
+    wide = CHANNELS - LAT
+    ids = jnp.zeros((top, n_ep * rows), jnp.float32)
+    for d, piece in enumerate(pieces):
+        tail = piece[: 2 * top, piece.shape[1] - wide :][:top]
+        lane = lax.broadcasted_iota(jnp.int32, (wide, n_ep * rows), 0)
+        column = lax.broadcasted_iota(jnp.int32, (wide, n_ep * rows), 1)
+        take = (lane == ROPE + column % rows) & (column // rows == d)
+        ids += jnp.dot(
+            tail, jnp.where(take, 1.0, 0.0).astype(jnp.bfloat16), preferred_element_type=jnp.float32
+        )
+    shape = slots_ref.shape
+    place = lax.broadcasted_iota(jnp.int32, shape, 0)
+    column = lax.broadcasted_iota(jnp.int32, shape, 1)
+    expert = lax.axis_index("ep") * experts + place // (n_ep * slots)
+    named = jnp.zeros(shape, jnp.float32)
+    for k in range(top):
+        named += jnp.where(ids[k : k + 1, :].astype(jnp.int32) == expert, 1.0, 0.0)
+    named = jnp.where(place % (n_ep * slots) // slots == column // rows, named, 0.0)
+    above = lax.broadcasted_iota(jnp.int32, (n_ep * rows,) * 2, 0)
+    below = lax.broadcasted_iota(jnp.int32, (n_ep * rows,) * 2, 1)
+    before = jnp.where((above // rows == below // rows) & (above < below), 1.0, 0.0)
+    rank = jnp.dot(
+        named.astype(jnp.bfloat16), before.astype(jnp.bfloat16), preferred_element_type=jnp.float32
+    )
+    slot = (place % slots).astype(jnp.float32)
+    slots_ref[...] = jnp.where((named > 0.5) & (rank == slot), 1.0, 0.0).astype(jnp.bfloat16)
+
+
+def first_kernel(own, came, hg, hu, next_gate, next_up, g_hbm, u_hbm, *refs):
+    pieces, (gate, up, g_to, u_to, slots_ref, x_ref, sems) = refs[:-7], refs[-7:]
+    experts = hg.shape[0]
+    copies = part_copies(1, EARLY, g_hbm, u_hbm, g_to, u_to, sems)
+    start_all(copies)
+    set_rows(0, x_ref, own, came)
+
+    @pl.loop(0, experts)
     def _(e):
-        gate_part, up_part = times(x_ref, hg, e), times(x_ref, hu, e)
-        gate[e] = gate_part if first else gate_part + total[0][e]
-        up[e] = up_part if first else up_part + total[1][e]
-
-    for pair in copies:
-        for copy in pair:
-            copy.wait()
-
-
-def in_vmem(x):
-    return pltpu.with_memory_space_constraint(x, pltpu.VMEM)
-
-
-def stage(b, own, came, held, total, w_gate, w_up):
+        gate[e] = times(x_ref, hg, e)
+        up[e] = times(x_ref, hu, e)
+
+    set_slots(pieces, slots_ref, experts, own.shape[0], TOP)
+    wait_all(copies)
+
+
+def second_kernel(own, came, hg, hu, mg, mu, g_hbm, u_hbm, gate_in, up_in, *refs):
+    gate, up, g_to, u_to, x_ref, sems = refs
+    copies = part_copies(2, 0, g_hbm, u_hbm, g_to, u_to, sems)
+    start_all(copies)
+    set_rows(1, x_ref, own, came)
+    done = 0
+    for g_from, u_from in ((hg, hu), (mg, mu)):
+
+        @pl.loop(0, g_from.shape[0])
+        def _(e):
+            at = done + e
+            gate[at] = gate_in[at] + times(x_ref, g_from, e)
+            up[at] = up_in[at] + times(x_ref, u_from, e)
+
+        done += g_from.shape[0]
+    wait_all(copies)
+
+
+def stages(own, x0, x1, held, pieces, w_gate, w_up):
     experts, depth, wide = w_gate.shape
-    rows = own.shape[0] + came.shape[0]
-    sums = jax.ShapeDtypeStruct((experts, rows, wide), jnp.float32)
-    *total, g_next, u_next = pl.pallas_call(
-        functools.partial(stage_kernel, b, not total),
-        in_specs=[VM] * 4 + [HBM] * 2 + [VM] * len(total),
+    rows = own.shape[0] + x0.shape[0]
+    part = depth // 4
+    later = experts - EARLY
+    sums = [jax.ShapeDtypeStruct((experts, rows, wide), jnp.float32)] * 2
+    weights = [pltpu.VMEM((later, part, wide), jnp.bfloat16)] * 2
+    scratch = [pltpu.VMEM((rows, part), jnp.bfloat16), pltpu.SemaphoreType.DMA((2, later))]
+    cost = pl.CostEstimate(
+        flops=rows * depth * wide * experts,
+        bytes_accessed=later * depth * wide,
+        transcendentals=0,
+    )
+    held = [in_vmem(x) for x in held]
+    gate, up, mid_gate, mid_up, slots = pl.pallas_call(
+        first_kernel,
+        in_specs=[VM] * 6 + [HBM] * 2 + [VM] * len(pieces),
+        out_specs=[VM] * 5,
+        out_shape=sums
+        + weights
+        + [jax.ShapeDtypeStruct((experts * rows // 2, rows), jnp.bfloat16)],
+        scratch_shapes=scratch,
+        cost_estimate=cost,
+        compiler_params=pltpu.CompilerParams(vmem_limit_bytes=SCOPE),
+        name="first",
+    )(own, x0, *held, w_gate, w_up, *pieces)
+    gate, up, *weights = pl.pallas_call(
+        second_kernel,
+        in_specs=[VM] * 6 + [HBM] * 2 + [VM] * 2,
         out_specs=[VM] * 4,
-        out_shape=[sums] * 2 + [pltpu.VMEM((experts, depth // 4, wide), jnp.bfloat16)] * 2,
-        scratch_shapes=[
-            pltpu.VMEM((rows, depth // 4), jnp.bfloat16),
-            pltpu.SemaphoreType.DMA((2, experts)),
-        ],
-        cost_estimate=pl.CostEstimate(
-            flops=rows * depth * wide * experts,
-            bytes_accessed=experts * depth * wide,
-            transcendentals=0,
-        ),
-        compiler_params=pltpu.CompilerParams(vmem_limit_bytes=SCOPE + b * HELD),
-        name="stage",
-    )(own, came, *map(in_vmem, held), w_gate, w_up, *total)
-    return total, (g_next, u_next)
-
-
-def last_kernel(n_ep, own, came, came_too, hg, hu, g_hbm, u_hbm, gate, up, *refs):
-    outs, (gb, ub, x_ref, y_ref, sems) = refs[:-5], refs[-5:]
-    experts, part = hg.shape[0], own.shape[0]
-    copies = part_copies(3, g_hbm, u_hbm, gb, ub, sems)
-    for pair in copies:
-        for copy in pair:
-            copy.start()
+        out_shape=sums + weights,
+        scratch_shapes=scratch,
+        cost_estimate=cost,
+        compiler_params=pltpu.CompilerParams(vmem_limit_bytes=SCOPE + HELD),
+        name="second",
+    )(own, x1, *held[2:], in_vmem(mid_gate), in_vmem(mid_up), w_gate, w_up, gate, up)
+    return gate, up, weights, slots
+
+
+def last_kernel(n_ep, own, came, came_too, hg, hu, g_hbm, u_hbm, gate, up, slots_ref, *refs):
+    outs, (tg, tu, gb, ub, x_ref, y_ref, few_sems, sems) = refs[:-8], refs[-8:]
+    experts, held = gate.shape[0], hg.shape[0]
+    slots = outs[0].shape[1]
+    copies = part_copies(3, 0, g_hbm, u_hbm, gb, ub, sems)
+    few = part_copies(2, held, g_hbm, u_hbm, tg, tu, few_sems)
+    start_all(copies[:held])
+    for pairs in zip(few, copies[held:]):
+        start_all(pairs)
     set_rows(2, x_ref, own, came)
     set_rows(3, y_ref, own, came_too)
     for e in range(experts):
-        gate_part = gate[e] + times(x_ref, hg, e)
-        up_part = up[e] + times(x_ref, hu, e)
-        for copy in copies[e]:
-            copy.wait()
+        if e < held:
+            gate_part = gate[e] + times(x_ref, hg, e)
+            up_part = up[e] + times(x_ref, hu, e)
+        else:
+            wait_all(few[e - held : e - held + 1])
+            gate_part = gate[e] + times(x_ref, tg, e - held)
+            up_part = up[e] + times(x_ref, tu, e - held)
+        wait_all(copies[e : e + 1])
         gate_part += times(y_ref, gb, e)
         up_part += times(y_ref, ub, e)
         hidden = (gate_part * jax.nn.sigmoid(gate_part) * up_part).astype(jnp.bfloat16)
+        back = jnp.dot(
+            slots_ref[e * n_ep * slots : (e + 1) * n_ep * slots, :],
+            hidden,
+            preferred_element_type=jnp.float32,
+        ).astype(jnp.bfloat16)
         for d in range(n_ep):
-            outs[d][e] = hidden[d * part : (d + 1) * part]
-
-
-def last(n_ep, own, came, came_too, held, total, w_gate, w_up):
+            outs[d][e] = back[d * slots : (d + 1) * slots]
+
+
+def last(n_ep, own, came, came_too, held, gate, up, slots, w_gate, w_up):
     experts, depth, wide = w_gate.shape
-    rows = own.shape[0] + came.shape[0]
-    out = jax.ShapeDtypeStruct((experts, own.shape[0], wide), jnp.bfloat16)
+    rows, part = own.shape[0] + came.shape[0], depth // 4
+    rest = experts - held[0].shape[0]
+    out = jax.ShapeDtypeStruct((experts, own.shape[0] // 2, wide), jnp.bfloat16)
     return pl.pallas_call(
         functools.partial(last_kernel, n_ep),
-        in_specs=[VM] * 5 + [HBM] * 2 + [VM] * 2,
+        in_specs=[VM] * 5 + [HBM] * 2 + [VM] * 3,
         out_specs=[VM] * n_ep,
         out_shape=[out] * n_ep,
-        scratch_shapes=[
-            pltpu.VMEM((experts, depth // 4, wide), jnp.bfloat16),
-            pltpu.VMEM((experts, depth // 4, wide), jnp.bfloat16),
-            pltpu.VMEM((rows, depth // 4), jnp.bfloat16),
-            pltpu.VMEM((rows, depth // 4), jnp.bfloat16),
-            pltpu.SemaphoreType.DMA((2, experts)),
-        ],
+        scratch_shapes=[pltpu.VMEM((n, part, wide), jnp.bfloat16) for n in (rest, rest, experts, experts)]
+        + [pltpu.VMEM((rows, part), jnp.bfloat16)] * 2
+        + [pltpu.SemaphoreType.DMA((2, rest)), pltpu.SemaphoreType.DMA((2, experts))],
         cost_estimate=pl.CostEstimate(
             flops=2 * rows * depth * wide * experts,
-            bytes_accessed=experts * depth * wide,
+            bytes_accessed=(experts + rest) * depth * wide,
             transcendentals=experts * rows * wide,
         ),
         compiler_params=pltpu.CompilerParams(vmem_limit_bytes=SCOPE + 2 * HELD),
         name="last",
-    )(own, came, came_too, *map(in_vmem, held), w_gate, w_up, *total)
+    )(own, came, came_too, *[in_vmem(x) for x in held], w_gate, w_up, gate, up, slots)
 
 
 def pick_kernel(select_ref, column_ref, *refs):
@@ -363,20 +504,21 @@
     per = cache_codes.shape[1]
     half = tokens.shape[1] // 8
     rows = tokens.shape[0]
-    *sent, own_piece = pack(cache_codes, cache_scales, tokens, n_ep)
-    came = [crossed(x, "ep", d) for d, x in enumerate(sent, 1)]
-    w_gate, w_up = [pltpu.with_memory_space_constraint(w, pltpu.HBM) for w in (w_gate, w_up)]
+    *sent, own_piece = pack(cache_codes, cache_scales, tokens, expert_ids, n_ep)
+    came = [crossed(x, "ep", d) for d, x in zip(ORDER, sent)]
+    w_gate, w_up = in_hbm(w_gate), in_hbm(w_up)
     *held, select, column = hold(expert_ids, routing_weights, w_gate, w_up, n_ep)
     came, held, select, column = lax.optimization_barrier((came, held, select, column))
+    came = [came[ORDER.index(d)] for d in range(1, n_ep)]
     x0 = merge(came, rows, half)
     x1 = crossed(x0, "pf", 1)
     x2 = crossed(x0, "pf", 2)
     x3 = crossed(x0, "pf", 3)
-    total, held = stage(0, tokens, x0, held, (), w_gate, w_up)
-    total, held = stage(1, tokens, x1, held, total, w_gate, w_up)
-    blocks = last(n_ep, tokens, x2, x3, held, total, w_gate, w_up)
-    back = [blocks[0]] + [crossed(blocks[d], "ep", d) for d in range(1, n_ep)]
-    attention_out = attend(queries, new_latent, prompt_lengths, per, [own_piece] + came)
+    pieces = [own_piece] + came
+    gate, up, held, slots = stages(tokens, x0, x1, held, pieces, w_gate, w_up)
+    blocks = last(n_ep, tokens, x2, x3, held, gate, up, slots, w_gate, w_up)
+    back = [blocks[0]] + [crossed(blocks[d], "ep", d) for d in ORDER]
+    attention_out = attend(queries, new_latent, prompt_lengths, per, pieces)
     moe_hidden = pick(select, column, back)
     return attention_out, moe_hidden.reshape(rows, -1, moe_hidden.shape[1])
 

time: 47.6 us -> 43.5 us (0.914)
  local copies, waits for them, and re-layouts: 3.95 us -> 0.02 us
  Pallas kernels: 26.9 us -> 28.2 us
  waiting for transfers between devices: 3.57 us -> 2.41 us
    unnamed x18 -> x8, local copies, waits for them, and re-layouts: 3.95 us -> 0.02 us
    pallas_call x1, Pallas kernels: 6.79 us -> 8.09 us  [last(): pl.pallas_call(functools.partial(last_kernel, n_ep), in_specs=[VM] * 5 +...]
    ppermute x9, waiting for transfers between devices: 3.57 us -> 2.41 us  [crossed(): return lax.ppermute(x, axis, [(s, s ^ bit) for s in range(n)])]
  transfers between devices with their start and end apart: 9 -> 9, of which waited for: 2 -> 2; matrix products, arithmetic and copies ran while one was open for 0% -> 0% of each run, Pallas kernels for 40% -> 42%
where the time goes in v4:
time: 43.5 us; the launch traced here: 43.3 us
  Pallas kernels  28.2 us (65%)
  starting transfers between devices  12 us (28%)
  waiting for transfers between devices  2.41 us (6%)
  between operations  0.75 us (2%)
    ppermute x9, starting transfers between devices, crossed(): return lax.ppermute(x, axis, [(s, s ^ bit) for s in range(n)])  12 us
    pallas_call x1, Pallas kernels, last(): pl.pallas_call(functools.partial(last_kernel, n_ep), in_specs=[VM] * 5 +...  8.09 us
    pallas_call x1, Pallas kernels, hold(): pl.pallas_call(hold_kernel, in_specs=[HBM] * 4, out_specs=[VM] * 6, out_s...  6.46 us
    pallas_call x1, Pallas kernels, stages(): pl.pallas_call(second_kernel, in_specs=[VM] * 6 + [HBM] * 2 + [VM] * 2, o...  4.26 us
    pallas_call x1, Pallas kernels, stages(): pl.pallas_call(first_kernel, in_specs=[VM] * 6 + [HBM] * 2 + [VM] * len(p...  4.26 us
    pallas_call x1, Pallas kernels, attend(): pl.pallas_call(functools.partial(attend_kernel, per), in_specs=[VM, VM, S...  2.99 us
    ppermute x9, waiting for transfers between devices, crossed(): return lax.ppermute(x, axis, [(s, s ^ bit) for s in range(n)])  2.41 us
    pallas_call x1, Pallas kernels, pack(): pl.pallas_call(pack_kernel, in_specs=[HBM] * 4, out_specs=[VM] * n_ep, ou...  1.18 us
  transfers between devices with their start and end apart: 9, of which 2 were waited for; matrix products, arithmetic and copies ran while one was open for 0% of the time, Pallas kernels for 42%

profile of v4, /device:TPU:0, one launch (start us, length us, event | category | flops | bytes accessed | tf_op | source)
XLA Modules:
  0.0 43.3 jit_solution(15739335019918903740)
XLA Ops:
  0.6 1.2 %pack.1 = (bf16[32,1536]{1,0:T(8,128)(2,1)S(1)}, bf16[32,1536]{1,0:T(8,128)(2,1)S(1)}, bf16[32,1536]{1,0:T(8,128)(2,1)S(1)}, bf16[32,640]{1,0:T(8,128)(2,1)S(1)}) custom-call(bf16[16,8,576]{2,1,0:T(8,128)(2,1)} %codes_hbm.1, bf16[5,8,16]{2,1,0:T(8,128)(2,1)} %bitcast.9, bf16[16,7168]{1,0:T(8,128)(2,1)} %own.5, s32[8,16]{1,0:T(8,128)} %bitcast.7), custom_call_target="tpu_custom_call" | custom-call | tf_op jit(solution)/shard_map/pack/pallas_call | solution.py:157
  1.8 4.1 %collective-permute-start = (bf16[32,1536]{1,0:T(8,128)(2,1)S(1)}, bf16[32,1536]{1,0:T(8,128)(2,1)S(1)}, u32[]{:S(2)}, u32[]{:S(2)}) collective-permute-start(bf16[32,1536]{1,0:T(8,128)(2,1)S(1)} %get-tuple-element.35), channel_id=1, source_target_pairs={{0,8},{4,12},{8,0},{12,4},{1,9},{5,13},{9,1},{13,5},{2,10},{6,14},... | collective-permute-start | bytes 294920 | tf_op jit(solution)/shard_map/ppermute | solution.py:488
  5.9 1.3 %collective-permute-start.1 = (bf16[32,1536]{1,0:T(8,128)(2,1)S(1)}, bf16[32,1536]{1,0:T(8,128)(2,1)S(1)}, u32[]{:S(2)}, u32[]{:S(2)}) collective-permute-start(bf16[32,1536]{1,0:T(8,128)(2,1)S(1)} %get-tuple-element.36), channel_id=1, source_target_pairs={{0,12},{4,8},{8,4},{12,0},{1,13},{5,9},{9,5},{13,1},{2,14},{6,10},... | collective-permute-start | bytes 294920 | tf_op jit(solution)/shard_map/ppermute | solution.py:488
  7.3 0.2 collective-permute-start.2
  7.5 0.0 copy-start
  7.5 6.5 %hold.1 = (bf16[8,1792,256]{2,1,0:T(8,128)(2,1)S(1)}, bf16[8,1792,256]{2,1,0:T(8,128)(2,1)S(1)}, bf16[2,1792,256]{2,1,0:T(8,128)(2,1)S(1)}, bf16[2,1792,256]{2,1...) custom-call(s32[8,16]{1,0:T(8,128)} %bitcast.8, f32[8,16]{1,0:T(8,128)} %bitcast.10, ...), custom_call_target="tpu_custom_call" | custom-call | bytes 18350080 | tf_op jit(solution)/shard_map/hold/pallas_call | solution.py:267
  14.0 0.0 collective-permute-done.refs_2_.refs_1_
  14.0 0.0 collective-permute-done.1.refs_3_.refs_2_
  14.0 0.3 collective-permute-done.2.refs_1_.refs_0_
  14.3 0.1 collective-permute-start.5
  14.4 1.7 %collective-permute-start.4 = (bf16[48,1792]{1,0:T(8,128)(2,1)S(1)}, bf16[48,1792]{1,0:T(8,128)(2,1)S(1)}, u32[]{:S(2)}, u32[]{:S(2)}) collective-permute-start(bf16[48,1792]{1,0:T(8,128)(2,1)S(1)} %merge.1.came), channel_id=1, source_target_pairs={{0,3},{1,2},{2,1},{3,0},{4,7},{5,6},{6,5},{7,4},{8,11},{9,10},{10,... | collective-permute-start | bytes 516104 | tf_op jit(solution)/shard_map/ppermute | solution.py:488
  16.1 0.5 %collective-permute-start.3 = (bf16[48,1792]{1,0:T(8,128)(2,1)S(1)}, bf16[48,1792]{1,0:T(8,128)(2,1)S(1)}, u32[]{:S(2)}, u32[]{:S(2)}) collective-permute-start(bf16[48,1792]{1,0:T(8,128)(2,1)S(1)} %merge.1.came), channel_id=1, source_target_pairs={{0,2},{1,3},{2,0},{3,1},{4,6},{5,7},{6,4},{7,5},{8,10},{9,11},{10,... | collective-permute-start | bytes 516104 | tf_op jit(solution)/shard_map/ppermute | solution.py:488
  16.6 0.0 copy-done
  16.6 4.3 %first.1 = (f32[8,64,256]{2,1,0:T(8,128)S(1)}, f32[8,64,256]{2,1,0:T(8,128)S(1)}, bf16[6,1792,256]{2,1,0:T(8,128)(2,1)S(1)}, bf16[6,1792,256]{2,1,0:T(8,128)(2,1)S(1)}, bf16[256,64]{1,0:T(8,128)(2,1)S(1)}) custom-call(bf16[16,7168]{1,0:T(8,128)(2,1)S(1)} %copy-done, bf16[48,1792]{1,0:T(8,128)(2,1)S(1)} %merge.1.came, ...), custom_call_target="tpu_custom_call" | custom-call | flops 939524096 | bytes 11010048 | tf_op jit(solution)/shard_map/first/pallas_call | solution.py:381
  20.8 0.0 collective-permute-done.5.came
  20.8 4.3 %second.1 = (f32[8,64,256]{2,1,0:T(8,128)S(1)}, f32[8,64,256]{2,1,0:T(8,128)S(1)}, bf16[6,1792,256]{2,1,0:T(8,128)(2,1)S(1)}, bf16[6,1792,256]{2,1,0:T(8,128)(2,1)S(1)}) custom-call(bf16[16,7168]{1,0:T(8,128)(2,1)S(1)} %copy-done, bf16[48,1792]{1,0:T(8,128)(2,1)S(1)} %collective-permute-done.5.came, ...), custom_call_target="tpu_custom_call" | custom-call | flops 939524096 | bytes 11010048 | tf_op jit(solution)/shard_map/second/pallas_call | solution.py:393
  25.1 0.0 collective-permute-done.4.came_too
  25.1 0.0 collective-permute-done.3.came
  25.1 0.0 copy-start.1
  25.1 0.0 copy-start.2
  25.2 0.0 copy-start.3
  25.2 8.1 %last.1 = (bf16[8,8,256]{2,1,0:T(8,128)(2,1)S(1)}, bf16[8,8,256]{2,1,0:T(8,128)(2,1)S(1)}, bf16[8,8,256]{2,1,0:T(8,128)(2,1)S(1)}, bf16[8,8,256]{2,1,0:T(8,128)(2,1)S(1)}) custom-call(bf16[16,7168]{1,0:T(8,128)(2,1)S(1)} %copy-done, bf16[48,1792]{1,0:T(8,128)(2,1)S(1)} %collective-permute-done.3.came, bf16[48,1792]{1,0:T(8,128)(2,1)S(1)} %collective-permute-done.4.came_too, ...), custom_call_target="tpu_custom_call" | custom-call | flops 1879048192 | bytes 18350080 | tf_op jit(solution)/shard_map/last/pallas_call | solution.py:443
  33.3 3.5 %collective-permute-start.6 = (bf16[8,8,256]{2,1,0:T(8,128)(2,1)S(1)}, bf16[8,8,256]{2,1,0:T(8,128)(2,1)S(1)}, u32[]{:S(2)}, u32[]{:S(2)}) collective-permute-start(bf16[8,8,256]{2,1,0:T(8,128)(2,1)S(1)} %get-tuple-element.63), channel_id=1, source_target_pairs={{0,8},{4,12},{8,0},{12,4},{1,9},{5,13},{9,1},{13,5},{2,10},{6,14},... | collective-permute-start | bytes 98312 | tf_op jit(solution)/shard_map/ppermute | solution.py:488
  36.7 0.4 %collective-permute-start.7 = (bf16[8,8,256]{2,1,0:T(8,128)(2,1)S(1)}, bf16[8,8,256]{2,1,0:T(8,128)(2,1)S(1)}, u32[]{:S(2)}, u32[]{:S(2)}) collective-permute-start(bf16[8,8,256]{2,1,0:T(8,128)(2,1)S(1)} %get-tuple-element.64), channel_id=1, source_target_pairs={{0,12},{4,8},{8,4},{12,0},{1,13},{5,9},{9,5},{13,1},{2,14},{6,10},... | collective-permute-start | bytes 98312 | tf_op jit(solution)/shard_map/ppermute | solution.py:488
  37.2 0.2 collective-permute-start.8
  37.4 0.0 copy-done.1
  37.4 0.0 copy-done.2
  37.4 0.0 copy-done.3
  37.4 3.0 %attend.1 = bf16[4,128,512]{2,1,0:T(8,128)(2,1)} custom-call(bf16[4,576,128]{2,1,0:T(8,128)(2,1)S(1)} %bitcast.5, bf16[4,576]{1,0:T(4,128)(2,1)S(1)} %copy-done.2, s32[4]{0:T(128)S(1)} %copy-done.3, bf16[32,640]{1,0:T(8,128)(2,1)S(1)} %get-tuple-element.34.refs_0_, bf16[32,1536]{1,0:T(8,128)(2,1)S(1)} %collective-permute-done.2.refs_1_.refs_0_, ...), custom_call_target="tpu_custom_call" | custom-call | flops 301989888 | bytes 1114112 | tf_op jit(solution)/shard_map/attend/pallas_call | solution.py:73
  40.4 0.0 collective-permute-done.6.refs_1_
  40.4 2.1 %collective-permute-done.7.refs_2_ = bf16[8,8,256]{2,1,0:T(8,128)(2,1)S(1)} collective-permute-done((bf16[8,8,256]{2,1,0:T(8,128)(2,1)S(1)}, bf16[8,8,256]{2,1,0:T(8,128)(2,1)S(1)}, u32[]{:S(2)}, u32[]{:S(2)}) %collective-permute-start.7) | collective-permute-done | bytes 32800 | tf_op jit(solution)/shard_map/ppermute | solution.py:488
  42.4 0.0 collective-permute-done.8.refs_3_
  42.4 0.9 %pick.1 = bf16[128,256]{1,0:T(8,128)(2,1)} custom-call(bf16[128,256]{1,0:T(8,128)(2,1)S(1)} %get-tuple-element.47.select_ref, f32[128,1]{1,0:T(8,128)S(1)} %get-tuple-element.48.column_ref, bf16[8,8,256]{2,1,0:T(8,128)(2,1)S(1)} %get-tuple-element.62.refs_0_, bf16[8,8,256]{2,1,0:T(8,128)(2,1)S(1)} %collective-permute-done.6.refs_1_, ...), custom_call_target="tpu_custom_call" | custom-call | tf_op jit(solution)/shard_map/pick/pallas_call | solution.py:476
  (1 shorter events, 0.0 us)
Async XLA Ops:
  1.8 12.2 %collective-permute-start = (bf16[32,1536]{1,0:T(8,128)(2,1)S(1)}, bf16[32,1536]{1,0:T(8,128)(2,1)S(1)}, u32[]{:S(2)}, u32[]{:S(2)}) collective-permute-start(bf16[32,1536]{1,0:T(8,128)(2,1)S(1)} %get-tuple-element.35), channel_id=1, source_target_pairs={{0,8},{4,12},{8,0},{12,4},{1,9},{5,13},{9,1},{13,5},{2,10},{6,14},... | collective-permute-start | bytes 294920 | tf_op jit(solution)/shard_map/ppermute | solution.py:488
  5.9 8.1 %collective-permute-start.1 = (bf16[32,1536]{1,0:T(8,128)(2,1)S(1)}, bf16[32,1536]{1,0:T(8,128)(2,1)S(1)}, u32[]{:S(2)}, u32[]{:S(2)}) collective-permute-start(bf16[32,1536]{1,0:T(8,128)(2,1)S(1)} %get-tuple-element.36), channel_id=1, source_target_pairs={{0,12},{4,8},{8,4},{12,0},{1,13},{5,9},{9,5},{13,1},{2,14},{6,10},... | collective-permute-start | bytes 294920 | tf_op jit(solution)/shard_map/ppermute | solution.py:488
  7.3 7.1 %collective-permute-start.2 = (bf16[32,1536]{1,0:T(8,128)(2,1)S(1)}, bf16[32,1536]{1,0:T(8,128)(2,1)S(1)}, u32[]{:S(2)}, u32[]{:S(2)}) collective-permute-start(bf16[32,1536]{1,0:T(8,128)(2,1)S(1)} %get-tuple-element.37), channel_id=1, source_target_pairs={{0,4},{4,0},{8,12},{12,8},{1,5},{5,1},{9,13},{13,9},{2,6},{6,2},{1... | collective-permute-start | bytes 294920 | tf_op jit(solution)/shard_map/ppermute | solution.py:488
  7.5 9.1 %copy-start = (bf16[16,7168]{1,0:T(8,128)(2,1)S(1)}, bf16[16,7168]{1,0:T(8,128)(2,1)}, u32[]{:S(2)}) copy-start(bf16[16,7168]{1,0:T(8,128)(2,1)} %own.5) | copy-start | bytes 688132
  14.3 6.5 %collective-permute-start.5 = (bf16[48,1792]{1,0:T(8,128)(2,1)S(1)}, bf16[48,1792]{1,0:T(8,128)(2,1)S(1)}, u32[]{:S(2)}, u32[]{:S(2)}) collective-permute-start(bf16[48,1792]{1,0:T(8,128)(2,1)S(1)} %merge.1.came), channel_id=1, source_target_pairs={{0,1},{1,0},{2,3},{3,2},{4,5},{5,4},{6,7},{7,6},{8,9},{9,8},{10,11... | collective-permute-start | bytes 516104 | tf_op jit(solution)/shard_map/ppermute | solution.py:488
  14.4 10.7 %collective-permute-start.4 = (bf16[48,1792]{1,0:T(8,128)(2,1)S(1)}, bf16[48,1792]{1,0:T(8,128)(2,1)S(1)}, u32[]{:S(2)}, u32[]{:S(2)}) collective-permute-start(bf16[48,1792]{1,0:T(8,128)(2,1)S(1)} %merge.1.came), channel_id=1, source_target_pairs={{0,3},{1,2},{2,1},{3,0},{4,7},{5,6},{6,5},{7,4},{8,11},{9,10},{10,... | collective-permute-start | bytes 516104 | tf_op jit(solution)/shard_map/ppermute | solution.py:488
  16.1 9.0 %collective-permute-start.3 = (bf16[48,1792]{1,0:T(8,128)(2,1)S(1)}, bf16[48,1792]{1,0:T(8,128)(2,1)S(1)}, u32[]{:S(2)}, u32[]{:S(2)}) collective-permute-start(bf16[48,1792]{1,0:T(8,128)(2,1)S(1)} %merge.1.came), channel_id=1, source_target_pairs={{0,2},{1,3},{2,0},{3,1},{4,6},{5,7},{6,4},{7,5},{8,10},{9,11},{10,... | collective-permute-start | bytes 516104 | tf_op jit(solution)/shard_map/ppermute | solution.py:488
  25.1 12.2 %copy-start.1 = (bf16[4,128,576]{1,2,0:T(8,128)(2,1)S(1)}, bf16[4,128,576]{1,2,0:T(8,128)(2,1)}, u32[]{:S(2)}) copy-start(bf16[4,128,576]{1,2,0:T(8,128)(2,1)} %param.12) | copy-start | bytes 1769476
  25.1 12.2 %copy-start.2 = (bf16[4,576]{1,0:T(4,128)(2,1)S(1)}, bf16[4,576]{1,0:T(4,128)(2,1)}, u32[]{:S(2)}) copy-start(bf16[4,576]{1,0:T(4,128)(2,1)} %new_ref.1) | copy-start | bytes 13828
  25.2 12.2 %copy-start.3 = (s32[4]{0:T(128)S(1)}, s32[4]{0:T(128)}, u32[]{:S(2)}) copy-start(s32[4]{0:T(128)} %len_ref.1) | copy-start | bytes 52
  33.3 7.1 %collective-permute-start.6 = (bf16[8,8,256]{2,1,0:T(8,128)(2,1)S(1)}, bf16[8,8,256]{2,1,0:T(8,128)(2,1)S(1)}, u32[]{:S(2)}, u32[]{:S(2)}) collective-permute-start(bf16[8,8,256]{2,1,0:T(8,128)(2,1)S(1)} %get-tuple-element.63), channel_id=1, source_target_pairs={{0,8},{4,12},{8,0},{12,4},{1,9},{5,13},{9,1},{13,5},{2,10},{6,14},... | collective-permute-start | bytes 98312 | tf_op jit(solution)/shard_map/ppermute | solution.py:488
  36.7 5.7 %collective-permute-start.7 = (bf16[8,8,256]{2,1,0:T(8,128)(2,1)S(1)}, bf16[8,8,256]{2,1,0:T(8,128)(2,1)S(1)}, u32[]{:S(2)}, u32[]{:S(2)}) collective-permute-start(bf16[8,8,256]{2,1,0:T(8,128)(2,1)S(1)} %get-tuple-element.64), channel_id=1, source_target_pairs={{0,12},{4,8},{8,4},{12,0},{1,13},{5,9},{9,5},{13,1},{2,14},{6,10},... | collective-permute-start | bytes 98312 | tf_op jit(solution)/shard_map/ppermute | solution.py:488
  37.2 5.3 %collective-permute-start.8 = (bf16[8,8,256]{2,1,0:T(8,128)(2,1)S(1)}, bf16[8,8,256]{2,1,0:T(8,128)(2,1)S(1)}, u32[]{:S(2)}, u32[]{:S(2)}) collective-permute-start(bf16[8,8,256]{2,1,0:T(8,128)(2,1)S(1)} %get-tuple-element.65), channel_id=1, source_target_pairs={{0,4},{4,0},{8,12},{12,8},{1,5},{5,1},{9,13},{13,9},{2,6},{6,2},{1... | collective-permute-start | bytes 98312 | tf_op jit(solution)/shard_map/ppermute | solution.py:488

commit v5 on v4

--- a/solution.py
+++ b/solution.py
@@ -12,9 +12,11 @@
 GROUP = 128
 TOP = 8
 EARLY = 2
+AHEAD = 6
 CHANNELS = 640
 SCOPE = 4 << 20
-ORDER = (2, 3, 1)
+GRANT = 16 << 20
+ORDER = (3, 2, 1)
 HELD = 14 << 20
 
 qk_scale = 192.0 ** (-0.5)
@@ -196,43 +198,46 @@
 
 def part_copies(b, first, g_ref, u_ref, g_to, u_to, sems):
     depth = g_to.shape[1]
-    start = pl.multiple_of((lax.axis_index("pf") ^ b) * depth, 128)
-    rows = pl.ds(start, depth)
-    return [
-        (
+    rows = pl.ds(pl.multiple_of((lax.axis_index("pf") ^ b) * depth, 128), depth)
+
+    def pair(e):
+        return (
             pltpu.make_async_copy(g_ref.at[first + e, rows], g_to.at[e], sems.at[0, e]),
             pltpu.make_async_copy(u_ref.at[first + e, rows], u_to.at[e], sems.at[1, e]),
         )
-        for e in range(g_to.shape[0])
-    ]
-
-
-def start_all(pairs):
-    for pair in pairs:
-        for copy in pair:
+
+    def start(e):
+        for copy in pair(e):
             copy.start()
 
-
-def wait_all(pairs):
-    for pair in pairs:
-        for copy in pair:
+    def wait(e):
+        for copy in pair(e):
             copy.wait()
+
+    return start, wait
+
+
+def for_all(act, count):
+    @pl.loop(0, count)
+    def _(e):
+        act(e)
 
 
 def hold_kernel(ids_hbm, weight_hbm, g_ref, u_ref, *refs):
     own_gate, own_up, next_gate, next_up, select_ref, column_ref = refs[:6]
     ids_ref, weight_ref, few_sems, sems, next_sems = refs[6:]
     few = [
-        (
-            pltpu.make_async_copy(ids_hbm, ids_ref, few_sems.at[0]),
-            pltpu.make_async_copy(weight_hbm, weight_ref, few_sems.at[1]),
-        )
+        pltpu.make_async_copy(ids_hbm, ids_ref, few_sems.at[0]),
+        pltpu.make_async_copy(weight_hbm, weight_ref, few_sems.at[1]),
     ]
-    copies = part_copies(0, 0, g_ref, u_ref, own_gate, own_up, sems)
-    copies += part_copies(1, 0, g_ref, u_ref, next_gate, next_up, next_sems)
-    start_all(few)
-    start_all(copies)
-    wait_all(few)
+    for copy in few:
+        copy.start()
+    start, wait = part_copies(0, 0, g_ref, u_ref, own_gate, own_up, sems)
+    start_next, wait_next = part_copies(1, 0, g_ref, u_ref, next_gate, next_up, next_sems)
+    for_all(start, g_ref.shape[0])
+    for_all(start_next, EARLY)
+    for copy in few:
+        copy.wait()
     top, rows = ids_ref.shape
     experts = g_ref.shape[0]
     slots = rows // 2
@@ -257,7 +262,8 @@
         select_ref[:, i * experts * slots : (i + 1) * experts * slots] = jnp.where(
             match, 1.0, 0.0
         ).astype(jnp.bfloat16)
-    wait_all(copies)
+    for_all(wait, experts)
+    for_all(wait_next, EARLY)
 
 
 def hold(expert_ids, routing_weights, w_gate, w_up, n_ep):
@@ -283,7 +289,7 @@
         cost_estimate=pl.CostEstimate(
             flops=0, bytes_accessed=(experts + EARLY) * depth * wide, transcendentals=0
         ),
-        compiler_params=pltpu.CompilerParams(vmem_limit_bytes=SCOPE),
+        compiler_params=pltpu.CompilerParams(vmem_limit_bytes=GRANT),
         name="hold",
     )(in_hbm(expert_ids.T), in_hbm(routing_weights.T), w_gate, w_up)
 
@@ -292,11 +298,12 @@
     rows, quarter = own_ref.shape[0], came_ref.shape[1]
     start = pl.multiple_of((lax.axis_index("pf") ^ b) * quarter, 128)
     x_ref[:rows, :] = own_ref[:, pl.ds(start, quarter)]
-    x_ref[rows:, :] = came_ref[...]
+    x_ref[rows : rows + came_ref.shape[0], :] = came_ref[...]
 
 
 def times(x_ref, w_ref, e):
-    return jnp.dot(x_ref[...], w_ref[e], preferred_element_type=jnp.float32)
+    rows = x_ref.shape[0] // 2
+    return jnp.dot(x_ref[...], w_ref[e], preferred_element_type=jnp.float32)[:rows]
 
 
 def set_slots(pieces, slots_ref, experts, rows, top):
@@ -330,102 +337,105 @@
     slots_ref[...] = jnp.where((named > 0.5) & (rank == slot), 1.0, 0.0).astype(jnp.bfloat16)
 
 
-def first_kernel(own, came, hg, hu, next_gate, next_up, g_hbm, u_hbm, *refs):
-    pieces, (gate, up, g_to, u_to, slots_ref, x_ref, sems) = refs[:-7], refs[-7:]
-    experts = hg.shape[0]
-    copies = part_copies(1, EARLY, g_hbm, u_hbm, g_to, u_to, sems)
-    start_all(copies)
+def front_kernel(own, came, came_too, hg, hu, mg, mu, g_hbm, u_hbm, *refs):
+    pieces, (gate, up, g_to, u_to, slots_ref) = refs[:-11], refs[-11:-6]
+    tg, tu, x_ref, y_ref, few_sems, sems = refs[-6:]
+    experts, early = hg.shape[0], mg.shape[0]
+    start_few, wait_few = part_copies(1, early, g_hbm, u_hbm, tg, tu, few_sems)
+    start, wait = part_copies(2, 0, g_hbm, u_hbm, g_to, u_to, sems)
+    for_all(start_few, experts - early)
     set_rows(0, x_ref, own, came)
-
-    @pl.loop(0, experts)
-    def _(e):
+    set_rows(1, y_ref, own, came_too)
+
+    @pl.loop(0, experts, unroll=2)
+    def _(e):
+        @pl.when(e >= experts - AHEAD)
+        def _():
+            start(e - (experts - AHEAD))
+
         gate[e] = times(x_ref, hg, e)
         up[e] = times(x_ref, hu, e)
 
+    @pl.loop(0, early)
+    def _(e):
+        gate[e] += times(y_ref, mg, e)
+        up[e] += times(y_ref, mu, e)
+
     set_slots(pieces, slots_ref, experts, own.shape[0], TOP)
-    wait_all(copies)
-
-
-def second_kernel(own, came, hg, hu, mg, mu, g_hbm, u_hbm, gate_in, up_in, *refs):
-    gate, up, g_to, u_to, x_ref, sems = refs
-    copies = part_copies(2, 0, g_hbm, u_hbm, g_to, u_to, sems)
-    start_all(copies)
-    set_rows(1, x_ref, own, came)
-    done = 0
-    for g_from, u_from in ((hg, hu), (mg, mu)):
-
-        @pl.loop(0, g_from.shape[0])
-        def _(e):
-            at = done + e
-            gate[at] = gate_in[at] + times(x_ref, g_from, e)
-            up[at] = up_in[at] + times(x_ref, u_from, e)
-
-        done += g_from.shape[0]
-    wait_all(copies)
-
-
-def stages(own, x0, x1, held, pieces, w_gate, w_up):
+
+    @pl.loop(0, experts - early)
+    def _(e):
+        wait_few(e)
+        gate[early + e] += times(y_ref, tg, e)
+        up[early + e] += times(y_ref, tu, e)
+
+    for_all(wait, AHEAD)
+
+
+def front(own, x0, x1, held, pieces, w_gate, w_up):
     experts, depth, wide = w_gate.shape
     rows = own.shape[0] + x0.shape[0]
     part = depth // 4
-    later = experts - EARLY
+    rest = experts - EARLY
     sums = [jax.ShapeDtypeStruct((experts, rows, wide), jnp.float32)] * 2
-    weights = [pltpu.VMEM((later, part, wide), jnp.bfloat16)] * 2
-    scratch = [pltpu.VMEM((rows, part), jnp.bfloat16), pltpu.SemaphoreType.DMA((2, later))]
-    cost = pl.CostEstimate(
-        flops=rows * depth * wide * experts,
-        bytes_accessed=later * depth * wide,
-        transcendentals=0,
-    )
-    held = [in_vmem(x) for x in held]
-    gate, up, mid_gate, mid_up, slots = pl.pallas_call(
-        first_kernel,
-        in_specs=[VM] * 6 + [HBM] * 2 + [VM] * len(pieces),
+    *sums, gate, up, slots = pl.pallas_call(
+        front_kernel,
+        in_specs=[VM] * 7 + [HBM] * 2 + [VM] * len(pieces),
         out_specs=[VM] * 5,
         out_shape=sums
-        + weights
+        + [pltpu.VMEM((AHEAD, part, wide), jnp.bfloat16)] * 2
         + [jax.ShapeDtypeStruct((experts * rows // 2, rows), jnp.bfloat16)],
-        scratch_shapes=scratch,
-        cost_estimate=cost,
-        compiler_params=pltpu.CompilerParams(vmem_limit_bytes=SCOPE),
-        name="first",
-    )(own, x0, *held, w_gate, w_up, *pieces)
-    gate, up, *weights = pl.pallas_call(
-        second_kernel,
-        in_specs=[VM] * 6 + [HBM] * 2 + [VM] * 2,
-        out_specs=[VM] * 4,
-        out_shape=sums + weights,
-        scratch_shapes=scratch,
-        cost_estimate=cost,
-        compiler_params=pltpu.CompilerParams(vmem_limit_bytes=SCOPE + HELD),
-        name="second",
-    )(own, x1, *held[2:], in_vmem(mid_gate), in_vmem(mid_up), w_gate, w_up, gate, up)
-    return gate, up, weights, slots
+        scratch_shapes=[pltpu.VMEM((rest, part, wide), jnp.bfloat16)] * 2
+        + [pltpu.VMEM((2 * rows, part), jnp.bfloat16)] * 2
+        + [pltpu.SemaphoreType.DMA((2, rest)), pltpu.SemaphoreType.DMA((2, AHEAD))],
+        cost_estimate=pl.CostEstimate(
+            flops=2 * rows * depth * wide * experts,
+            bytes_accessed=(rest + AHEAD) * depth * wide,
+            transcendentals=0,
+        ),
+        compiler_params=pltpu.CompilerParams(vmem_limit_bytes=GRANT),
+        name="front",
+    )(own, x0, x1, *map(in_vmem, held), w_gate, w_up, *pieces)
+    return sums, (gate, up), slots
 
 
 def last_kernel(n_ep, own, came, came_too, hg, hu, g_hbm, u_hbm, gate, up, slots_ref, *refs):
-    outs, (tg, tu, gb, ub, x_ref, y_ref, few_sems, sems) = refs[:-8], refs[-8:]
+    outs, (gate_sum, up_sum, tg, tu, gb, ub, x_ref, y_ref, few_sems, sems) = refs[:-10], refs[-10:]
     experts, held = gate.shape[0], hg.shape[0]
     slots = outs[0].shape[1]
-    copies = part_copies(3, 0, g_hbm, u_hbm, gb, ub, sems)
-    few = part_copies(2, held, g_hbm, u_hbm, tg, tu, few_sems)
-    start_all(copies[:held])
-    for pairs in zip(few, copies[held:]):
-        start_all(pairs)
+    start_few, wait_few = part_copies(2, held, g_hbm, u_hbm, tg, tu, few_sems)
+    start, wait = part_copies(3, 0, g_hbm, u_hbm, gb, ub, sems)
+    for_all(start_few, experts - held)
+    start(0)
     set_rows(2, x_ref, own, came)
     set_rows(3, y_ref, own, came_too)
+
+    @pl.loop(0, held, unroll=2)
+    def _(e):
+        start(e + 1)
+        gate_sum[e] = gate[e] + times(x_ref, hg, e)
+        up_sum[e] = up[e] + times(x_ref, hu, e)
+
+    @pl.loop(0, experts - held)
+    def _(e):
+        wait_few(e)
+
+        @pl.when(held + e + 1 < experts)
+        def _():
+            start(held + e + 1)
+
+        gate_sum[held + e] = gate[held + e] + times(x_ref, tg, e)
+        up_sum[held + e] = up[held + e] + times(x_ref, tu, e)
+
+    @pl.loop(0, experts)
+    def _(e):
+        wait(e)
+        gate_sum[e] += times(y_ref, gb, e)
+        up_sum[e] += times(y_ref, ub, e)
+
     for e in range(experts):
-        if e < held:
-            gate_part = gate[e] + times(x_ref, hg, e)
-            up_part = up[e] + times(x_ref, hu, e)
-        else:
-            wait_all(few[e - held : e - held + 1])
-            gate_part = gate[e] + times(x_ref, tg, e - held)
-            up_part = up[e] + times(x_ref, tu, e - held)
-        wait_all(copies[e : e + 1])
-        gate_part += times(y_ref, gb, e)
-        up_part += times(y_ref, ub, e)
-        hidden = (gate_part * jax.nn.sigmoid(gate_part) * up_part).astype(jnp.bfloat16)
+        gate_part = gate_sum[e]
+        hidden = (gate_part * jax.nn.sigmoid(gate_part) * up_sum[e]).astype(jnp.bfloat16)
         back = jnp.dot(
             slots_ref[e * n_ep * slots : (e + 1) * n_ep * slots, :],
             hidden,
@@ -438,22 +448,25 @@
 def last(n_ep, own, came, came_too, held, gate, up, slots, w_gate, w_up):
     experts, depth, wide = w_gate.shape
     rows, part = own.shape[0] + came.shape[0], depth // 4
-    rest = experts - held[0].shape[0]
+    rest = experts - AHEAD
     out = jax.ShapeDtypeStruct((experts, own.shape[0] // 2, wide), jnp.bfloat16)
     return pl.pallas_call(
         functools.partial(last_kernel, n_ep),
         in_specs=[VM] * 5 + [HBM] * 2 + [VM] * 3,
         out_specs=[VM] * n_ep,
         out_shape=[out] * n_ep,
-        scratch_shapes=[pltpu.VMEM((n, part, wide), jnp.bfloat16) for n in (rest, rest, experts, experts)]
-        + [pltpu.VMEM((rows, part), jnp.bfloat16)] * 2
+        scratch_shapes=[pltpu.VMEM((experts, rows, wide), jnp.float32)] * 2
+        + [pltpu.VMEM((n, part, wide), jnp.bfloat16) for n in (rest, rest, experts, experts)]
+        + [pltpu.VMEM((2 * rows, part), jnp.bfloat16)] * 2
         + [pltpu.SemaphoreType.DMA((2, rest)), pltpu.SemaphoreType.DMA((2, experts))],
         cost_estimate=pl.CostEstimate(
             flops=2 * rows * depth * wide * experts,
             bytes_accessed=(experts + rest) * depth * wide,
             transcendentals=experts * rows * wide,
         ),
-        compiler_params=pltpu.CompilerParams(vmem_limit_bytes=SCOPE + 2 * HELD),
+        compiler_params=pltpu.CompilerParams(
+            vmem_limit_bytes=GRANT + (experts + EARLY) * 4 * part * wide
+        ),
         name="last",
     )(own, came, came_too, *[in_vmem(x) for x in held], w_gate, w_up, gate, up, slots)
 
@@ -515,8 +528,8 @@
     x2 = crossed(x0, "pf", 2)
     x3 = crossed(x0, "pf", 3)
     pieces = [own_piece] + came
-    gate, up, held, slots = stages(tokens, x0, x1, held, pieces, w_gate, w_up)
-    blocks = last(n_ep, tokens, x2, x3, held, gate, up, slots, w_gate, w_up)
+    sums, held, slots = front(tokens, x0, x1, held, pieces, w_gate, w_up)
+    blocks = last(n_ep, tokens, x2, x3, held, *sums, slots, w_gate, w_up)
     back = [blocks[0]] + [crossed(blocks[d], "ep", d) for d in ORDER]
     attention_out = attend(queries, new_latent, prompt_lengths, per, pieces)
     moe_hidden = pick(select, column, back)

time: 43.5 us -> 41.6 us (0.956)
  Pallas kernels: 28.2 us -> 26.6 us
  waiting for transfers between devices: 2.41 us -> 1.77 us
    pallas_call x2 -> x1, Pallas kernels: 8.52 us -> 7.7 us  [front(): pl.pallas_call(front_kernel, in_specs=[VM] * 7 + [HBM] * 2 + [VM] * len(p...]
    pallas_call x1, Pallas kernels: 8.09 us -> 7.29 us  [last(): pl.pallas_call(functools.partial(last_kernel, n_ep), in_specs=[VM] * 5 +...]
    ppermute x9, waiting for transfers between devices: 2.41 us -> 1.77 us  [crossed(): return lax.ppermute(x, axis, [(s, s ^ bit) for s in range(n)])]
  transfers between devices with their start and end apart: 9 -> 9, of which waited for: 2 -> 3; matrix products, arithmetic and copies ran while one was open for 0% -> 0% of each run, Pallas kernels for 42% -> 41%
where the time goes in v5:
time: 41.6 us; the launch traced here: 41.5 us
  Pallas kernels  26.6 us (64%)
  starting transfers between devices  12.4 us (30%)
  waiting for transfers between devices  1.77 us (4%)
  between operations  0.7 us (2%)
    ppermute x9, starting transfers between devices, crossed(): return lax.ppermute(x, axis, [(s, s ^ bit) for s in range(n)])  12.4 us
    pallas_call x1, Pallas kernels, front(): pl.pallas_call(front_kernel, in_specs=[VM] * 7 + [HBM] * 2 + [VM] * len(p...  7.7 us
    pallas_call x1, Pallas kernels, last(): pl.pallas_call(functools.partial(last_kernel, n_ep), in_specs=[VM] * 5 +...  7.29 us
    pallas_call x1, Pallas kernels, hold(): pl.pallas_call(hold_kernel, in_specs=[HBM] * 4, out_specs=[VM] * 6, out_s...  6.49 us
    pallas_call x1, Pallas kernels, attend(): pl.pallas_call(functools.partial(attend_kernel, per), in_specs=[VM, VM, S...  2.98 us
    ppermute x9, waiting for transfers between devices, crossed(): return lax.ppermute(x, axis, [(s, s ^ bit) for s in range(n)])  1.77 us
    pallas_call x1, Pallas kernels, pack(): pl.pallas_call(pack_kernel, in_specs=[HBM] * 4, out_specs=[VM] * n_ep, ou...  1.18 us
    pallas_call x1, Pallas kernels, pick(): pl.pallas_call(pick_kernel, in_specs=[VM] * (2 + len(blocks)), out_specs=...  0.9 us
  transfers between devices with their start and end apart: 9, of which 3 were waited for; matrix products, arithmetic and copies ran while one was open for 0% of the time, Pallas kernels for 41%

profile of v5, /device:TPU:0, one launch (start us, length us, event | category | flops | bytes accessed | tf_op | source)
XLA Modules:
  0.0 41.5 jit_solution(12707249502140628509)
XLA Ops:
  0.6 1.2 %pack.1 = (bf16[32,1536]{1,0:T(8,128)(2,1)S(1)}, bf16[32,1536]{1,0:T(8,128)(2,1)S(1)}, bf16[32,1536]{1,0:T(8,128)(2,1)S(1)}, bf16[32,640]{1,0:T(8,128)(2,1)S(1)}) custom-call(bf16[16,8,576]{2,1,0:T(8,128)(2,1)} %codes_hbm.1, bf16[5,8,16]{2,1,0:T(8,128)(2,1)} %bitcast.9, bf16[16,7168]{1,0:T(8,128)(2,1)} %own.3, s32[8,16]{1,0:T(8,128)} %bitcast.7), custom_call_target="tpu_custom_call" | custom-call | tf_op jit(solution)/shard_map/pack/pallas_call | solution.py:159
  1.8 5.1 %collective-permute-start = (bf16[32,1536]{1,0:T(8,128)(2,1)S(1)}, bf16[32,1536]{1,0:T(8,128)(2,1)S(1)}, u32[]{:S(2)}, u32[]{:S(2)}) collective-permute-start(bf16[32,1536]{1,0:T(8,128)(2,1)S(1)} %get-tuple-element.31), channel_id=1, source_target_pairs={{0,12},{4,8},{8,4},{12,0},{1,13},{5,9},{9,5},{13,1},{2,14},{6,10},... | collective-permute-start | bytes 294920 | tf_op jit(solution)/shard_map/ppermute | solution.py:501
  6.9 0.0 collective-permute-start.1
  6.9 0.6 %collective-permute-start.2 = (bf16[32,1536]{1,0:T(8,128)(2,1)S(1)}, bf16[32,1536]{1,0:T(8,128)(2,1)S(1)}, u32[]{:S(2)}, u32[]{:S(2)}) collective-permute-start(bf16[32,1536]{1,0:T(8,128)(2,1)S(1)} %get-tuple-element.33), channel_id=1, source_target_pairs={{0,4},{4,0},{8,12},{12,8},{1,5},{5,1},{9,13},{13,9},{2,6},{6,2},{1... | collective-permute-start | bytes 294920 | tf_op jit(solution)/shard_map/ppermute | solution.py:501
  7.6 0.0 copy-start
  7.6 6.5 %hold.1 = (bf16[8,1792,256]{2,1,0:T(8,128)(2,1)S(1)}, bf16[8,1792,256]{2,1,0:T(8,128)(2,1)S(1)}, bf16[2,1792,256]{2,1,0:T(8,128)(2,1)S(1)}, bf16[2,1792,256]{2,1...) custom-call(s32[8,16]{1,0:T(8,128)} %bitcast.8, f32[8,16]{1,0:T(8,128)} %bitcast.10, ...), custom_call_target="tpu_custom_call" | custom-call | bytes 18350080 | tf_op jit(solution)/shard_map/hold/pallas_call | solution.py:273
  14.1 0.0 collective-permute-done.refs_3_.refs_2_
  14.1 1.1 %collective-permute-done.1.refs_2_.refs_1_ = bf16[32,1536]{1,0:T(8,128)(2,1)S(1)} collective-permute-done((bf16[32,1536]{1,0:T(8,128)(2,1)S(1)}, bf16[32,1536]{1,0:T(8,128)(2,1)S(1)}, u32[]{:S(2)}, u32[]{:S(2)}) %collective-permute-start.1) | collective-permute-done | bytes 98336 | tf_op jit(solution)/shard_map/ppermute | solution.py:501
  15.2 0.0 collective-permute-done.2.refs_1_.refs_0_
  15.2 0.1 collective-permute-start.5
  15.3 1.6 %collective-permute-start.4 = (bf16[48,1792]{1,0:T(8,128)(2,1)S(1)}, bf16[48,1792]{1,0:T(8,128)(2,1)S(1)}, u32[]{:S(2)}, u32[]{:S(2)}) collective-permute-start(bf16[48,1792]{1,0:T(8,128)(2,1)S(1)} %merge.1.came), channel_id=1, source_target_pairs={{0,3},{1,2},{2,1},{3,0},{4,7},{5,6},{6,5},{7,4},{8,11},{9,10},{10,... | collective-permute-start | bytes 516104 | tf_op jit(solution)/shard_map/ppermute | solution.py:501
  16.9 0.5 %collective-permute-start.3 = (bf16[48,1792]{1,0:T(8,128)(2,1)S(1)}, bf16[48,1792]{1,0:T(8,128)(2,1)S(1)}, u32[]{:S(2)}, u32[]{:S(2)}) collective-permute-start(bf16[48,1792]{1,0:T(8,128)(2,1)S(1)} %merge.1.came), channel_id=1, source_target_pairs={{0,2},{1,3},{2,0},{3,1},{4,6},{5,7},{6,4},{7,5},{8,10},{9,11},{10,... | collective-permute-start | bytes 516104 | tf_op jit(solution)/shard_map/ppermute | solution.py:501
  17.4 0.0 collective-permute-done.5.came_too
  17.4 0.0 copy-done
  17.4 7.7 %front.1 = (f32[8,64,256]{2,1,0:T(8,128)S(1)}, f32[8,64,256]{2,1,0:T(8,128)S(1)}, bf16[6,1792,256]{2,1,0:T(8,128)(2,1)S(1)}, bf16[6,1792,256]{2,1,0:T(8,128)(2,1)S(1)}, bf16[256,64]{1,0:T(8,128)(2,1)S(1)}) custom-call(bf16[16,7168]{1,0:T(8,128)(2,1)S(1)} %copy-done, bf16[48,1792]{1,0:T(8,128)(2,1)S(1)} %merge.1.came, ...), custom_call_target="tpu_custom_call" | custom-call | flops 1879048192 | bytes 22020096 | tf_op jit(solution)/shard_map/front/pallas_call | solution.py:381
  25.1 0.0 collective-permute-done.4.came_too
  25.2 0.6 %collective-permute-done.3.came = bf16[48,1792]{1,0:T(8,128)(2,1)S(1)} collective-permute-done((bf16[48,1792]{1,0:T(8,128)(2,1)S(1)}, bf16[48,1792]{1,0:T(8,128)(2,1)S(1)}, u32[]{:S(2)}, u32[]{:S(2)}) %collective-permute-start.3) | collective-permute-done | bytes 172064 | tf_op jit(solution)/shard_map/ppermute | solution.py:501
  25.7 0.0 copy-start.1
  25.7 0.0 copy-start.2
  25.7 0.0 copy-start.3
  25.7 7.3 %last.1 = (bf16[8,8,256]{2,1,0:T(8,128)(2,1)S(1)}, bf16[8,8,256]{2,1,0:T(8,128)(2,1)S(1)}, bf16[8,8,256]{2,1,0:T(8,128)(2,1)S(1)}, bf16[8,8,256]{2,1,0:T(8,128)(2,1)S(1)}) custom-call(bf16[16,7168]{1,0:T(8,128)(2,1)S(1)} %copy-done, bf16[48,1792]{1,0:T(8,128)(2,1)S(1)} %collective-permute-done.3.came, bf16[48,1792]{1,0:T(8,128)(2,1)S(1)} %collective-permute-done.4.came_too, ...), custom_call_target="tpu_custom_call" | custom-call | flops 1879048192 | bytes 18350080 | tf_op jit(solution)/shard_map/last/pallas_call | solution.py:453
  33.0 2.7 %collective-permute-start.6 = (bf16[8,8,256]{2,1,0:T(8,128)(2,1)S(1)}, bf16[8,8,256]{2,1,0:T(8,128)(2,1)S(1)}, u32[]{:S(2)}, u32[]{:S(2)}) collective-permute-start(bf16[8,8,256]{2,1,0:T(8,128)(2,1)S(1)} %get-tuple-element.55), channel_id=1, source_target_pairs={{0,12},{4,8},{8,4},{12,0},{1,13},{5,9},{9,5},{13,1},{2,14},{6,10},... | collective-permute-start | bytes 98312 | tf_op jit(solution)/shard_map/ppermute | solution.py:501
  35.8 0.0 collective-permute-start.7
  35.8 1.7 %collective-permute-start.8 = (bf16[8,8,256]{2,1,0:T(8,128)(2,1)S(1)}, bf16[8,8,256]{2,1,0:T(8,128)(2,1)S(1)}, u32[]{:S(2)}, u32[]{:S(2)}) collective-permute-start(bf16[8,8,256]{2,1,0:T(8,128)(2,1)S(1)} %get-tuple-element.57), channel_id=1, source_target_pairs={{0,4},{4,0},{8,12},{12,8},{1,5},{5,1},{9,13},{13,9},{2,6},{6,2},{1... | collective-permute-start | bytes 98312 | tf_op jit(solution)/shard_map/ppermute | solution.py:501
  37.5 0.0 copy-done.1
  37.5 0.0 copy-done.2
  37.5 0.0 copy-done.3
  37.5 3.0 %attend.1 = bf16[4,128,512]{2,1,0:T(8,128)(2,1)} custom-call(bf16[4,576,128]{2,1,0:T(8,128)(2,1)S(1)} %bitcast.5, bf16[4,576]{1,0:T(4,128)(2,1)S(1)} %copy-done.2, s32[4]{0:T(128)S(1)} %copy-done.3, bf16[32,640]{1,0:T(8,128)(2,1)S(1)} %get-tuple-element.30.refs_0_, bf16[32,1536]{1,0:T(8,128)(2,1)S(1)} %collective-permute-done.2.refs_1_.refs_0_, ...), custom_call_target="tpu_custom_call" | custom-call | flops 301989888 | bytes 1114112 | tf_op jit(solution)/shard_map/attend/pallas_call | solution.py:75
  40.5 0.0 collective-permute-done.6.refs_1_
  40.5 0.1 collective-permute-done.7.refs_2_
  40.6 0.0 collective-permute-done.8.refs_3_
  40.6 0.9 %pick.1 = bf16[128,256]{1,0:T(8,128)(2,1)} custom-call(bf16[128,256]{1,0:T(8,128)(2,1)S(1)} %get-tuple-element.43.select_ref, f32[128,1]{1,0:T(8,128)S(1)} %get-tuple-element.44.column_ref, bf16[8,8,256]{2,1,0:T(8,128)(2,1)S(1)} %get-tuple-element.54.refs_0_, bf16[8,8,256]{2,1,0:T(8,128)(2,1)S(1)} %collective-permute-done.6.refs_1_, ...), custom_call_target="tpu_custom_call" | custom-call | tf_op jit(solution)/shard_map/pick/pallas_call | solution.py:489
  (1 shorter events, 0.0 us)
Async XLA Ops:
  1.8 12.3 %collective-permute-start = (bf16[32,1536]{1,0:T(8,128)(2,1)S(1)}, bf16[32,1536]{1,0:T(8,128)(2,1)S(1)}, u32[]{:S(2)}, u32[]{:S(2)}) collective-permute-start(bf16[32,1536]{1,0:T(8,128)(2,1)S(1)} %get-tuple-element.31), channel_id=1, source_target_pairs={{0,12},{4,8},{8,4},{12,0},{1,13},{5,9},{9,5},{13,1},{2,14},{6,10},... | collective-permute-start | bytes 294920 | tf_op jit(solution)/shard_map/ppermute | solution.py:501
  6.9 8.3 %collective-permute-start.1 = (bf16[32,1536]{1,0:T(8,128)(2,1)S(1)}, bf16[32,1536]{1,0:T(8,128)(2,1)S(1)}, u32[]{:S(2)}, u32[]{:S(2)}) collective-permute-start(bf16[32,1536]{1,0:T(8,128)(2,1)S(1)} %get-tuple-element.32), channel_id=1, source_target_pairs={{0,8},{4,12},{8,0},{12,4},{1,9},{5,13},{9,1},{13,5},{2,10},{6,14},... | collective-permute-start | bytes 294920 | tf_op jit(solution)/shard_map/ppermute | solution.py:501
  6.9 8.3 %collective-permute-start.2 = (bf16[32,1536]{1,0:T(8,128)(2,1)S(1)}, bf16[32,1536]{1,0:T(8,128)(2,1)S(1)}, u32[]{:S(2)}, u32[]{:S(2)}) collective-permute-start(bf16[32,1536]{1,0:T(8,128)(2,1)S(1)} %get-tuple-element.33), channel_id=1, source_target_pairs={{0,4},{4,0},{8,12},{12,8},{1,5},{5,1},{9,13},{13,9},{2,6},{6,2},{1... | collective-permute-start | bytes 294920 | tf_op jit(solution)/shard_map/ppermute | solution.py:501
  7.6 9.9 %copy-start = (bf16[16,7168]{1,0:T(8,128)(2,1)S(1)}, bf16[16,7168]{1,0:T(8,128)(2,1)}, u32[]{:S(2)}) copy-start(bf16[16,7168]{1,0:T(8,128)(2,1)} %own.3) | copy-start | bytes 688132
  15.2 2.2 %collective-permute-start.5 = (bf16[48,1792]{1,0:T(8,128)(2,1)S(1)}, bf16[48,1792]{1,0:T(8,128)(2,1)S(1)}, u32[]{:S(2)}, u32[]{:S(2)}) collective-permute-start(bf16[48,1792]{1,0:T(8,128)(2,1)S(1)} %merge.1.came), channel_id=1, source_target_pairs={{0,1},{1,0},{2,3},{3,2},{4,5},{5,4},{6,7},{7,6},{8,9},{9,8},{10,11... | collective-permute-start | bytes 516104 | tf_op jit(solution)/shard_map/ppermute | solution.py:501
  15.3 9.9 %collective-permute-start.4 = (bf16[48,1792]{1,0:T(8,128)(2,1)S(1)}, bf16[48,1792]{1,0:T(8,128)(2,1)S(1)}, u32[]{:S(2)}, u32[]{:S(2)}) collective-permute-start(bf16[48,1792]{1,0:T(8,128)(2,1)S(1)} %merge.1.came), channel_id=1, source_target_pairs={{0,3},{1,2},{2,1},{3,0},{4,7},{5,6},{6,5},{7,4},{8,11},{9,10},{10,... | collective-permute-start | bytes 516104 | tf_op jit(solution)/shard_map/ppermute | solution.py:501
  16.9 8.8 %collective-permute-start.3 = (bf16[48,1792]{1,0:T(8,128)(2,1)S(1)}, bf16[48,1792]{1,0:T(8,128)(2,1)S(1)}, u32[]{:S(2)}, u32[]{:S(2)}) collective-permute-start(bf16[48,1792]{1,0:T(8,128)(2,1)S(1)} %merge.1.came), channel_id=1, source_target_pairs={{0,2},{1,3},{2,0},{3,1},{4,6},{5,7},{6,4},{7,5},{8,10},{9,11},{10,... | collective-permute-start | bytes 516104 | tf_op jit(solution)/shard_map/ppermute | solution.py:501
  25.7 11.8 %copy-start.1 = (bf16[4,128,576]{1,2,0:T(8,128)(2,1)S(1)}, bf16[4,128,576]{1,2,0:T(8,128)(2,1)}, u32[]{:S(2)}) copy-start(bf16[4,128,576]{1,2,0:T(8,128)(2,1)} %param.12) | copy-start | bytes 1769476
  25.7 11.8 %copy-start.2 = (bf16[4,576]{1,0:T(4,128)(2,1)S(1)}, bf16[4,576]{1,0:T(4,128)(2,1)}, u32[]{:S(2)}) copy-start(bf16[4,576]{1,0:T(4,128)(2,1)} %new_ref.1) | copy-start | bytes 13828
  25.7 11.8 %copy-start.3 = (s32[4]{0:T(128)S(1)}, s32[4]{0:T(128)}, u32[]{:S(2)}) copy-start(s32[4]{0:T(128)} %len_ref.1) | copy-start | bytes 52
  33.0 7.4 %collective-permute-start.6 = (bf16[8,8,256]{2,1,0:T(8,128)(2,1)S(1)}, bf16[8,8,256]{2,1,0:T(8,128)(2,1)S(1)}, u32[]{:S(2)}, u32[]{:S(2)}) collective-permute-start(bf16[8,8,256]{2,1,0:T(8,128)(2,1)S(1)} %get-tuple-element.55), channel_id=1, source_target_pairs={{0,12},{4,8},{8,4},{12,0},{1,13},{5,9},{9,5},{13,1},{2,14},{6,10},... | collective-permute-start | bytes 98312 | tf_op jit(solution)/shard_map/ppermute | solution.py:501
  35.8 4.8 %collective-permute-start.7 = (bf16[8,8,256]{2,1,0:T(8,128)(2,1)S(1)}, bf16[8,8,256]{2,1,0:T(8,128)(2,1)S(1)}, u32[]{:S(2)}, u32[]{:S(2)}) collective-permute-start(bf16[8,8,256]{2,1,0:T(8,128)(2,1)S(1)} %get-tuple-element.56), channel_id=1, source_target_pairs={{0,8},{4,12},{8,0},{12,4},{1,9},{5,13},{9,1},{13,5},{2,10},{6,14},... | collective-permute-start | bytes 98312 | tf_op jit(solution)/shard_map/ppermute | solution.py:501
  35.8 4.8 %collective-permute-start.8 = (bf16[8,8,256]{2,1,0:T(8,128)(2,1)S(1)}, bf16[8,8,256]{2,1,0:T(8,128)(2,1)S(1)}, u32[]{:S(2)}, u32[]{:S(2)}) collective-permute-start(bf16[8,8,256]{2,1,0:T(8,128)(2,1)S(1)} %get-tuple-element.57), channel_id=1, source_target_pairs={{0,4},{4,0},{8,12},{12,8},{1,5},{5,1},{9,13},{13,9},{2,6},{6,2},{1... | collective-permute-start | bytes 98312 | tf_op jit(solution)/shard_map/ppermute | solution.py:501

commit v6 on v5

--- a/solution.py
+++ b/solution.py
@@ -11,12 +11,14 @@
 ROPE = 64
 GROUP = 128
 TOP = 8
-EARLY = 2
+EARLY = 3
 AHEAD = 6
 CHANNELS = 640
 SCOPE = 4 << 20
 GRANT = 16 << 20
-ORDER = (3, 2, 1)
+PARTS = {1: (0, 2), 2: (0,), 3: (0,)}
+ORDER = (2, 3, 1)
+BACK = (3, 2, 1)
 HELD = 14 << 20
 
 qk_scale = 192.0 ** (-0.5)
@@ -105,16 +107,17 @@
         pltpu.make_async_copy(ids_hbm, ids_ref, sems.at[2]),
     ]
     token_copies = []
-    for d, out in enumerate(outs):
-        for c in range(2):
-            start = pl.multiple_of((2 * me + c) * half, 128)
-            token_copies.append(
-                pltpu.make_async_copy(
-                    tokens_hbm.at[:, pl.ds(start, half)],
-                    out.at[pl.ds(c * block // 2, block // 2), pl.ds(0, half)],
-                    token_sems.at[d, c],
+    for i, out in enumerate(outs):
+        for j, b in enumerate(PARTS[ORDER[i]]):
+            for c in range(2):
+                start = pl.multiple_of((2 * (me ^ b) + c) * half, 128)
+                token_copies.append(
+                    pltpu.make_async_copy(
+                        tokens_hbm.at[:, pl.ds(start, half)],
+                        out.at[pl.ds(c * block // 2, block // 2), pl.ds(j * half, half)],
+                        token_sems.at[i, 2 * j + c],
+                    )
                 )
-            )
     for copy in cache + token_copies:
         copy.start()
     lat_ref[:, width:] = jnp.zeros((rows * per, CHANNELS - width), jnp.float32)
@@ -138,7 +141,7 @@
         if d == 0:
             own[...] = part
         else:
-            outs[ORDER.index(d)][:, half:] = part
+            outs[ORDER.index(d)][:, len(PARTS[d]) * half :] = part
     for copy in token_copies:
         copy.wait()
 
@@ -154,13 +157,13 @@
 def pack(codes, scales, tokens, expert_ids, n_ep):
     rows, per, width = codes.shape
     block = rows * per // n_ep
-    wide = tokens.shape[1] // 8 + CHANNELS
+    wide = [len(PARTS[d]) * tokens.shape[1] // 8 + CHANNELS for d in ORDER]
     scales, ids = scales.transpose(2, 1, 0), expert_ids.T
     return pl.pallas_call(
         pack_kernel,
         in_specs=[HBM] * 4,
         out_specs=[VM] * n_ep,
-        out_shape=[jax.ShapeDtypeStruct((block, wide), jnp.bfloat16)] * (n_ep - 1)
+        out_shape=[jax.ShapeDtypeStruct((block, w), jnp.bfloat16) for w in wide]
         + [jax.ShapeDtypeStruct((block, CHANNELS), jnp.bfloat16)],
         scratch_shapes=[
             pltpu.VMEM(codes.shape, jnp.bfloat16),
@@ -168,29 +171,39 @@
             pltpu.VMEM(ids.shape, jnp.int32),
             pltpu.VMEM((rows * per, CHANNELS), jnp.float32),
             pltpu.SemaphoreType.DMA((3,)),
-            pltpu.SemaphoreType.DMA((n_ep - 1, 2)),
+            pltpu.SemaphoreType.DMA((n_ep - 1, 4)),
         ],
         compiler_params=pltpu.CompilerParams(vmem_limit_bytes=SCOPE),
         name="pack",
     )(in_hbm(codes), in_hbm(scales), in_hbm(tokens), in_hbm(ids))
 
 
-def merge_kernel(*refs):
-    sources, out = refs[:-1], refs[-1]
-    rows, half = out.shape[0] // len(sources), out.shape[1] // 2
+def set_part(ref, at, source, j):
+    rows, half = source.shape[0] // 2, ref.shape[1] // 2
+    for c in range(2):
+        ref[at : at + rows, c * half : (c + 1) * half] = source[
+            c * rows : (c + 1) * rows, j * half : (j + 1) * half
+        ]
+
+
+def merge_kernel(near, *refs):
+    sources, (out, far) = refs[:-2], refs[-2:]
+    rows = near.shape[0] // 2
+    set_part(out, 0, near, 0)
     for d, source in enumerate(sources):
-        for c in range(2):
-            out[d * rows : (d + 1) * rows, c * half : (c + 1) * half] = source[
-                c * rows : (c + 1) * rows, :half
-            ]
-
-
-def merge(came, rows, half):
+        set_part(out, (d + 1) * rows, source, 0)
+        set_part(far, d * rows, source, 0)
+
+
+def merge(came, rows, quarter):
     return pl.pallas_call(
         merge_kernel,
         in_specs=[VM] * len(came),
-        out_specs=VM,
-        out_shape=jax.ShapeDtypeStruct((len(came) * rows, 2 * half), jnp.bfloat16),
+        out_specs=[VM] * 2,
+        out_shape=[
+            jax.ShapeDtypeStruct((n * rows, quarter), jnp.bfloat16)
+            for n in (len(came), len(came) - 1)
+        ],
         compiler_params=pltpu.CompilerParams(vmem_limit_bytes=SCOPE),
         name="merge",
     )(*came)
@@ -257,7 +270,7 @@
         earlier += jnp.where((ids_ref[k : k + 1, :] == ids) & (other < pair // top), 1, 0)
     slot = jnp.sum(earlier, axis=1, keepdims=True)
     column = lax.broadcasted_iota(jnp.int32, (1, experts * slots), 1)
-    for i, d in enumerate((0,) + ORDER):
+    for i, d in enumerate((0,) + BACK):
         match = (ids == (here ^ d) * experts + column // slots) & (column % slots == slot)
         select_ref[:, i * experts * slots : (i + 1) * experts * slots] = jnp.where(
             match, 1.0, 0.0
@@ -299,6 +312,14 @@
     start = pl.multiple_of((lax.axis_index("pf") ^ b) * quarter, 128)
     x_ref[:rows, :] = own_ref[:, pl.ds(start, quarter)]
     x_ref[rows : rows + came_ref.shape[0], :] = came_ref[...]
+
+
+def set_far_rows(b, x_ref, own_ref, near_ref, far_ref):
+    rows, quarter = own_ref.shape[0], far_ref.shape[1]
+    start = pl.multiple_of((lax.axis_index("pf") ^ b) * quarter, 128)
+    x_ref[:rows, :] = own_ref[:, pl.ds(start, quarter)]
+    set_part(x_ref, rows, near_ref, PARTS[1].index(b))
+    x_ref[2 * rows : 2 * rows + far_ref.shape[0], :] = far_ref[...]
 
 
 def times(x_ref, w_ref, e):
@@ -347,28 +368,25 @@
     set_rows(0, x_ref, own, came)
     set_rows(1, y_ref, own, came_too)
 
-    @pl.loop(0, experts, unroll=2)
-    def _(e):
-        @pl.when(e >= experts - AHEAD)
-        def _():
-            start(e - (experts - AHEAD))
-
-        gate[e] = times(x_ref, hg, e)
-        up[e] = times(x_ref, hu, e)
-
     @pl.loop(0, early)
     def _(e):
-        gate[e] += times(y_ref, mg, e)
-        up[e] += times(y_ref, mu, e)
-
-    set_slots(pieces, slots_ref, experts, own.shape[0], TOP)
+        gate[e] = times(x_ref, hg, e) + times(y_ref, mg, e)
+        up[e] = times(x_ref, hu, e) + times(y_ref, mu, e)
 
     @pl.loop(0, experts - early)
     def _(e):
+        for at in (2 * e, 2 * e + 1):
+
+            @pl.when(at < AHEAD)
+            def _():
+                start(at)
+
         wait_few(e)
-        gate[early + e] += times(y_ref, tg, e)
-        up[early + e] += times(y_ref, tu, e)
-
+        at = early + e
+        gate[at] = times(x_ref, hg, at) + times(y_ref, tg, e)
+        up[at] = times(x_ref, hu, at) + times(y_ref, tu, e)
+
+    set_slots(pieces, slots_ref, experts, own.shape[0], TOP)
     for_all(wait, AHEAD)
 
 
@@ -399,7 +417,7 @@
     return sums, (gate, up), slots
 
 
-def last_kernel(n_ep, own, came, came_too, hg, hu, g_hbm, u_hbm, gate, up, slots_ref, *refs):
+def last_kernel(n_ep, own, near, far, far_too, hg, hu, g_hbm, u_hbm, gate, up, slots_ref, *refs):
     outs, (gate_sum, up_sum, tg, tu, gb, ub, x_ref, y_ref, few_sems, sems) = refs[:-10], refs[-10:]
     experts, held = gate.shape[0], hg.shape[0]
     slots = outs[0].shape[1]
@@ -407,8 +425,8 @@
     start, wait = part_copies(3, 0, g_hbm, u_hbm, gb, ub, sems)
     for_all(start_few, experts - held)
     start(0)
-    set_rows(2, x_ref, own, came)
-    set_rows(3, y_ref, own, came_too)
+    set_far_rows(2, x_ref, own, near, far)
+    set_rows(3, y_ref, own, far_too)
 
     @pl.loop(0, held, unroll=2)
     def _(e):
@@ -427,32 +445,38 @@
         gate_sum[held + e] = gate[held + e] + times(x_ref, tg, e)
         up_sum[held + e] = up[held + e] + times(x_ref, tu, e)
 
-    @pl.loop(0, experts)
-    def _(e):
+    def add(e):
         wait(e)
         gate_sum[e] += times(y_ref, gb, e)
         up_sum[e] += times(y_ref, ub, e)
 
-    for e in range(experts):
+    def finish(e):
         gate_part = gate_sum[e]
         hidden = (gate_part * jax.nn.sigmoid(gate_part) * up_sum[e]).astype(jnp.bfloat16)
-        back = jnp.dot(
-            slots_ref[e * n_ep * slots : (e + 1) * n_ep * slots, :],
-            hidden,
-            preferred_element_type=jnp.float32,
-        ).astype(jnp.bfloat16)
+        places = pl.ds(pl.multiple_of(e * n_ep * slots, n_ep * slots), n_ep * slots)
+        back = jnp.dot(slots_ref[places, :], hidden, preferred_element_type=jnp.float32)
+        back = back.astype(jnp.bfloat16)
         for d in range(n_ep):
             outs[d][e] = back[d * slots : (d + 1) * slots]
 
-
-def last(n_ep, own, came, came_too, held, gate, up, slots, w_gate, w_up):
+    add(0)
+
+    @pl.loop(1, experts)
+    def _(e):
+        add(e)
+        finish(e - 1)
+
+    finish(experts - 1)
+
+
+def last(n_ep, own, near, far, far_too, held, gate, up, slots, w_gate, w_up):
     experts, depth, wide = w_gate.shape
-    rows, part = own.shape[0] + came.shape[0], depth // 4
+    rows, part = n_ep * own.shape[0], depth // 4
     rest = experts - AHEAD
     out = jax.ShapeDtypeStruct((experts, own.shape[0] // 2, wide), jnp.bfloat16)
     return pl.pallas_call(
         functools.partial(last_kernel, n_ep),
-        in_specs=[VM] * 5 + [HBM] * 2 + [VM] * 3,
+        in_specs=[VM] * 6 + [HBM] * 2 + [VM] * 3,
         out_specs=[VM] * n_ep,
         out_shape=[out] * n_ep,
         scratch_shapes=[pltpu.VMEM((experts, rows, wide), jnp.float32)] * 2
@@ -468,7 +492,7 @@
             vmem_limit_bytes=GRANT + (experts + EARLY) * 4 * part * wide
         ),
         name="last",
-    )(own, came, came_too, *[in_vmem(x) for x in held], w_gate, w_up, gate, up, slots)
+    )(own, near, far, far_too, *[in_vmem(x) for x in held], w_gate, w_up, gate, up, slots)
 
 
 def pick_kernel(select_ref, column_ref, *refs):
@@ -523,14 +547,14 @@
     *held, select, column = hold(expert_ids, routing_weights, w_gate, w_up, n_ep)
     came, held, select, column = lax.optimization_barrier((came, held, select, column))
     came = [came[ORDER.index(d)] for d in range(1, n_ep)]
-    x0 = merge(came, rows, half)
+    x0, far = merge(came, rows, 2 * half)
     x1 = crossed(x0, "pf", 1)
-    x2 = crossed(x0, "pf", 2)
+    x2 = crossed(far, "pf", 2)
     x3 = crossed(x0, "pf", 3)
     pieces = [own_piece] + came
     sums, held, slots = front(tokens, x0, x1, held, pieces, w_gate, w_up)
-    blocks = last(n_ep, tokens, x2, x3, held, *sums, slots, w_gate, w_up)
-    back = [blocks[0]] + [crossed(blocks[d], "ep", d) for d in ORDER]
+    blocks = last(n_ep, tokens, came[0], x2, x3, held, *sums, slots, w_gate, w_up)
+    back = [blocks[0]] + [crossed(blocks[d], "ep", d) for d in BACK]
     attention_out = attend(queries, new_latent, prompt_lengths, per, pieces)
     moe_hidden = pick(select, column, back)
     return attention_out, moe_hidden.reshape(rows, -1, moe_hidden.shape[1])

time: 41.6 us -> 41.2 us (level)
    pallas_call x1, Pallas kernels: 7.7 us -> 7.11 us  [front(): pl.pallas_call(front_kernel, in_specs=[VM] * 7 + [HBM] * 2 + [VM] * len(p...]
    pallas_call x1, Pallas kernels: 6.49 us -> 7.03 us  [hold(): pl.pallas_call(hold_kernel, in_specs=[HBM] * 4, out_specs=[VM] * 6, out_s...]
  transfers between devices with their start and end apart: 9 -> 9, of which waited for: 3 -> 2; matrix products, arithmetic and copies ran while one was open for 0% -> 0% of each run, Pallas kernels for 41% -> 42%
where the time goes in v6:
time: 41.2 us; the launch traced here: 41.1 us
  Pallas kernels  26.6 us (65%)
  starting transfers between devices  12.4 us (30%)
  waiting for transfers between devices  1.39 us (3%)
  between operations  0.73 us (2%)
    ppermute x9, starting transfers between devices, crossed(): return lax.ppermute(x, axis, [(s, s ^ bit) for s in range(n)])  12.4 us
    pallas_call x1, Pallas kernels, last(): pl.pallas_call(functools.partial(last_kernel, n_ep), in_specs=[VM] * 6 +...  7.2 us
    pallas_call x1, Pallas kernels, front(): pl.pallas_call(front_kernel, in_specs=[VM] * 7 + [HBM] * 2 + [VM] * len(p...  7.11 us
    pallas_call x1, Pallas kernels, hold(): pl.pallas_call(hold_kernel, in_specs=[HBM] * 4, out_specs=[VM] * 6, out_s...  7.03 us
    pallas_call x1, Pallas kernels, attend(): pl.pallas_call(functools.partial(attend_kernel, per), in_specs=[VM, VM, S...  2.99 us
    ppermute x9, waiting for transfers between devices, crossed(): return lax.ppermute(x, axis, [(s, s ^ bit) for s in range(n)])  1.39 us
    pallas_call x1, Pallas kernels, pack(): pl.pallas_call(pack_kernel, in_specs=[HBM] * 4, out_specs=[VM] * n_ep, ou...  1.33 us
    pallas_call x1, Pallas kernels, pick(): pl.pallas_call(pick_kernel, in_specs=[VM] * (2 + len(blocks)), out_specs=...  0.9 us
  transfers between devices with their start and end apart: 9, of which 2 were waited for; matrix products, arithmetic and copies ran while one was open for 0% of the time, Pallas kernels for 42%

profile of v6, /device:TPU:0, one launch (start us, length us, event | category | flops | bytes accessed | tf_op | source)
XLA Modules:
  0.0 41.1 jit_solution(14477382221326576729)
XLA Ops:
  0.6 1.3 %pack.1 = (bf16[32,1536]{1,0:T(8,128)(2,1)S(1)}, bf16[32,1536]{1,0:T(8,128)(2,1)S(1)}, bf16[32,2432]{1,0:T(8,128)(2,1)S(1)}, bf16[32,640]{1,0:T(8,128)(2,1)S(1)}) custom-call(bf16[16,8,576]{2,1,0:T(8,128)(2,1)} %codes_hbm.1, bf16[5,8,16]{2,1,0:T(8,128)(2,1)} %bitcast.9, bf16[16,7168]{1,0:T(8,128)(2,1)} %own.3, s32[8,16]{1,0:T(8,128)} %bitcast.7), custom_call_target="tpu_custom_call" | custom-call | tf_op jit(solution)/shard_map/pack/pallas_call | solution.py:162
  2.0 3.1 %collective-permute-start.2 = (bf16[32,2432]{1,0:T(8,128)(2,1)S(1)}, bf16[32,2432]{1,0:T(8,128)(2,1)S(1)}, u32[]{:S(2)}, u32[]{:S(2)}) collective-permute-start(bf16[32,2432]{1,0:T(8,128)(2,1)S(1)} %get-tuple-element.35), channel_id=1, source_target_pairs={{0,4},{4,0},{8,12},{12,8},{1,5},{5,1},{9,13},{13,9},{2,6},{6,2},{1... | collective-permute-start | bytes 466952 | tf_op jit(solution)/shard_map/ppermute | solution.py:525
  5.1 2.6 %collective-permute-start = (bf16[32,1536]{1,0:T(8,128)(2,1)S(1)}, bf16[32,1536]{1,0:T(8,128)(2,1)S(1)}, u32[]{:S(2)}, u32[]{:S(2)}) collective-permute-start(bf16[32,1536]{1,0:T(8,128)(2,1)S(1)} %get-tuple-element.33), channel_id=1, source_target_pairs={{0,8},{4,12},{8,0},{12,4},{1,9},{5,13},{9,1},{13,5},{2,10},{6,14},... | collective-permute-start | bytes 294920 | tf_op jit(solution)/shard_map/ppermute | solution.py:525
  7.7 0.0 collective-permute-start.1
  7.7 0.0 copy-start
  7.7 7.0 %hold.1 = (bf16[8,1792,256]{2,1,0:T(8,128)(2,1)S(1)}, bf16[8,1792,256]{2,1,0:T(8,128)(2,1)S(1)}, bf16[3,1792,256]{2,1,0:T(8,128)(2,1)S(1)}, bf16[3,1792,256]{2,1...) custom-call(s32[8,16]{1,0:T(8,128)} %bitcast.8, f32[8,16]{1,0:T(8,128)} %bitcast.10, ...), custom_call_target="tpu_custom_call" | custom-call | bytes 20185088 | tf_op jit(solution)/shard_map/hold/pallas_call | solution.py:286
  14.7 1.0 %collective-permute-done.refs_2_.refs_0_ = bf16[32,1536]{1,0:T(8,128)(2,1)S(1)} collective-permute-done((bf16[32,1536]{1,0:T(8,128)(2,1)S(1)}, bf16[32,1536]{1,0:T(8,128)(2,1)S(1)}, u32[]{:S(2)}, u32[]{:S(2)}) %collective-permute-start) | collective-permute-done | bytes 98336 | tf_op jit(solution)/shard_map/ppermute | solution.py:525
  15.7 0.0 collective-permute-done.1.refs_3_.refs_1_
  15.7 0.0 collective-permute-done.2.refs_1_.near
  15.8 0.1 collective-permute-start.5
  15.8 1.6 %collective-permute-start.4 = (bf16[48,1792]{1,0:T(8,128)(2,1)S(1)}, bf16[48,1792]{1,0:T(8,128)(2,1)S(1)}, u32[]{:S(2)}, u32[]{:S(2)}) collective-permute-start(bf16[48,1792]{1,0:T(8,128)(2,1)S(1)} %get-tuple-element.48.came), channel_id=1, source_target_pairs={{0,3},{1,2},{2,1},{3,0},{4,7},{5,6},{6,5},{7,4},{8,11},{9,10},{10,... | collective-permute-start | bytes 516104 | tf_op jit(solution)/shard_map/ppermute | solution.py:525
  17.4 0.5 %collective-permute-start.3 = (bf16[32,1792]{1,0:T(8,128)(2,1)S(1)}, bf16[32,1792]{1,0:T(8,128)(2,1)S(1)}, u32[]{:S(2)}, u32[]{:S(2)}) collective-permute-start(bf16[32,1792]{1,0:T(8,128)(2,1)S(1)} %get-tuple-element.47), channel_id=1, source_target_pairs={{0,2},{1,3},{2,0},{3,1},{4,6},{5,7},{6,4},{7,5},{8,10},{9,11},{10,... | collective-permute-start | bytes 344072 | tf_op jit(solution)/shard_map/ppermute | solution.py:525
  18.0 0.0 collective-permute-done.5.came_too
  18.0 0.0 copy-done
  18.0 7.1 %front.1 = (f32[8,64,256]{2,1,0:T(8,128)S(1)}, f32[8,64,256]{2,1,0:T(8,128)S(1)}, bf16[6,1792,256]{2,1,0:T(8,128)(2,1)S(1)}, bf16[6,1792,256]{2,1,0:T(8,128)(2,1)S(1)}, bf16[256,64]{1,0:T(8,128)(2,1)S(1)}) custom-call(bf16[16,7168]{1,0:T(8,128)(2,1)S(1)} %copy-done, bf16[48,1792]{1,0:T(8,128)(2,1)S(1)} %get-tuple-element.48.came, ...), custom_call_target="tpu_custom_call" | custom-call | flops 1879048192 | bytes 20185088 | tf_op jit(solution)/shard_map/front/pallas_call | solution.py:399
  25.1 0.0 collective-permute-done.3.far
  25.1 0.0 collective-permute-done.4.far_too
  25.1 0.0 copy-start.1
  25.1 0.0 copy-start.2
  25.2 0.0 copy-start.3
  25.2 7.2 %last.1 = (bf16[8,8,256]{2,1,0:T(8,128)(2,1)S(1)}, bf16[8,8,256]{2,1,0:T(8,128)(2,1)S(1)}, bf16[8,8,256]{2,1,0:T(8,128)(2,1)S(1)}, bf16[8,8,256]{2,1,0:T(8,128)(2,1)S(1)}) custom-call(bf16[16,7168]{1,0:T(8,128)(2,1)S(1)} %copy-done, bf16[32,2432]{1,0:T(8,128)(2,1)S(1)} %collective-permute-done.2.refs_1_.near, ...), custom_call_target="tpu_custom_call" | custom-call | flops 1879048192 | bytes 18350080 | tf_op jit(solution)/shard_map/last/pallas_call | solution.py:477
  32.4 2.9 %collective-permute-start.6 = (bf16[8,8,256]{2,1,0:T(8,128)(2,1)S(1)}, bf16[8,8,256]{2,1,0:T(8,128)(2,1)S(1)}, u32[]{:S(2)}, u32[]{:S(2)}) collective-permute-start(bf16[8,8,256]{2,1,0:T(8,128)(2,1)S(1)} %get-tuple-element.59), channel_id=1, source_target_pairs={{0,12},{4,8},{8,4},{12,0},{1,13},{5,9},{9,5},{13,1},{2,14},{6,10},... | collective-permute-start | bytes 98312 | tf_op jit(solution)/shard_map/ppermute | solution.py:525
  35.3 0.3 collective-permute-start.7
  35.5 1.3 %collective-permute-start.8 = (bf16[8,8,256]{2,1,0:T(8,128)(2,1)S(1)}, bf16[8,8,256]{2,1,0:T(8,128)(2,1)S(1)}, u32[]{:S(2)}, u32[]{:S(2)}) collective-permute-start(bf16[8,8,256]{2,1,0:T(8,128)(2,1)S(1)} %get-tuple-element.61), channel_id=1, source_target_pairs={{0,4},{4,0},{8,12},{12,8},{1,5},{5,1},{9,13},{13,9},{2,6},{6,2},{1... | collective-permute-start | bytes 98312 | tf_op jit(solution)/shard_map/ppermute | solution.py:525
  36.8 0.0 copy-done.1
  36.8 0.0 copy-done.2
  36.8 0.0 copy-done.3
  36.8 3.0 %attend.1 = bf16[4,128,512]{2,1,0:T(8,128)(2,1)} custom-call(bf16[4,576,128]{2,1,0:T(8,128)(2,1)S(1)} %bitcast.5, bf16[4,576]{1,0:T(4,128)(2,1)S(1)} %copy-done.2, s32[4]{0:T(128)S(1)} %copy-done.3, bf16[32,640]{1,0:T(8,128)(2,1)S(1)} %get-tuple-element.32.refs_0_, bf16[32,2432]{1,0:T(8,128)(2,1)S(1)} %collective-permute-done.2.refs_1_.near, ...), custom_call_target="tpu_custom_call" | custom-call | flops 301989888 | bytes 1114112 | tf_op jit(solution)/shard_map/attend/pallas_call | solution.py:77
  39.8 0.0 collective-permute-done.6.refs_1_
  39.8 0.3 collective-permute-done.7.refs_2_
  40.2 0.0 collective-permute-done.8.refs_3_
  40.2 0.9 %pick.1 = bf16[128,256]{1,0:T(8,128)(2,1)} custom-call(bf16[128,256]{1,0:T(8,128)(2,1)S(1)} %get-tuple-element.45.select_ref, f32[128,1]{1,0:T(8,128)S(1)} %get-tuple-element.46.column_ref, bf16[8,8,256]{2,1,0:T(8,128)(2,1)S(1)} %get-tuple-element.58.refs_0_, bf16[8,8,256]{2,1,0:T(8,128)(2,1)S(1)} %collective-permute-done.6.refs_1_, ...), custom_call_target="tpu_custom_call" | custom-call | tf_op jit(solution)/shard_map/pick/pallas_call | solution.py:513
  (1 shorter events, 0.0 us)
Async XLA Ops:
  2.0 13.8 %collective-permute-start.2 = (bf16[32,2432]{1,0:T(8,128)(2,1)S(1)}, bf16[32,2432]{1,0:T(8,128)(2,1)S(1)}, u32[]{:S(2)}, u32[]{:S(2)}) collective-permute-start(bf16[32,2432]{1,0:T(8,128)(2,1)S(1)} %get-tuple-element.35), channel_id=1, source_target_pairs={{0,4},{4,0},{8,12},{12,8},{1,5},{5,1},{9,13},{13,9},{2,6},{6,2},{1... | collective-permute-start | bytes 466952 | tf_op jit(solution)/shard_map/ppermute | solution.py:525
  5.1 10.7 %collective-permute-start = (bf16[32,1536]{1,0:T(8,128)(2,1)S(1)}, bf16[32,1536]{1,0:T(8,128)(2,1)S(1)}, u32[]{:S(2)}, u32[]{:S(2)}) collective-permute-start(bf16[32,1536]{1,0:T(8,128)(2,1)S(1)} %get-tuple-element.33), channel_id=1, source_target_pairs={{0,8},{4,12},{8,0},{12,4},{1,9},{5,13},{9,1},{13,5},{2,10},{6,14},... | collective-permute-start | bytes 294920 | tf_op jit(solution)/shard_map/ppermute | solution.py:525
  7.7 8.1 %collective-permute-start.1 = (bf16[32,1536]{1,0:T(8,128)(2,1)S(1)}, bf16[32,1536]{1,0:T(8,128)(2,1)S(1)}, u32[]{:S(2)}, u32[]{:S(2)}) collective-permute-start(bf16[32,1536]{1,0:T(8,128)(2,1)S(1)} %get-tuple-element.34), channel_id=1, source_target_pairs={{0,12},{4,8},{8,4},{12,0},{1,13},{5,9},{9,5},{13,1},{2,14},{6,10},... | collective-permute-start | bytes 294920 | tf_op jit(solution)/shard_map/ppermute | solution.py:525
  7.7 10.3 %copy-start = (bf16[16,7168]{1,0:T(8,128)(2,1)S(1)}, bf16[16,7168]{1,0:T(8,128)(2,1)}, u32[]{:S(2)}) copy-start(bf16[16,7168]{1,0:T(8,128)(2,1)} %own.3) | copy-start | bytes 688132
  15.8 2.2 %collective-permute-start.5 = (bf16[48,1792]{1,0:T(8,128)(2,1)S(1)}, bf16[48,1792]{1,0:T(8,128)(2,1)S(1)}, u32[]{:S(2)}, u32[]{:S(2)}) collective-permute-start(bf16[48,1792]{1,0:T(8,128)(2,1)S(1)} %get-tuple-element.48.came), channel_id=1, source_target_pairs={{0,1},{1,0},{2,3},{3,2},{4,5},{5,4},{6,7},{7,6},{8,9},{9,8},{10,11... | collective-permute-start | bytes 516104 | tf_op jit(solution)/shard_map/ppermute | solution.py:525
  15.8 9.3 %collective-permute-start.4 = (bf16[48,1792]{1,0:T(8,128)(2,1)S(1)}, bf16[48,1792]{1,0:T(8,128)(2,1)S(1)}, u32[]{:S(2)}, u32[]{:S(2)}) collective-permute-start(bf16[48,1792]{1,0:T(8,128)(2,1)S(1)} %get-tuple-element.48.came), channel_id=1, source_target_pairs={{0,3},{1,2},{2,1},{3,0},{4,7},{5,6},{6,5},{7,4},{8,11},{9,10},{10,... | collective-permute-start | bytes 516104 | tf_op jit(solution)/shard_map/ppermute | solution.py:525
  17.4 7.7 %collective-permute-start.3 = (bf16[32,1792]{1,0:T(8,128)(2,1)S(1)}, bf16[32,1792]{1,0:T(8,128)(2,1)S(1)}, u32[]{:S(2)}, u32[]{:S(2)}) collective-permute-start(bf16[32,1792]{1,0:T(8,128)(2,1)S(1)} %get-tuple-element.47), channel_id=1, source_target_pairs={{0,2},{1,3},{2,0},{3,1},{4,6},{5,7},{6,4},{7,5},{8,10},{9,11},{10,... | collective-permute-start | bytes 344072 | tf_op jit(solution)/shard_map/ppermute | solution.py:525
  25.1 11.7 %copy-start.1 = (bf16[4,128,576]{1,2,0:T(8,128)(2,1)S(1)}, bf16[4,128,576]{1,2,0:T(8,128)(2,1)}, u32[]{:S(2)}) copy-start(bf16[4,128,576]{1,2,0:T(8,128)(2,1)} %param.12) | copy-start | bytes 1769476
  25.1 11.7 %copy-start.2 = (bf16[4,576]{1,0:T(4,128)(2,1)S(1)}, bf16[4,576]{1,0:T(4,128)(2,1)}, u32[]{:S(2)}) copy-start(bf16[4,576]{1,0:T(4,128)(2,1)} %new_ref.1) | copy-start | bytes 13828
  25.2 11.7 %copy-start.3 = (s32[4]{0:T(128)S(1)}, s32[4]{0:T(128)}, u32[]{:S(2)}) copy-start(s32[4]{0:T(128)} %len_ref.1) | copy-start | bytes 52
  32.4 7.5 %collective-permute-start.6 = (bf16[8,8,256]{2,1,0:T(8,128)(2,1)S(1)}, bf16[8,8,256]{2,1,0:T(8,128)(2,1)S(1)}, u32[]{:S(2)}, u32[]{:S(2)}) collective-permute-start(bf16[8,8,256]{2,1,0:T(8,128)(2,1)S(1)} %get-tuple-element.59), channel_id=1, source_target_pairs={{0,12},{4,8},{8,4},{12,0},{1,13},{5,9},{9,5},{13,1},{2,14},{6,10},... | collective-permute-start | bytes 98312 | tf_op jit(solution)/shard_map/ppermute | solution.py:525
  35.3 4.9 %collective-permute-start.7 = (bf16[8,8,256]{2,1,0:T(8,128)(2,1)S(1)}, bf16[8,8,256]{2,1,0:T(8,128)(2,1)S(1)}, u32[]{:S(2)}, u32[]{:S(2)}) collective-permute-start(bf16[8,8,256]{2,1,0:T(8,128)(2,1)S(1)} %get-tuple-element.60), channel_id=1, source_target_pairs={{0,8},{4,12},{8,0},{12,4},{1,9},{5,13},{9,1},{13,5},{2,10},{6,14},... | collective-permute-start | bytes 98312 | tf_op jit(solution)/shard_map/ppermute | solution.py:525
  35.5 4.7 %collective-permute-start.8 = (bf16[8,8,256]{2,1,0:T(8,128)(2,1)S(1)}, bf16[8,8,256]{2,1,0:T(8,128)(2,1)S(1)}, u32[]{:S(2)}, u32[]{:S(2)}) collective-permute-start(bf16[8,8,256]{2,1,0:T(8,128)(2,1)S(1)} %get-tuple-element.61), channel_id=1, source_target_pairs={{0,4},{4,0},{8,12},{12,8},{1,5},{5,1},{9,13},{13,9},{2,6},{6,2},{1... | collective-permute-start | bytes 98312 | tf_op jit(solution)/shard_map/ppermute | solution.py:525

commit v7 on v6

--- a/solution.py
+++ b/solution.py
@@ -368,7 +368,11 @@
     set_rows(0, x_ref, own, came)
     set_rows(1, y_ref, own, came_too)
 
-    @pl.loop(0, early)
+    gate[0] = times(x_ref, hg, 0) + times(y_ref, mg, 0)
+    set_slots(pieces, slots_ref, experts, own.shape[0], TOP)
+    up[0] = times(x_ref, hu, 0) + times(y_ref, mu, 0)
+
+    @pl.loop(1, early)
     def _(e):
         gate[e] = times(x_ref, hg, e) + times(y_ref, mg, e)
         up[e] = times(x_ref, hu, e) + times(y_ref, mu, e)
@@ -386,7 +390,6 @@
         gate[at] = times(x_ref, hg, at) + times(y_ref, tg, e)
         up[at] = times(x_ref, hu, at) + times(y_ref, tu, e)
 
-    set_slots(pieces, slots_ref, experts, own.shape[0], TOP)
     for_all(wait, AHEAD)
 
 

time: 41.2 us -> 41.2 us (level)
  no operation moved by 1% of the time
where the time goes in v7:
time: 41.2 us; the launch traced here: 41.1 us
  Pallas kernels  26.6 us (65%)
  starting transfers between devices  12.4 us (30%)
  waiting for transfers between devices  1.39 us (3%)
  between operations  0.73 us (2%)
    ppermute x9, starting transfers between devices, crossed(): return lax.ppermute(x, axis, [(s, s ^ bit) for s in range(n)])  12.4 us
    pallas_call x1, Pallas kernels, last(): pl.pallas_call(functools.partial(last_kernel, n_ep), in_specs=[VM] * 6 +...  7.2 us
    pallas_call x1, Pallas kernels, front(): pl.pallas_call(front_kernel, in_specs=[VM] * 7 + [HBM] * 2 + [VM] * len(p...  7.11 us
    pallas_call x1, Pallas kernels, hold(): pl.pallas_call(hold_kernel, in_specs=[HBM] * 4, out_specs=[VM] * 6, out_s...  7.03 us
    pallas_call x1, Pallas kernels, attend(): pl.pallas_call(functools.partial(attend_kernel, per), in_specs=[VM, VM, S...  2.99 us
    ppermute x9, waiting for transfers between devices, crossed(): return lax.ppermute(x, axis, [(s, s ^ bit) for s in range(n)])  1.39 us
    pallas_call x1, Pallas kernels, pack(): pl.pallas_call(pack_kernel, in_specs=[HBM] * 4, out_specs=[VM] * n_ep, ou...  1.33 us
    pallas_call x1, Pallas kernels, pick(): pl.pallas_call(pick_kernel, in_specs=[VM] * (2 + len(blocks)), out_specs=...  0.9 us
  transfers between devices with their start and end apart: 9, of which 2 were waited for; matrix products, arithmetic and copies ran while one was open for 0% of the time, Pallas kernels for 42%

profile of v7, /device:TPU:0, one launch (start us, length us, event | category | flops | bytes accessed | tf_op | source)
XLA Modules:
  0.0 41.1 jit_solution(2972933548404625645)
XLA Ops:
  0.6 1.3 %pack.1 = (bf16[32,1536]{1,0:T(8,128)(2,1)S(1)}, bf16[32,1536]{1,0:T(8,128)(2,1)S(1)}, bf16[32,2432]{1,0:T(8,128)(2,1)S(1)}, bf16[32,640]{1,0:T(8,128)(2,1)S(1)}) custom-call(bf16[16,8,576]{2,1,0:T(8,128)(2,1)} %codes_hbm.1, bf16[5,8,16]{2,1,0:T(8,128)(2,1)} %bitcast.9, bf16[16,7168]{1,0:T(8,128)(2,1)} %own.3, s32[8,16]{1,0:T(8,128)} %bitcast.7), custom_call_target="tpu_custom_call" | custom-call | tf_op jit(solution)/shard_map/pack/pallas_call | solution.py:162
  2.0 3.1 %collective-permute-start.2 = (bf16[32,2432]{1,0:T(8,128)(2,1)S(1)}, bf16[32,2432]{1,0:T(8,128)(2,1)S(1)}, u32[]{:S(2)}, u32[]{:S(2)}) collective-permute-start(bf16[32,2432]{1,0:T(8,128)(2,1)S(1)} %get-tuple-element.35), channel_id=1, source_target_pairs={{0,4},{4,0},{8,12},{12,8},{1,5},{5,1},{9,13},{13,9},{2,6},{6,2},{1... | collective-permute-start | bytes 466952 | tf_op jit(solution)/shard_map/ppermute | solution.py:528
  5.1 2.6 %collective-permute-start = (bf16[32,1536]{1,0:T(8,128)(2,1)S(1)}, bf16[32,1536]{1,0:T(8,128)(2,1)S(1)}, u32[]{:S(2)}, u32[]{:S(2)}) collective-permute-start(bf16[32,1536]{1,0:T(8,128)(2,1)S(1)} %get-tuple-element.33), channel_id=1, source_target_pairs={{0,8},{4,12},{8,0},{12,4},{1,9},{5,13},{9,1},{13,5},{2,10},{6,14},... | collective-permute-start | bytes 294920 | tf_op jit(solution)/shard_map/ppermute | solution.py:528
  7.7 0.0 collective-permute-start.1
  7.7 0.0 copy-start
  7.7 7.0 %hold.1 = (bf16[8,1792,256]{2,1,0:T(8,128)(2,1)S(1)}, bf16[8,1792,256]{2,1,0:T(8,128)(2,1)S(1)}, bf16[3,1792,256]{2,1,0:T(8,128)(2,1)S(1)}, bf16[3,1792,256]{2,1...) custom-call(s32[8,16]{1,0:T(8,128)} %bitcast.8, f32[8,16]{1,0:T(8,128)} %bitcast.10, ...), custom_call_target="tpu_custom_call" | custom-call | bytes 20185088 | tf_op jit(solution)/shard_map/hold/pallas_call | solution.py:286
  14.7 1.0 %collective-permute-done.refs_2_.refs_0_ = bf16[32,1536]{1,0:T(8,128)(2,1)S(1)} collective-permute-done((bf16[32,1536]{1,0:T(8,128)(2,1)S(1)}, bf16[32,1536]{1,0:T(8,128)(2,1)S(1)}, u32[]{:S(2)}, u32[]{:S(2)}) %collective-permute-start) | collective-permute-done | bytes 98336 | tf_op jit(solution)/shard_map/ppermute | solution.py:528
  15.7 0.0 collective-permute-done.1.refs_3_.refs_1_
  15.7 0.0 collective-permute-done.2.refs_1_.near
  15.8 0.1 collective-permute-start.5
  15.8 1.6 %collective-permute-start.4 = (bf16[48,1792]{1,0:T(8,128)(2,1)S(1)}, bf16[48,1792]{1,0:T(8,128)(2,1)S(1)}, u32[]{:S(2)}, u32[]{:S(2)}) collective-permute-start(bf16[48,1792]{1,0:T(8,128)(2,1)S(1)} %get-tuple-element.48.came), channel_id=1, source_target_pairs={{0,3},{1,2},{2,1},{3,0},{4,7},{5,6},{6,5},{7,4},{8,11},{9,10},{10,... | collective-permute-start | bytes 516104 | tf_op jit(solution)/shard_map/ppermute | solution.py:528
  17.4 0.5 %collective-permute-start.3 = (bf16[32,1792]{1,0:T(8,128)(2,1)S(1)}, bf16[32,1792]{1,0:T(8,128)(2,1)S(1)}, u32[]{:S(2)}, u32[]{:S(2)}) collective-permute-start(bf16[32,1792]{1,0:T(8,128)(2,1)S(1)} %get-tuple-element.47), channel_id=1, source_target_pairs={{0,2},{1,3},{2,0},{3,1},{4,6},{5,7},{6,4},{7,5},{8,10},{9,11},{10,... | collective-permute-start | bytes 344072 | tf_op jit(solution)/shard_map/ppermute | solution.py:528
  18.0 0.0 collective-permute-done.5.came_too
  18.0 0.0 copy-done
  18.0 7.1 %front.1 = (f32[8,64,256]{2,1,0:T(8,128)S(1)}, f32[8,64,256]{2,1,0:T(8,128)S(1)}, bf16[6,1792,256]{2,1,0:T(8,128)(2,1)S(1)}, bf16[6,1792,256]{2,1,0:T(8,128)(2,1)S(1)}, bf16[256,64]{1,0:T(8,128)(2,1)S(1)}) custom-call(bf16[16,7168]{1,0:T(8,128)(2,1)S(1)} %copy-done, bf16[48,1792]{1,0:T(8,128)(2,1)S(1)} %get-tuple-element.48.came, ...), custom_call_target="tpu_custom_call" | custom-call | flops 1879048192 | bytes 20185088 | tf_op jit(solution)/shard_map/front/pallas_call | solution.py:402
  25.1 0.0 collective-permute-done.3.far
  25.1 0.0 collective-permute-done.4.far_too
  25.1 0.0 copy-start.1
  25.1 0.0 copy-start.2
  25.2 0.0 copy-start.3
  25.2 7.2 %last.1 = (bf16[8,8,256]{2,1,0:T(8,128)(2,1)S(1)}, bf16[8,8,256]{2,1,0:T(8,128)(2,1)S(1)}, bf16[8,8,256]{2,1,0:T(8,128)(2,1)S(1)}, bf16[8,8,256]{2,1,0:T(8,128)(2,1)S(1)}) custom-call(bf16[16,7168]{1,0:T(8,128)(2,1)S(1)} %copy-done, bf16[32,2432]{1,0:T(8,128)(2,1)S(1)} %collective-permute-done.2.refs_1_.near, ...), custom_call_target="tpu_custom_call" | custom-call | flops 1879048192 | bytes 18350080 | tf_op jit(solution)/shard_map/last/pallas_call | solution.py:480
  32.4 2.9 %collective-permute-start.6 = (bf16[8,8,256]{2,1,0:T(8,128)(2,1)S(1)}, bf16[8,8,256]{2,1,0:T(8,128)(2,1)S(1)}, u32[]{:S(2)}, u32[]{:S(2)}) collective-permute-start(bf16[8,8,256]{2,1,0:T(8,128)(2,1)S(1)} %get-tuple-element.59), channel_id=1, source_target_pairs={{0,12},{4,8},{8,4},{12,0},{1,13},{5,9},{9,5},{13,1},{2,14},{6,10},... | collective-permute-start | bytes 98312 | tf_op jit(solution)/shard_map/ppermute | solution.py:528
  35.3 0.3 collective-permute-start.7
  35.5 1.3 %collective-permute-start.8 = (bf16[8,8,256]{2,1,0:T(8,128)(2,1)S(1)}, bf16[8,8,256]{2,1,0:T(8,128)(2,1)S(1)}, u32[]{:S(2)}, u32[]{:S(2)}) collective-permute-start(bf16[8,8,256]{2,1,0:T(8,128)(2,1)S(1)} %get-tuple-element.61), channel_id=1, source_target_pairs={{0,4},{4,0},{8,12},{12,8},{1,5},{5,1},{9,13},{13,9},{2,6},{6,2},{1... | collective-permute-start | bytes 98312 | tf_op jit(solution)/shard_map/ppermute | solution.py:528
  36.8 0.0 copy-done.1
  36.8 0.0 copy-done.2
  36.8 0.0 copy-done.3
  36.8 3.0 %attend.1 = bf16[4,128,512]{2,1,0:T(8,128)(2,1)} custom-call(bf16[4,576,128]{2,1,0:T(8,128)(2,1)S(1)} %bitcast.5, bf16[4,576]{1,0:T(4,128)(2,1)S(1)} %copy-done.2, s32[4]{0:T(128)S(1)} %copy-done.3, bf16[32,640]{1,0:T(8,128)(2,1)S(1)} %get-tuple-element.32.refs_0_, bf16[32,2432]{1,0:T(8,128)(2,1)S(1)} %collective-permute-done.2.refs_1_.near, ...), custom_call_target="tpu_custom_call" | custom-call | flops 301989888 | bytes 1114112 | tf_op jit(solution)/shard_map/attend/pallas_call | solution.py:77
  39.8 0.0 collective-permute-done.6.refs_1_
  39.8 0.3 collective-permute-done.7.refs_2_
  40.2 0.0 collective-permute-done.8.refs_3_
  40.2 0.9 %pick.1 = bf16[128,256]{1,0:T(8,128)(2,1)} custom-call(bf16[128,256]{1,0:T(8,128)(2,1)S(1)} %get-tuple-element.45.select_ref, f32[128,1]{1,0:T(8,128)S(1)} %get-tuple-element.46.column_ref, bf16[8,8,256]{2,1,0:T(8,128)(2,1)S(1)} %get-tuple-element.58.refs_0_, bf16[8,8,256]{2,1,0:T(8,128)(2,1)S(1)} %collective-permute-done.6.refs_1_, ...), custom_call_target="tpu_custom_call" | custom-call | tf_op jit(solution)/shard_map/pick/pallas_call | solution.py:516
  (1 shorter events, 0.0 us)
Async XLA Ops:
  2.0 13.8 %collective-permute-start.2 = (bf16[32,2432]{1,0:T(8,128)(2,1)S(1)}, bf16[32,2432]{1,0:T(8,128)(2,1)S(1)}, u32[]{:S(2)}, u32[]{:S(2)}) collective-permute-start(bf16[32,2432]{1,0:T(8,128)(2,1)S(1)} %get-tuple-element.35), channel_id=1, source_target_pairs={{0,4},{4,0},{8,12},{12,8},{1,5},{5,1},{9,13},{13,9},{2,6},{6,2},{1... | collective-permute-start | bytes 466952 | tf_op jit(solution)/shard_map/ppermute | solution.py:528
  5.1 10.7 %collective-permute-start = (bf16[32,1536]{1,0:T(8,128)(2,1)S(1)}, bf16[32,1536]{1,0:T(8,128)(2,1)S(1)}, u32[]{:S(2)}, u32[]{:S(2)}) collective-permute-start(bf16[32,1536]{1,0:T(8,128)(2,1)S(1)} %get-tuple-element.33), channel_id=1, source_target_pairs={{0,8},{4,12},{8,0},{12,4},{1,9},{5,13},{9,1},{13,5},{2,10},{6,14},... | collective-permute-start | bytes 294920 | tf_op jit(solution)/shard_map/ppermute | solution.py:528
  7.7 8.1 %collective-permute-start.1 = (bf16[32,1536]{1,0:T(8,128)(2,1)S(1)}, bf16[32,1536]{1,0:T(8,128)(2,1)S(1)}, u32[]{:S(2)}, u32[]{:S(2)}) collective-permute-start(bf16[32,1536]{1,0:T(8,128)(2,1)S(1)} %get-tuple-element.34), channel_id=1, source_target_pairs={{0,12},{4,8},{8,4},{12,0},{1,13},{5,9},{9,5},{13,1},{2,14},{6,10},... | collective-permute-start | bytes 294920 | tf_op jit(solution)/shard_map/ppermute | solution.py:528
  7.7 10.3 %copy-start = (bf16[16,7168]{1,0:T(8,128)(2,1)S(1)}, bf16[16,7168]{1,0:T(8,128)(2,1)}, u32[]{:S(2)}) copy-start(bf16[16,7168]{1,0:T(8,128)(2,1)} %own.3) | copy-start | bytes 688132
  15.8 2.2 %collective-permute-start.5 = (bf16[48,1792]{1,0:T(8,128)(2,1)S(1)}, bf16[48,1792]{1,0:T(8,128)(2,1)S(1)}, u32[]{:S(2)}, u32[]{:S(2)}) collective-permute-start(bf16[48,1792]{1,0:T(8,128)(2,1)S(1)} %get-tuple-element.48.came), channel_id=1, source_target_pairs={{0,1},{1,0},{2,3},{3,2},{4,5},{5,4},{6,7},{7,6},{8,9},{9,8},{10,11... | collective-permute-start | bytes 516104 | tf_op jit(solution)/shard_map/ppermute | solution.py:528
  15.8 9.3 %collective-permute-start.4 = (bf16[48,1792]{1,0:T(8,128)(2,1)S(1)}, bf16[48,1792]{1,0:T(8,128)(2,1)S(1)}, u32[]{:S(2)}, u32[]{:S(2)}) collective-permute-start(bf16[48,1792]{1,0:T(8,128)(2,1)S(1)} %get-tuple-element.48.came), channel_id=1, source_target_pairs={{0,3},{1,2},{2,1},{3,0},{4,7},{5,6},{6,5},{7,4},{8,11},{9,10},{10,... | collective-permute-start | bytes 516104 | tf_op jit(solution)/shard_map/ppermute | solution.py:528
  17.4 7.7 %collective-permute-start.3 = (bf16[32,1792]{1,0:T(8,128)(2,1)S(1)}, bf16[32,1792]{1,0:T(8,128)(2,1)S(1)}, u32[]{:S(2)}, u32[]{:S(2)}) collective-permute-start(bf16[32,1792]{1,0:T(8,128)(2,1)S(1)} %get-tuple-element.47), channel_id=1, source_target_pairs={{0,2},{1,3},{2,0},{3,1},{4,6},{5,7},{6,4},{7,5},{8,10},{9,11},{10,... | collective-permute-start | bytes 344072 | tf_op jit(solution)/shard_map/ppermute | solution.py:528
  25.1 11.7 %copy-start.1 = (bf16[4,128,576]{1,2,0:T(8,128)(2,1)S(1)}, bf16[4,128,576]{1,2,0:T(8,128)(2,1)}, u32[]{:S(2)}) copy-start(bf16[4,128,576]{1,2,0:T(8,128)(2,1)} %param.12) | copy-start | bytes 1769476
  25.1 11.7 %copy-start.2 = (bf16[4,576]{1,0:T(4,128)(2,1)S(1)}, bf16[4,576]{1,0:T(4,128)(2,1)}, u32[]{:S(2)}) copy-start(bf16[4,576]{1,0:T(4,128)(2,1)} %new_ref.1) | copy-start | bytes 13828
  25.2 11.7 %copy-start.3 = (s32[4]{0:T(128)S(1)}, s32[4]{0:T(128)}, u32[]{:S(2)}) copy-start(s32[4]{0:T(128)} %len_ref.1) | copy-start | bytes 52
  32.4 7.5 %collective-permute-start.6 = (bf16[8,8,256]{2,1,0:T(8,128)(2,1)S(1)}, bf16[8,8,256]{2,1,0:T(8,128)(2,1)S(1)}, u32[]{:S(2)}, u32[]{:S(2)}) collective-permute-start(bf16[8,8,256]{2,1,0:T(8,128)(2,1)S(1)} %get-tuple-element.59), channel_id=1, source_target_pairs={{0,12},{4,8},{8,4},{12,0},{1,13},{5,9},{9,5},{13,1},{2,14},{6,10},... | collective-permute-start | bytes 98312 | tf_op jit(solution)/shard_map/ppermute | solution.py:528
  35.3 4.9 %collective-permute-start.7 = (bf16[8,8,256]{2,1,0:T(8,128)(2,1)S(1)}, bf16[8,8,256]{2,1,0:T(8,128)(2,1)S(1)}, u32[]{:S(2)}, u32[]{:S(2)}) collective-permute-start(bf16[8,8,256]{2,1,0:T(8,128)(2,1)S(1)} %get-tuple-element.60), channel_id=1, source_target_pairs={{0,8},{4,12},{8,0},{12,4},{1,9},{5,13},{9,1},{13,5},{2,10},{6,14},... | collective-permute-start | bytes 98312 | tf_op jit(solution)/shard_map/ppermute | solution.py:528
  35.5 4.7 %collective-permute-start.8 = (bf16[8,8,256]{2,1,0:T(8,128)(2,1)S(1)}, bf16[8,8,256]{2,1,0:T(8,128)(2,1)S(1)}, u32[]{:S(2)}, u32[]{:S(2)}) collective-permute-start(bf16[8,8,256]{2,1,0:T(8,128)(2,1)S(1)} %get-tuple-element.61), channel_id=1, source_target_pairs={{0,4},{4,0},{8,12},{12,8},{1,5},{5,1},{9,13},{13,9},{2,6},{6,2},{1... | collective-permute-start | bytes 98312 | tf_op jit(solution)/shard_map/ppermute | solution.py:528

commit v8 on v7

--- a/solution.py
+++ b/solution.py
@@ -17,7 +17,7 @@
 SCOPE = 4 << 20
 GRANT = 16 << 20
 PARTS = {1: (0, 2), 2: (0,), 3: (0,)}
-ORDER = (2, 3, 1)
+ORDER = (2, 1, 3)
 BACK = (3, 2, 1)
 HELD = 14 << 20
 

time: 41.2 us -> 41.2 us (level)
  no operation moved by 1% of the time
where the time goes in v8:
time: 41.2 us; the launch traced here: 41.1 us
  Pallas kernels  26.6 us (65%)
  starting transfers between devices  12.4 us (30%)
  waiting for transfers between devices  1.39 us (3%)
  between operations  0.73 us (2%)
    ppermute x9, starting transfers between devices, crossed(): return lax.ppermute(x, axis, [(s, s ^ bit) for s in range(n)])  12.4 us
    pallas_call x1, Pallas kernels, last(): pl.pallas_call(functools.partial(last_kernel, n_ep), in_specs=[VM] * 6 +...  7.2 us
    pallas_call x1, Pallas kernels, front(): pl.pallas_call(front_kernel, in_specs=[VM] * 7 + [HBM] * 2 + [VM] * len(p...  7.11 us
    pallas_call x1, Pallas kernels, hold(): pl.pallas_call(hold_kernel, in_specs=[HBM] * 4, out_specs=[VM] * 6, out_s...  7.03 us
    pallas_call x1, Pallas kernels, attend(): pl.pallas_call(functools.partial(attend_kernel, per), in_specs=[VM, VM, S...  2.99 us
    ppermute x9, waiting for transfers between devices, crossed(): return lax.ppermute(x, axis, [(s, s ^ bit) for s in range(n)])  1.39 us
    pallas_call x1, Pallas kernels, pack(): pl.pallas_call(pack_kernel, in_specs=[HBM] * 4, out_specs=[VM] * n_ep, ou...  1.33 us
    pallas_call x1, Pallas kernels, pick(): pl.pallas_call(pick_kernel, in_specs=[VM] * (2 + len(blocks)), out_specs=...  0.9 us
  transfers between devices with their start and end apart: 9, of which 2 were waited for; matrix products, arithmetic and copies ran while one was open for 0% of the time, Pallas kernels for 42%

profile of v8, /device:TPU:0, one launch (start us, length us, event | category | flops | bytes accessed | tf_op | source)
XLA Modules:
  0.0 41.1 jit_solution(2789567064178093437)
XLA Ops:
  0.6 1.3 %pack.1 = (bf16[32,1536]{1,0:T(8,128)(2,1)S(1)}, bf16[32,2432]{1,0:T(8,128)(2,1)S(1)}, bf16[32,1536]{1,0:T(8,128)(2,1)S(1)}, bf16[32,640]{1,0:T(8,128)(2,1)S(1)}) custom-call(bf16[16,8,576]{2,1,0:T(8,128)(2,1)} %codes_hbm.1, bf16[5,8,16]{2,1,0:T(8,128)(2,1)} %bitcast.9, bf16[16,7168]{1,0:T(8,128)(2,1)} %own.3, s32[8,16]{1,0:T(8,128)} %bitcast.7), custom_call_target="tpu_custom_call" | custom-call | tf_op jit(solution)/shard_map/pack/pallas_call | solution.py:162
  2.0 3.1 %collective-permute-start.1 = (bf16[32,2432]{1,0:T(8,128)(2,1)S(1)}, bf16[32,2432]{1,0:T(8,128)(2,1)S(1)}, u32[]{:S(2)}, u32[]{:S(2)}) collective-permute-start(bf16[32,2432]{1,0:T(8,128)(2,1)S(1)} %get-tuple-element.34), channel_id=1, source_target_pairs={{0,4},{4,0},{8,12},{12,8},{1,5},{5,1},{9,13},{13,9},{2,6},{6,2},{1... | collective-permute-start | bytes 466952 | tf_op jit(solution)/shard_map/ppermute | solution.py:528
  5.1 2.6 %collective-permute-start = (bf16[32,1536]{1,0:T(8,128)(2,1)S(1)}, bf16[32,1536]{1,0:T(8,128)(2,1)S(1)}, u32[]{:S(2)}, u32[]{:S(2)}) collective-permute-start(bf16[32,1536]{1,0:T(8,128)(2,1)S(1)} %get-tuple-element.33), channel_id=1, source_target_pairs={{0,8},{4,12},{8,0},{12,4},{1,9},{5,13},{9,1},{13,5},{2,10},{6,14},... | collective-permute-start | bytes 294920 | tf_op jit(solution)/shard_map/ppermute | solution.py:528
  7.7 0.0 collective-permute-start.2
  7.7 0.0 copy-start
  7.7 7.0 %hold.1 = (bf16[8,1792,256]{2,1,0:T(8,128)(2,1)S(1)}, bf16[8,1792,256]{2,1,0:T(8,128)(2,1)S(1)}, bf16[3,1792,256]{2,1,0:T(8,128)(2,1)S(1)}, bf16[3,1792,256]{2,1...) custom-call(s32[8,16]{1,0:T(8,128)} %bitcast.8, f32[8,16]{1,0:T(8,128)} %bitcast.10, ...), custom_call_target="tpu_custom_call" | custom-call | bytes 20185088 | tf_op jit(solution)/shard_map/hold/pallas_call | solution.py:286
  14.7 1.0 %collective-permute-done.refs_2_.refs_0_ = bf16[32,1536]{1,0:T(8,128)(2,1)S(1)} collective-permute-done((bf16[32,1536]{1,0:T(8,128)(2,1)S(1)}, bf16[32,1536]{1,0:T(8,128)(2,1)S(1)}, u32[]{:S(2)}, u32[]{:S(2)}) %collective-permute-start) | collective-permute-done | bytes 98336 | tf_op jit(solution)/shard_map/ppermute | solution.py:528
  15.7 0.0 collective-permute-done.2.refs_3_.refs_1_
  15.7 0.0 collective-permute-done.1.refs_1_.near
  15.8 0.1 collective-permute-start.5
  15.8 1.6 %collective-permute-start.4 = (bf16[48,1792]{1,0:T(8,128)(2,1)S(1)}, bf16[48,1792]{1,0:T(8,128)(2,1)S(1)}, u32[]{:S(2)}, u32[]{:S(2)}) collective-permute-start(bf16[48,1792]{1,0:T(8,128)(2,1)S(1)} %get-tuple-element.48.came), channel_id=1, source_target_pairs={{0,3},{1,2},{2,1},{3,0},{4,7},{5,6},{6,5},{7,4},{8,11},{9,10},{10,... | collective-permute-start | bytes 516104 | tf_op jit(solution)/shard_map/ppermute | solution.py:528
  17.4 0.5 %collective-permute-start.3 = (bf16[32,1792]{1,0:T(8,128)(2,1)S(1)}, bf16[32,1792]{1,0:T(8,128)(2,1)S(1)}, u32[]{:S(2)}, u32[]{:S(2)}) collective-permute-start(bf16[32,1792]{1,0:T(8,128)(2,1)S(1)} %get-tuple-element.47), channel_id=1, source_target_pairs={{0,2},{1,3},{2,0},{3,1},{4,6},{5,7},{6,4},{7,5},{8,10},{9,11},{10,... | collective-permute-start | bytes 344072 | tf_op jit(solution)/shard_map/ppermute | solution.py:528
  18.0 0.0 collective-permute-done.5.came_too
  18.0 0.0 copy-done
  18.0 7.1 %front.1 = (f32[8,64,256]{2,1,0:T(8,128)S(1)}, f32[8,64,256]{2,1,0:T(8,128)S(1)}, bf16[6,1792,256]{2,1,0:T(8,128)(2,1)S(1)}, bf16[6,1792,256]{2,1,0:T(8,128)(2,1)S(1)}, bf16[256,64]{1,0:T(8,128)(2,1)S(1)}) custom-call(bf16[16,7168]{1,0:T(8,128)(2,1)S(1)} %copy-done, bf16[48,1792]{1,0:T(8,128)(2,1)S(1)} %get-tuple-element.48.came, ...), custom_call_target="tpu_custom_call" | custom-call | flops 1879048192 | bytes 20185088 | tf_op jit(solution)/shard_map/front/pallas_call | solution.py:402
  25.1 0.0 collective-permute-done.3.far
  25.1 0.0 collective-permute-done.4.far_too
  25.1 0.0 copy-start.1
  25.1 0.0 copy-start.2
  25.2 0.0 copy-start.3
  25.2 7.2 %last.1 = (bf16[8,8,256]{2,1,0:T(8,128)(2,1)S(1)}, bf16[8,8,256]{2,1,0:T(8,128)(2,1)S(1)}, bf16[8,8,256]{2,1,0:T(8,128)(2,1)S(1)}, bf16[8,8,256]{2,1,0:T(8,128)(2,1)S(1)}) custom-call(bf16[16,7168]{1,0:T(8,128)(2,1)S(1)} %copy-done, bf16[32,2432]{1,0:T(8,128)(2,1)S(1)} %collective-permute-done.1.refs_1_.near, ...), custom_call_target="tpu_custom_call" | custom-call | flops 1879048192 | bytes 18350080 | tf_op jit(solution)/shard_map/last/pallas_call | solution.py:480
  32.4 2.9 %collective-permute-start.6 = (bf16[8,8,256]{2,1,0:T(8,128)(2,1)S(1)}, bf16[8,8,256]{2,1,0:T(8,128)(2,1)S(1)}, u32[]{:S(2)}, u32[]{:S(2)}) collective-permute-start(bf16[8,8,256]{2,1,0:T(8,128)(2,1)S(1)} %get-tuple-element.59), channel_id=1, source_target_pairs={{0,12},{4,8},{8,4},{12,0},{1,13},{5,9},{9,5},{13,1},{2,14},{6,10},... | collective-permute-start | bytes 98312 | tf_op jit(solution)/shard_map/ppermute | solution.py:528
  35.3 0.3 collective-permute-start.7
  35.5 1.3 %collective-permute-start.8 = (bf16[8,8,256]{2,1,0:T(8,128)(2,1)S(1)}, bf16[8,8,256]{2,1,0:T(8,128)(2,1)S(1)}, u32[]{:S(2)}, u32[]{:S(2)}) collective-permute-start(bf16[8,8,256]{2,1,0:T(8,128)(2,1)S(1)} %get-tuple-element.61), channel_id=1, source_target_pairs={{0,4},{4,0},{8,12},{12,8},{1,5},{5,1},{9,13},{13,9},{2,6},{6,2},{1... | collective-permute-start | bytes 98312 | tf_op jit(solution)/shard_map/ppermute | solution.py:528
  36.8 0.0 copy-done.1
  36.8 0.0 copy-done.2
  36.8 0.0 copy-done.3
  36.8 3.0 %attend.1 = bf16[4,128,512]{2,1,0:T(8,128)(2,1)} custom-call(bf16[4,576,128]{2,1,0:T(8,128)(2,1)S(1)} %bitcast.5, bf16[4,576]{1,0:T(4,128)(2,1)S(1)} %copy-done.2, s32[4]{0:T(128)S(1)} %copy-done.3, bf16[32,640]{1,0:T(8,128)(2,1)S(1)} %get-tuple-element.32.refs_0_, bf16[32,2432]{1,0:T(8,128)(2,1)S(1)} %collective-permute-done.1.refs_1_.near, ...), custom_call_target="tpu_custom_call" | custom-call | flops 301989888 | bytes 1114112 | tf_op jit(solution)/shard_map/attend/pallas_call | solution.py:77
  39.8 0.0 collective-permute-done.6.refs_1_
  39.8 0.3 collective-permute-done.7.refs_2_
  40.2 0.0 collective-permute-done.8.refs_3_
  40.2 0.9 %pick.1 = bf16[128,256]{1,0:T(8,128)(2,1)} custom-call(bf16[128,256]{1,0:T(8,128)(2,1)S(1)} %get-tuple-element.45.select_ref, f32[128,1]{1,0:T(8,128)S(1)} %get-tuple-element.46.column_ref, bf16[8,8,256]{2,1,0:T(8,128)(2,1)S(1)} %get-tuple-element.58.refs_0_, bf16[8,8,256]{2,1,0:T(8,128)(2,1)S(1)} %collective-permute-done.6.refs_1_, ...), custom_call_target="tpu_custom_call" | custom-call | tf_op jit(solution)/shard_map/pick/pallas_call | solution.py:516
  (1 shorter events, 0.0 us)
Async XLA Ops:
  2.0 13.8 %collective-permute-start.1 = (bf16[32,2432]{1,0:T(8,128)(2,1)S(1)}, bf16[32,2432]{1,0:T(8,128)(2,1)S(1)}, u32[]{:S(2)}, u32[]{:S(2)}) collective-permute-start(bf16[32,2432]{1,0:T(8,128)(2,1)S(1)} %get-tuple-element.34), channel_id=1, source_target_pairs={{0,4},{4,0},{8,12},{12,8},{1,5},{5,1},{9,13},{13,9},{2,6},{6,2},{1... | collective-permute-start | bytes 466952 | tf_op jit(solution)/shard_map/ppermute | solution.py:528
  5.1 10.7 %collective-permute-start = (bf16[32,1536]{1,0:T(8,128)(2,1)S(1)}, bf16[32,1536]{1,0:T(8,128)(2,1)S(1)}, u32[]{:S(2)}, u32[]{:S(2)}) collective-permute-start(bf16[32,1536]{1,0:T(8,128)(2,1)S(1)} %get-tuple-element.33), channel_id=1, source_target_pairs={{0,8},{4,12},{8,0},{12,4},{1,9},{5,13},{9,1},{13,5},{2,10},{6,14},... | collective-permute-start | bytes 294920 | tf_op jit(solution)/shard_map/ppermute | solution.py:528
  7.7 8.1 %collective-permute-start.2 = (bf16[32,1536]{1,0:T(8,128)(2,1)S(1)}, bf16[32,1536]{1,0:T(8,128)(2,1)S(1)}, u32[]{:S(2)}, u32[]{:S(2)}) collective-permute-start(bf16[32,1536]{1,0:T(8,128)(2,1)S(1)} %get-tuple-element.35), channel_id=1, source_target_pairs={{0,12},{4,8},{8,4},{12,0},{1,13},{5,9},{9,5},{13,1},{2,14},{6,10},... | collective-permute-start | bytes 294920 | tf_op jit(solution)/shard_map/ppermute | solution.py:528
  7.7 10.3 %copy-start = (bf16[16,7168]{1,0:T(8,128)(2,1)S(1)}, bf16[16,7168]{1,0:T(8,128)(2,1)}, u32[]{:S(2)}) copy-start(bf16[16,7168]{1,0:T(8,128)(2,1)} %own.3) | copy-start | bytes 688132
  15.8 2.2 %collective-permute-start.5 = (bf16[48,1792]{1,0:T(8,128)(2,1)S(1)}, bf16[48,1792]{1,0:T(8,128)(2,1)S(1)}, u32[]{:S(2)}, u32[]{:S(2)}) collective-permute-start(bf16[48,1792]{1,0:T(8,128)(2,1)S(1)} %get-tuple-element.48.came), channel_id=1, source_target_pairs={{0,1},{1,0},{2,3},{3,2},{4,5},{5,4},{6,7},{7,6},{8,9},{9,8},{10,11... | collective-permute-start | bytes 516104 | tf_op jit(solution)/shard_map/ppermute | solution.py:528
  15.8 9.3 %collective-permute-start.4 = (bf16[48,1792]{1,0:T(8,128)(2,1)S(1)}, bf16[48,1792]{1,0:T(8,128)(2,1)S(1)}, u32[]{:S(2)}, u32[]{:S(2)}) collective-permute-start(bf16[48,1792]{1,0:T(8,128)(2,1)S(1)} %get-tuple-element.48.came), channel_id=1, source_target_pairs={{0,3},{1,2},{2,1},{3,0},{4,7},{5,6},{6,5},{7,4},{8,11},{9,10},{10,... | collective-permute-start | bytes 516104 | tf_op jit(solution)/shard_map/ppermute | solution.py:528
  17.4 7.7 %collective-permute-start.3 = (bf16[32,1792]{1,0:T(8,128)(2,1)S(1)}, bf16[32,1792]{1,0:T(8,128)(2,1)S(1)}, u32[]{:S(2)}, u32[]{:S(2)}) collective-permute-start(bf16[32,1792]{1,0:T(8,128)(2,1)S(1)} %get-tuple-element.47), channel_id=1, source_target_pairs={{0,2},{1,3},{2,0},{3,1},{4,6},{5,7},{6,4},{7,5},{8,10},{9,11},{10,... | collective-permute-start | bytes 344072 | tf_op jit(solution)/shard_map/ppermute | solution.py:528
  25.1 11.7 %copy-start.1 = (bf16[4,128,576]{1,2,0:T(8,128)(2,1)S(1)}, bf16[4,128,576]{1,2,0:T(8,128)(2,1)}, u32[]{:S(2)}) copy-start(bf16[4,128,576]{1,2,0:T(8,128)(2,1)} %param.12) | copy-start | bytes 1769476
  25.1 11.7 %copy-start.2 = (bf16[4,576]{1,0:T(4,128)(2,1)S(1)}, bf16[4,576]{1,0:T(4,128)(2,1)}, u32[]{:S(2)}) copy-start(bf16[4,576]{1,0:T(4,128)(2,1)} %new_ref.1) | copy-start | bytes 13828
  25.2 11.7 %copy-start.3 = (s32[4]{0:T(128)S(1)}, s32[4]{0:T(128)}, u32[]{:S(2)}) copy-start(s32[4]{0:T(128)} %len_ref.1) | copy-start | bytes 52
  32.4 7.5 %collective-permute-start.6 = (bf16[8,8,256]{2,1,0:T(8,128)(2,1)S(1)}, bf16[8,8,256]{2,1,0:T(8,128)(2,1)S(1)}, u32[]{:S(2)}, u32[]{:S(2)}) collective-permute-start(bf16[8,8,256]{2,1,0:T(8,128)(2,1)S(1)} %get-tuple-element.59), channel_id=1, source_target_pairs={{0,12},{4,8},{8,4},{12,0},{1,13},{5,9},{9,5},{13,1},{2,14},{6,10},... | collective-permute-start | bytes 98312 | tf_op jit(solution)/shard_map/ppermute | solution.py:528
  35.3 4.9 %collective-permute-start.7 = (bf16[8,8,256]{2,1,0:T(8,128)(2,1)S(1)}, bf16[8,8,256]{2,1,0:T(8,128)(2,1)S(1)}, u32[]{:S(2)}, u32[]{:S(2)}) collective-permute-start(bf16[8,8,256]{2,1,0:T(8,128)(2,1)S(1)} %get-tuple-element.60), channel_id=1, source_target_pairs={{0,8},{4,12},{8,0},{12,4},{1,9},{5,13},{9,1},{13,5},{2,10},{6,14},... | collective-permute-start | bytes 98312 | tf_op jit(solution)/shard_map/ppermute | solution.py:528
  35.5 4.7 %collective-permute-start.8 = (bf16[8,8,256]{2,1,0:T(8,128)(2,1)S(1)}, bf16[8,8,256]{2,1,0:T(8,128)(2,1)S(1)}, u32[]{:S(2)}, u32[]{:S(2)}) collective-permute-start(bf16[8,8,256]{2,1,0:T(8,128)(2,1)S(1)} %get-tuple-element.61), channel_id=1, source_target_pairs={{0,4},{4,0},{8,12},{12,8},{1,5},{5,1},{9,13},{13,9},{2,6},{6,2},{1... | collective-permute-start | bytes 98312 | tf_op jit(solution)/shard_map/ppermute | solution.py:528
